TPU v7x, 128 devices: a whole 4x4x4 slice. The times are simulated.
128 devices in a mesh: batch: 16 (over x, y_hi, core), replica: 8 (over z, y_lo).
Axes of the slice: x: 4, y: 4 (y_hi: 2, y_lo: 2; y = y_hi * 2 + y_lo), z: 4, core: 2. Of those that a mesh axis runs over, the one named last changes fastest.
Arguments:
- sensor_feats: bfloat16 [40960, 1024], P(('batch', 'replica')), may hold values from -6 to 6
- proj_weight: bfloat16 [1024, 1024], replicated, may hold values from -0.1875 to 0.1875
- text_feats: bfloat16 [40960, 1024], P(('batch', 'replica')), may hold values from -0.29882812 to 0.29882812
Outputs:
- text_grad: float32 [40960, 1024], P(('batch', 'replica'))
- weight_grad: float32 [1024, 1024], P('batch')
All inputs are finite; a program needn't handle non-finite values.
Results may differ from a plain program's by a relative error of at most 0.0051.
Values may be sent and summed in bfloat16 or wider, within the bound.
No kernel may reach another device: no remote copies, remote signals or barrier semaphores. Data moves between devices by JAX's collectives and lax.ppermute only.
A program may use at most 128 MiB of HBM per device.

v0:
```python
import jax
import jax.numpy as jnp
from jax import lax
from jax.sharding import PartitionSpec as P

LOGIT_SCALE = 10.0
LOGIT_BIAS = -2.0
EPSILON = 1e-06


def from_behind(block, axis, distance):
    devices = range(lax.axis_size(axis))
    route = [((i - distance) % len(devices), i) for i in devices]
    return lax.ppermute(block, axis, route)


def normalize(values):
    length = jnp.sqrt(jnp.sum(values * values, axis=-1, keepdims=True) + EPSILON)
    return (values / length, length)


def slope_tile(opening, sensor_rows, text_rows, diagonal):
    logits = (
        LOGIT_SCALE * jnp.dot(sensor_rows, text_rows.T, preferred_element_type=jnp.float32)
        + LOGIT_BIAS
    )
    return (jax.nn.sigmoid(logits) - opening * diagonal).astype(jnp.bfloat16)


def tile_grads(opening, sensor_unit, visiting, diagonal):
    slopes = slope_tile(opening, sensor_unit, visiting, diagonal)
    sensor_add = LOGIT_SCALE * jnp.dot(slopes, visiting, preferred_element_type=jnp.float32)
    text_add = LOGIT_SCALE * jnp.dot(slopes.T, sensor_unit, preferred_element_type=jnp.float32)
    return (sensor_add, text_add)


def local(sensor_feats, proj_weight, text_feats):
    group_size = lax.axis_size("batch")
    block_rows = sensor_feats.shape[0]
    width = proj_weight.shape[1]
    sensor_raw = jnp.dot(sensor_feats, proj_weight, preferred_element_type=jnp.float32)
    sensor_norm, sensor_len = normalize(sensor_raw)
    text_norm, text_len = normalize(text_feats.astype(jnp.float32))
    sensor_unit = sensor_norm.astype(jnp.bfloat16)
    text_unit = text_norm.astype(jnp.bfloat16)
    diagonal = jnp.eye(block_rows, dtype=jnp.float32)
    zero_rows = jnp.zeros((block_rows, width), jnp.float32)

    def one_turn(turn_index, carried):
        sensor_grad, visiting, partial_value = carried
        opening = (turn_index == 0).astype(jnp.float32)
        arriving = from_behind(visiting, "batch", 1)
        sensor_add, text_add = tile_grads(opening, sensor_unit, visiting, diagonal)
        partial_value = from_behind(partial_value + text_add, "batch", 1)
        return (sensor_grad + sensor_add, arriving, partial_value)

    sensor_grad, unused_texts, text_part = lax.fori_loop(
        0, group_size, one_turn, (zero_rows, text_unit, zero_rows)
    )
    text_grad = (
        text_part - text_norm * jnp.sum(text_norm * text_part, axis=-1, keepdims=True)
    ) / text_len
    raw_grad = (
        (sensor_grad - sensor_norm * jnp.sum(sensor_norm * sensor_grad, axis=-1, keepdims=True))
        / sensor_len
    ).astype(jnp.bfloat16)
    partial_rows = lax.psum_scatter(
        jnp.dot(sensor_feats.T, raw_grad, preferred_element_type=jnp.float32),
        "batch",
        scatter_dimension=0,
        tiled=True,
    )
    weight_grad = lax.psum(partial_rows, "replica")
    return (text_grad, weight_grad)


def solution(mesh):
    return jax.shard_map(
        local,
        mesh=mesh,
        in_specs=(P(("batch", "replica"), None), P(), P(("batch", "replica"), None)),
        out_specs=(P(("batch", "replica"), None), P("batch", None)),
        check_vma=False,
    )
```

profile of v0, /device:TPU:0, one launch (start us, length us, event | category | flops | bytes accessed | tf_op | source)
XLA Modules:
  0.0 723.3 jit_solution(5367150134255600244)
XLA Ops:
  9.0 2.1 multiply_reduce_fusion.2
  12.7 533.0 %while.18 = (s32[]{:T(128)}, f32[320,1024]{1,0:T(8,128)}, bf16[320,1024]{1,0:T(8,128)(2,1)}, f32[320,1024]{1,0:T(8,128)S(1)}, bf16[320,1024]{1,0:T(8,128)(2,1)}, /*index=5*/s32[]{:T(128)}, s32[]{:T(128)}) while((s32[]{:T(128)}, f32[320,1024]{1,0:T(8,128)}, bf16[320,1024]{1,0:T(8,128)(2,1)}, f32[320,1024]{1,0:T(8,128)S(1)}, ...), condition=%wide.region_3.0_spmd.clone, body=%wide.region_2.0_spmd.clone.sunk | while | flops 631705600 | bytes 21094632 | solution.py:57
  18.0 3.4 collective-permute-start
  21.4 2.8 fusion.41
  24.2 21.8 %collective-permute-done = bf16[320,1024]{1,0:T(8,128)(2,1)} collective-permute-done((bf16[320,1024]{1,0:T(8,128)(2,1)}, bf16[320,1024]{1,0:T(8,128)(2,1)}, u32[]{:S(2)}, u32[]{:S(2)}) %collective-permute-start) | collective-permute-done | bytes 655392 | tf_op jit(solution)/shard_map/while/body/eval_jaxpr/ppermute | solution.py:14
  46.0 2.0 copy.15
  52.6 3.2 fusion.41
  55.8 23.5 %collective-permute-done = bf16[320,1024]{1,0:T(8,128)(2,1)} collective-permute-done((bf16[320,1024]{1,0:T(8,128)(2,1)}, bf16[320,1024]{1,0:T(8,128)(2,1)}, u32[]{:S(2)}, u32[]{:S(2)}) %collective-permute-start) | collective-permute-done | bytes 655392 | tf_op jit(solution)/shard_map/while/body/eval_jaxpr/ppermute | solution.py:14
  79.3 2.0 copy.15
  84.7 3.2 fusion.41
  87.9 24.8 %collective-permute-done = bf16[320,1024]{1,0:T(8,128)(2,1)} collective-permute-done((bf16[320,1024]{1,0:T(8,128)(2,1)}, bf16[320,1024]{1,0:T(8,128)(2,1)}, u32[]{:S(2)}, u32[]{:S(2)}) %collective-permute-start) | collective-permute-done | bytes 655392 | tf_op jit(solution)/shard_map/while/body/eval_jaxpr/ppermute | solution.py:14
  112.6 2.0 copy.15
  118.0 3.2 fusion.41
  121.2 24.8 %collective-permute-done = bf16[320,1024]{1,0:T(8,128)(2,1)} collective-permute-done((bf16[320,1024]{1,0:T(8,128)(2,1)}, bf16[320,1024]{1,0:T(8,128)(2,1)}, u32[]{:S(2)}, u32[]{:S(2)}) %collective-permute-start) | collective-permute-done | bytes 655392 | tf_op jit(solution)/shard_map/while/body/eval_jaxpr/ppermute | solution.py:14
  146.0 2.0 copy.15
  151.3 3.2 fusion.41
  154.5 24.8 %collective-permute-done = bf16[320,1024]{1,0:T(8,128)(2,1)} collective-permute-done((bf16[320,1024]{1,0:T(8,128)(2,1)}, bf16[320,1024]{1,0:T(8,128)(2,1)}, u32[]{:S(2)}, u32[]{:S(2)}) %collective-permute-start) | collective-permute-done | bytes 655392 | tf_op jit(solution)/shard_map/while/body/eval_jaxpr/ppermute | solution.py:14
  184.6 3.2 fusion.41
  187.8 24.8 %collective-permute-done = bf16[320,1024]{1,0:T(8,128)(2,1)} collective-permute-done((bf16[320,1024]{1,0:T(8,128)(2,1)}, bf16[320,1024]{1,0:T(8,128)(2,1)}, u32[]{:S(2)}, u32[]{:S(2)}) %collective-permute-start) | collective-permute-done | bytes 655392 | tf_op jit(solution)/shard_map/while/body/eval_jaxpr/ppermute | solution.py:14
  217.9 3.2 fusion.41
  221.1 24.8 %collective-permute-done = bf16[320,1024]{1,0:T(8,128)(2,1)} collective-permute-done((bf16[320,1024]{1,0:T(8,128)(2,1)}, bf16[320,1024]{1,0:T(8,128)(2,1)}, u32[]{:S(2)}, u32[]{:S(2)}) %collective-permute-start) | collective-permute-done | bytes 655392 | tf_op jit(solution)/shard_map/while/body/eval_jaxpr/ppermute | solution.py:14
  251.2 3.2 fusion.41
  254.4 24.8 %collective-permute-done = bf16[320,1024]{1,0:T(8,128)(2,1)} collective-permute-done((bf16[320,1024]{1,0:T(8,128)(2,1)}, bf16[320,1024]{1,0:T(8,128)(2,1)}, u32[]{:S(2)}, u32[]{:S(2)}) %collective-permute-start) | collective-permute-done | bytes 655392 | tf_op jit(solution)/shard_map/while/body/eval_jaxpr/ppermute | solution.py:14
  279.2 2.0 copy.15
  284.5 3.2 fusion.41
  287.8 24.8 %collective-permute-done = bf16[320,1024]{1,0:T(8,128)(2,1)} collective-permute-done((bf16[320,1024]{1,0:T(8,128)(2,1)}, bf16[320,1024]{1,0:T(8,128)(2,1)}, u32[]{:S(2)}, u32[]{:S(2)}) %collective-permute-start) | collective-permute-done | bytes 655392 | tf_op jit(solution)/shard_map/while/body/eval_jaxpr/ppermute | solution.py:14
  317.8 3.2 fusion.41
  321.1 24.8 %collective-permute-done = bf16[320,1024]{1,0:T(8,128)(2,1)} collective-permute-done((bf16[320,1024]{1,0:T(8,128)(2,1)}, bf16[320,1024]{1,0:T(8,128)(2,1)}, u32[]{:S(2)}, u32[]{:S(2)}) %collective-permute-start) | collective-permute-done | bytes 655392 | tf_op jit(solution)/shard_map/while/body/eval_jaxpr/ppermute | solution.py:14
  351.2 3.2 fusion.41
  354.4 24.8 %collective-permute-done = bf16[320,1024]{1,0:T(8,128)(2,1)} collective-permute-done((bf16[320,1024]{1,0:T(8,128)(2,1)}, bf16[320,1024]{1,0:T(8,128)(2,1)}, u32[]{:S(2)}, u32[]{:S(2)}) %collective-permute-start) | collective-permute-done | bytes 655392 | tf_op jit(solution)/shard_map/while/body/eval_jaxpr/ppermute | solution.py:14
  379.1 2.0 copy.15
  384.5 3.2 fusion.41
  387.7 24.8 %collective-permute-done = bf16[320,1024]{1,0:T(8,128)(2,1)} collective-permute-done((bf16[320,1024]{1,0:T(8,128)(2,1)}, bf16[320,1024]{1,0:T(8,128)(2,1)}, u32[]{:S(2)}, u32[]{:S(2)}) %collective-permute-start) | collective-permute-done | bytes 655392 | tf_op jit(solution)/shard_map/while/body/eval_jaxpr/ppermute | solution.py:14
  417.8 3.2 fusion.41
  421.0 24.8 %collective-permute-done = bf16[320,1024]{1,0:T(8,128)(2,1)} collective-permute-done((bf16[320,1024]{1,0:T(8,128)(2,1)}, bf16[320,1024]{1,0:T(8,128)(2,1)}, u32[]{:S(2)}, u32[]{:S(2)}) %collective-permute-start) | collective-permute-done | bytes 655392 | tf_op jit(solution)/shard_map/while/body/eval_jaxpr/ppermute | solution.py:14
  451.1 3.2 fusion.41
  454.3 24.8 %collective-permute-done = bf16[320,1024]{1,0:T(8,128)(2,1)} collective-permute-done((bf16[320,1024]{1,0:T(8,128)(2,1)}, bf16[320,1024]{1,0:T(8,128)(2,1)}, u32[]{:S(2)}, u32[]{:S(2)}) %collective-permute-start) | collective-permute-done | bytes 655392 | tf_op jit(solution)/shard_map/while/body/eval_jaxpr/ppermute | solution.py:14
  479.1 2.0 copy.15
  484.4 3.2 fusion.41
  487.6 24.8 %collective-permute-done = bf16[320,1024]{1,0:T(8,128)(2,1)} collective-permute-done((bf16[320,1024]{1,0:T(8,128)(2,1)}, bf16[320,1024]{1,0:T(8,128)(2,1)}, u32[]{:S(2)}, u32[]{:S(2)}) %collective-permute-start) | collective-permute-done | bytes 655392 | tf_op jit(solution)/shard_map/while/body/eval_jaxpr/ppermute | solution.py:14
  517.7 3.2 fusion.41
  520.9 24.8 %collective-permute-done = bf16[320,1024]{1,0:T(8,128)(2,1)} collective-permute-done((bf16[320,1024]{1,0:T(8,128)(2,1)}, bf16[320,1024]{1,0:T(8,128)(2,1)}, u32[]{:S(2)}, u32[]{:S(2)}) %collective-permute-start) | collective-permute-done | bytes 655392 | tf_op jit(solution)/shard_map/while/body/eval_jaxpr/ppermute | solution.py:14
  545.7 2.2 multiply_reduce_fusion
  548.2 4.6 convolution_bitcast_fusion
  552.8 5.4 copy.7
  559.7 77.5 %reduce-scatter.4.cloned.1.call-done = f32[64,1024]{1,0:T(8,128)} async-done(((f32[1024,1024]{1,0:T(8,128)}), f32[64,1024]{1,0:T(8,128)}) %reduce-scatter.4.cloned.1.call-update) | async-done | bytes 262160
  639.1 2.4 subtract_divide_fusion
  641.5 73.0 %all-reduce.2.cloned.1.call-done = f32[64,1024]{0,1:T(8,128)} async-done(((f32[64,1024]{0,1:T(8,128)}), f32[64,1024]{0,1:T(8,128)}) %all-reduce.2.cloned.1.call-update) | async-done | bytes 262160 | tf_op jit(solution)/shard_map/psum | solution.py:73
  (175 shorter events, 81.1 us)
Async XLA Ops:
  7.2 630.0 %reduce-scatter.4.cloned.1.call-start = ((), (), s32[]{:S(2)}) async-start(), calls=%async_computation.2 | async-start | bytes 4456448
  9.0 2.1 copy-start.4
  12.7 2.0 copy-start.3
  18.0 28.0 %collective-permute-start.1 = (f32[320,1024]{1,0:T(8,128)}, f32[320,1024]{1,0:T(8,128)S(1)}, u32[]{:S(2)}, u32[]{:S(2)}) collective-permute-start(f32[320,1024]{1,0:T(8,128)} %fusion.42), channel_id=1, source_target_pairs={{120,0},{0,8},{8,16},{16,24},{24,32},{32,40},{40,48},{48,56},{56,6... | collective-permute-start | bytes 3932168 | tf_op jit(solution)/shard_map/while/body/eval_jaxpr/ppermute | solution.py:14
  18.0 28.0 %collective-permute-start = (bf16[320,1024]{1,0:T(8,128)(2,1)}, bf16[320,1024]{1,0:T(8,128)(2,1)}, u32[]{:S(2)}, u32[]{:S(2)}) collective-permute-start(bf16[320,1024]{1,0:T(8,128)(2,1)} %copy.15), channel_id=1, source_target_pairs={{120,0},{0,8},{8,16},{16,24},{24,32},{32,40},{40,48},{48,56},{56,6... | collective-permute-start | bytes 1966088 | tf_op jit(solution)/shard_map/while/body/eval_jaxpr/ppermute | solution.py:14
  46.0 2.0 copy-start.3
  51.3 28.0 %collective-permute-start.1 = (f32[320,1024]{1,0:T(8,128)}, f32[320,1024]{1,0:T(8,128)S(1)}, u32[]{:S(2)}, u32[]{:S(2)}) collective-permute-start(f32[320,1024]{1,0:T(8,128)} %fusion.42), channel_id=1, source_target_pairs={{120,0},{0,8},{8,16},{16,24},{24,32},{32,40},{40,48},{48,56},{56,6... | collective-permute-start | bytes 3932168 | tf_op jit(solution)/shard_map/while/body/eval_jaxpr/ppermute | solution.py:14
  51.3 28.0 %collective-permute-start = (bf16[320,1024]{1,0:T(8,128)(2,1)}, bf16[320,1024]{1,0:T(8,128)(2,1)}, u32[]{:S(2)}, u32[]{:S(2)}) collective-permute-start(bf16[320,1024]{1,0:T(8,128)(2,1)} %copy.15), channel_id=1, source_target_pairs={{120,0},{0,8},{8,16},{16,24},{24,32},{32,40},{40,48},{48,56},{56,6... | collective-permute-start | bytes 1966088 | tf_op jit(solution)/shard_map/while/body/eval_jaxpr/ppermute | solution.py:14
  79.3 2.0 copy-start.3
  84.7 28.0 %collective-permute-start.1 = (f32[320,1024]{1,0:T(8,128)}, f32[320,1024]{1,0:T(8,128)S(1)}, u32[]{:S(2)}, u32[]{:S(2)}) collective-permute-start(f32[320,1024]{1,0:T(8,128)} %fusion.42), channel_id=1, source_target_pairs={{120,0},{0,8},{8,16},{16,24},{24,32},{32,40},{40,48},{48,56},{56,6... | collective-permute-start | bytes 3932168 | tf_op jit(solution)/shard_map/while/body/eval_jaxpr/ppermute | solution.py:14
  84.7 28.0 %collective-permute-start = (bf16[320,1024]{1,0:T(8,128)(2,1)}, bf16[320,1024]{1,0:T(8,128)(2,1)}, u32[]{:S(2)}, u32[]{:S(2)}) collective-permute-start(bf16[320,1024]{1,0:T(8,128)(2,1)} %copy.15), channel_id=1, source_target_pairs={{120,0},{0,8},{8,16},{16,24},{24,32},{32,40},{40,48},{48,56},{56,6... | collective-permute-start | bytes 1966088 | tf_op jit(solution)/shard_map/while/body/eval_jaxpr/ppermute | solution.py:14
  112.6 2.0 copy-start.3
  118.0 28.0 %collective-permute-start.1 = (f32[320,1024]{1,0:T(8,128)}, f32[320,1024]{1,0:T(8,128)S(1)}, u32[]{:S(2)}, u32[]{:S(2)}) collective-permute-start(f32[320,1024]{1,0:T(8,128)} %fusion.42), channel_id=1, source_target_pairs={{120,0},{0,8},{8,16},{16,24},{24,32},{32,40},{40,48},{48,56},{56,6... | collective-permute-start | bytes 3932168 | tf_op jit(solution)/shard_map/while/body/eval_jaxpr/ppermute | solution.py:14
  118.0 28.0 %collective-permute-start = (bf16[320,1024]{1,0:T(8,128)(2,1)}, bf16[320,1024]{1,0:T(8,128)(2,1)}, u32[]{:S(2)}, u32[]{:S(2)}) collective-permute-start(bf16[320,1024]{1,0:T(8,128)(2,1)} %copy.15), channel_id=1, source_target_pairs={{120,0},{0,8},{8,16},{16,24},{24,32},{32,40},{40,48},{48,56},{56,6... | collective-permute-start | bytes 1966088 | tf_op jit(solution)/shard_map/while/body/eval_jaxpr/ppermute | solution.py:14
  146.0 2.0 copy-start.3
  151.3 28.0 %collective-permute-start.1 = (f32[320,1024]{1,0:T(8,128)}, f32[320,1024]{1,0:T(8,128)S(1)}, u32[]{:S(2)}, u32[]{:S(2)}) collective-permute-start(f32[320,1024]{1,0:T(8,128)} %fusion.42), channel_id=1, source_target_pairs={{120,0},{0,8},{8,16},{16,24},{24,32},{32,40},{40,48},{48,56},{56,6... | collective-permute-start | bytes 3932168 | tf_op jit(solution)/shard_map/while/body/eval_jaxpr/ppermute | solution.py:14
  151.3 28.0 %collective-permute-start = (bf16[320,1024]{1,0:T(8,128)(2,1)}, bf16[320,1024]{1,0:T(8,128)(2,1)}, u32[]{:S(2)}, u32[]{:S(2)}) collective-permute-start(bf16[320,1024]{1,0:T(8,128)(2,1)} %copy.15), channel_id=1, source_target_pairs={{120,0},{0,8},{8,16},{16,24},{24,32},{32,40},{40,48},{48,56},{56,6... | collective-permute-start | bytes 1966088 | tf_op jit(solution)/shard_map/while/body/eval_jaxpr/ppermute | solution.py:14
  179.3 2.0 copy-start.3
  184.6 28.0 %collective-permute-start.1 = (f32[320,1024]{1,0:T(8,128)}, f32[320,1024]{1,0:T(8,128)S(1)}, u32[]{:S(2)}, u32[]{:S(2)}) collective-permute-start(f32[320,1024]{1,0:T(8,128)} %fusion.42), channel_id=1, source_target_pairs={{120,0},{0,8},{8,16},{16,24},{24,32},{32,40},{40,48},{48,56},{56,6... | collective-permute-start | bytes 3932168 | tf_op jit(solution)/shard_map/while/body/eval_jaxpr/ppermute | solution.py:14
  184.6 28.0 %collective-permute-start = (bf16[320,1024]{1,0:T(8,128)(2,1)}, bf16[320,1024]{1,0:T(8,128)(2,1)}, u32[]{:S(2)}, u32[]{:S(2)}) collective-permute-start(bf16[320,1024]{1,0:T(8,128)(2,1)} %copy.15), channel_id=1, source_target_pairs={{120,0},{0,8},{8,16},{16,24},{24,32},{32,40},{40,48},{48,56},{56,6... | collective-permute-start | bytes 1966088 | tf_op jit(solution)/shard_map/while/body/eval_jaxpr/ppermute | solution.py:14
  212.6 2.0 copy-start.3
  217.9 28.0 %collective-permute-start.1 = (f32[320,1024]{1,0:T(8,128)}, f32[320,1024]{1,0:T(8,128)S(1)}, u32[]{:S(2)}, u32[]{:S(2)}) collective-permute-start(f32[320,1024]{1,0:T(8,128)} %fusion.42), channel_id=1, source_target_pairs={{120,0},{0,8},{8,16},{16,24},{24,32},{32,40},{40,48},{48,56},{56,6... | collective-permute-start | bytes 3932168 | tf_op jit(solution)/shard_map/while/body/eval_jaxpr/ppermute | solution.py:14
  217.9 28.0 %collective-permute-start = (bf16[320,1024]{1,0:T(8,128)(2,1)}, bf16[320,1024]{1,0:T(8,128)(2,1)}, u32[]{:S(2)}, u32[]{:S(2)}) collective-permute-start(bf16[320,1024]{1,0:T(8,128)(2,1)} %copy.15), channel_id=1, source_target_pairs={{120,0},{0,8},{8,16},{16,24},{24,32},{32,40},{40,48},{48,56},{56,6... | collective-permute-start | bytes 1966088 | tf_op jit(solution)/shard_map/while/body/eval_jaxpr/ppermute | solution.py:14
  245.9 2.0 copy-start.3
  251.2 28.0 %collective-permute-start.1 = (f32[320,1024]{1,0:T(8,128)}, f32[320,1024]{1,0:T(8,128)S(1)}, u32[]{:S(2)}, u32[]{:S(2)}) collective-permute-start(f32[320,1024]{1,0:T(8,128)} %fusion.42), channel_id=1, source_target_pairs={{120,0},{0,8},{8,16},{16,24},{24,32},{32,40},{40,48},{48,56},{56,6... | collective-permute-start | bytes 3932168 | tf_op jit(solution)/shard_map/while/body/eval_jaxpr/ppermute | solution.py:14
  251.2 28.0 %collective-permute-start = (bf16[320,1024]{1,0:T(8,128)(2,1)}, bf16[320,1024]{1,0:T(8,128)(2,1)}, u32[]{:S(2)}, u32[]{:S(2)}) collective-permute-start(bf16[320,1024]{1,0:T(8,128)(2,1)} %copy.15), channel_id=1, source_target_pairs={{120,0},{0,8},{8,16},{16,24},{24,32},{32,40},{40,48},{48,56},{56,6... | collective-permute-start | bytes 1966088 | tf_op jit(solution)/shard_map/while/body/eval_jaxpr/ppermute | solution.py:14
  279.2 2.0 copy-start.3
  284.5 28.0 %collective-permute-start.1 = (f32[320,1024]{1,0:T(8,128)}, f32[320,1024]{1,0:T(8,128)S(1)}, u32[]{:S(2)}, u32[]{:S(2)}) collective-permute-start(f32[320,1024]{1,0:T(8,128)} %fusion.42), channel_id=1, source_target_pairs={{120,0},{0,8},{8,16},{16,24},{24,32},{32,40},{40,48},{48,56},{56,6... | collective-permute-start | bytes 3932168 | tf_op jit(solution)/shard_map/while/body/eval_jaxpr/ppermute | solution.py:14
  284.5 28.0 %collective-permute-start = (bf16[320,1024]{1,0:T(8,128)(2,1)}, bf16[320,1024]{1,0:T(8,128)(2,1)}, u32[]{:S(2)}, u32[]{:S(2)}) collective-permute-start(bf16[320,1024]{1,0:T(8,128)(2,1)} %copy.15), channel_id=1, source_target_pairs={{120,0},{0,8},{8,16},{16,24},{24,32},{32,40},{40,48},{48,56},{56,6... | collective-permute-start | bytes 1966088 | tf_op jit(solution)/shard_map/while/body/eval_jaxpr/ppermute | solution.py:14
  312.5 2.0 copy-start.3
  317.8 28.0 %collective-permute-start.1 = (f32[320,1024]{1,0:T(8,128)}, f32[320,1024]{1,0:T(8,128)S(1)}, u32[]{:S(2)}, u32[]{:S(2)}) collective-permute-start(f32[320,1024]{1,0:T(8,128)} %fusion.42), channel_id=1, source_target_pairs={{120,0},{0,8},{8,16},{16,24},{24,32},{32,40},{40,48},{48,56},{56,6... | collective-permute-start | bytes 3932168 | tf_op jit(solution)/shard_map/while/body/eval_jaxpr/ppermute | solution.py:14
  317.8 28.0 %collective-permute-start = (bf16[320,1024]{1,0:T(8,128)(2,1)}, bf16[320,1024]{1,0:T(8,128)(2,1)}, u32[]{:S(2)}, u32[]{:S(2)}) collective-permute-start(bf16[320,1024]{1,0:T(8,128)(2,1)} %copy.15), channel_id=1, source_target_pairs={{120,0},{0,8},{8,16},{16,24},{24,32},{32,40},{40,48},{48,56},{56,6... | collective-permute-start | bytes 1966088 | tf_op jit(solution)/shard_map/while/body/eval_jaxpr/ppermute | solution.py:14
  351.2 28.0 %collective-permute-start.1 = (f32[320,1024]{1,0:T(8,128)}, f32[320,1024]{1,0:T(8,128)S(1)}, u32[]{:S(2)}, u32[]{:S(2)}) collective-permute-start(f32[320,1024]{1,0:T(8,128)} %fusion.42), channel_id=1, source_target_pairs={{120,0},{0,8},{8,16},{16,24},{24,32},{32,40},{40,48},{48,56},{56,6... | collective-permute-start | bytes 3932168 | tf_op jit(solution)/shard_map/while/body/eval_jaxpr/ppermute | solution.py:14
  351.2 28.0 %collective-permute-start = (bf16[320,1024]{1,0:T(8,128)(2,1)}, bf16[320,1024]{1,0:T(8,128)(2,1)}, u32[]{:S(2)}, u32[]{:S(2)}) collective-permute-start(bf16[320,1024]{1,0:T(8,128)(2,1)} %copy.15), channel_id=1, source_target_pairs={{120,0},{0,8},{8,16},{16,24},{24,32},{32,40},{40,48},{48,56},{56,6... | collective-permute-start | bytes 1966088 | tf_op jit(solution)/shard_map/while/body/eval_jaxpr/ppermute | solution.py:14
  384.5 28.0 %collective-permute-start.1 = (f32[320,1024]{1,0:T(8,128)}, f32[320,1024]{1,0:T(8,128)S(1)}, u32[]{:S(2)}, u32[]{:S(2)}) collective-permute-start(f32[320,1024]{1,0:T(8,128)} %fusion.42), channel_id=1, source_target_pairs={{120,0},{0,8},{8,16},{16,24},{24,32},{32,40},{40,48},{48,56},{56,6... | collective-permute-start | bytes 3932168 | tf_op jit(solution)/shard_map/while/body/eval_jaxpr/ppermute | solution.py:14
  384.5 28.0 %collective-permute-start = (bf16[320,1024]{1,0:T(8,128)(2,1)}, bf16[320,1024]{1,0:T(8,128)(2,1)}, u32[]{:S(2)}, u32[]{:S(2)}) collective-permute-start(bf16[320,1024]{1,0:T(8,128)(2,1)} %copy.15), channel_id=1, source_target_pairs={{120,0},{0,8},{8,16},{16,24},{24,32},{32,40},{40,48},{48,56},{56,6... | collective-permute-start | bytes 1966088 | tf_op jit(solution)/shard_map/while/body/eval_jaxpr/ppermute | solution.py:14
  417.8 28.0 %collective-permute-start.1 = (f32[320,1024]{1,0:T(8,128)}, f32[320,1024]{1,0:T(8,128)S(1)}, u32[]{:S(2)}, u32[]{:S(2)}) collective-permute-start(f32[320,1024]{1,0:T(8,128)} %fusion.42), channel_id=1, source_target_pairs={{120,0},{0,8},{8,16},{16,24},{24,32},{32,40},{40,48},{48,56},{56,6... | collective-permute-start | bytes 3932168 | tf_op jit(solution)/shard_map/while/body/eval_jaxpr/ppermute | solution.py:14
  417.8 28.0 %collective-permute-start = (bf16[320,1024]{1,0:T(8,128)(2,1)}, bf16[320,1024]{1,0:T(8,128)(2,1)}, u32[]{:S(2)}, u32[]{:S(2)}) collective-permute-start(bf16[320,1024]{1,0:T(8,128)(2,1)} %copy.15), channel_id=1, source_target_pairs={{120,0},{0,8},{8,16},{16,24},{24,32},{32,40},{40,48},{48,56},{56,6... | collective-permute-start | bytes 1966088 | tf_op jit(solution)/shard_map/while/body/eval_jaxpr/ppermute | solution.py:14
  451.1 28.0 %collective-permute-start.1 = (f32[320,1024]{1,0:T(8,128)}, f32[320,1024]{1,0:T(8,128)S(1)}, u32[]{:S(2)}, u32[]{:S(2)}) collective-permute-start(f32[320,1024]{1,0:T(8,128)} %fusion.42), channel_id=1, source_target_pairs={{120,0},{0,8},{8,16},{16,24},{24,32},{32,40},{40,48},{48,56},{56,6... | collective-permute-start | bytes 3932168 | tf_op jit(solution)/shard_map/while/body/eval_jaxpr/ppermute | solution.py:14
  451.1 28.0 %collective-permute-start = (bf16[320,1024]{1,0:T(8,128)(2,1)}, bf16[320,1024]{1,0:T(8,128)(2,1)}, u32[]{:S(2)}, u32[]{:S(2)}) collective-permute-start(bf16[320,1024]{1,0:T(8,128)(2,1)} %copy.15), channel_id=1, source_target_pairs={{120,0},{0,8},{8,16},{16,24},{24,32},{32,40},{40,48},{48,56},{56,6... | collective-permute-start | bytes 1966088 | tf_op jit(solution)/shard_map/while/body/eval_jaxpr/ppermute | solution.py:14
  484.4 28.0 %collective-permute-start.1 = (f32[320,1024]{1,0:T(8,128)}, f32[320,1024]{1,0:T(8,128)S(1)}, u32[]{:S(2)}, u32[]{:S(2)}) collective-permute-start(f32[320,1024]{1,0:T(8,128)} %fusion.42), channel_id=1, source_target_pairs={{120,0},{0,8},{8,16},{16,24},{24,32},{32,40},{40,48},{48,56},{56,6... | collective-permute-start | bytes 3932168 | tf_op jit(solution)/shard_map/while/body/eval_jaxpr/ppermute | solution.py:14
  484.4 28.0 %collective-permute-start = (bf16[320,1024]{1,0:T(8,128)(2,1)}, bf16[320,1024]{1,0:T(8,128)(2,1)}, u32[]{:S(2)}, u32[]{:S(2)}) collective-permute-start(bf16[320,1024]{1,0:T(8,128)(2,1)} %copy.15), channel_id=1, source_target_pairs={{120,0},{0,8},{8,16},{16,24},{24,32},{32,40},{40,48},{48,56},{56,6... | collective-permute-start | bytes 1966088 | tf_op jit(solution)/shard_map/while/body/eval_jaxpr/ppermute | solution.py:14
  512.4 2.0 copy-start.3
  517.7 28.0 %collective-permute-start.1 = (f32[320,1024]{1,0:T(8,128)}, f32[320,1024]{1,0:T(8,128)S(1)}, u32[]{:S(2)}, u32[]{:S(2)}) collective-permute-start(f32[320,1024]{1,0:T(8,128)} %fusion.42), channel_id=1, source_target_pairs={{120,0},{0,8},{8,16},{16,24},{24,32},{32,40},{40,48},{48,56},{56,6... | collective-permute-start | bytes 3932168 | tf_op jit(solution)/shard_map/while/body/eval_jaxpr/ppermute | solution.py:14
  517.7 28.0 %collective-permute-start = (bf16[320,1024]{1,0:T(8,128)(2,1)}, bf16[320,1024]{1,0:T(8,128)(2,1)}, u32[]{:S(2)}, u32[]{:S(2)}) collective-permute-start(bf16[320,1024]{1,0:T(8,128)(2,1)} %copy.15), channel_id=1, source_target_pairs={{120,0},{0,8},{8,16},{16,24},{24,32},{32,40},{40,48},{48,56},{56,6... | collective-permute-start | bytes 1966088 | tf_op jit(solution)/shard_map/while/body/eval_jaxpr/ppermute | solution.py:14
  545.7 2.2 copy-start.1
  545.7 2.5 copy-start.6
  558.2 156.3 %all-reduce.2.cloned.1.call-start = ((), (), s32[]{:S(2)}) async-start(), calls=%async_computation.1 | async-start | bytes 1048576 | tf_op jit(solution)/shard_map/psum | solution.py:73
  (23 other events, 39.7 us)
Sparse Core Ops, SparseCore 0:
  558.3 78.7 reduce-scatter.3
  639.8 74.6 all-reduce.1
where the time goes:
time: 725 us; the launch traced here: 723 us
  waiting for transfers between devices  542 us (75%)
  matrix products  110 us (15%)
  local copies, waits for them, and re-layouts  42.6 us (6%)
  between operations  14.1 us (2%)
  other arithmetic  8.94 us (1%)
    ppermute x32, waiting for transfers between devices, from_behind(): return lax.ppermute(block, axis, route)  392 us
    unnamed x3, waiting for transfers between devices  77.5 us
    psum x1, waiting for transfers between devices, local(): weight_grad = lax.psum(partial_rows, 'replica')  73 us
    dot_general x16, matrix products, tile_grads(): jnp.dot(slopes, visiting, preferred_element_type=jnp.float32)  51.1 us
    while x80, local copies, waits for them, and re-layouts  32.7 us
    dot_general x16, matrix products, slope_tile(): jnp.dot(sensor_rows, text_rows.T, preferred_element_type=jnp.float32)  26.3 us
    dot_general x16, matrix products, tile_grads(): jnp.dot(slopes.T, sensor_unit, preferred_element_type=jnp.float32)  26 us
  transfers between devices with their start and end apart: 34, of which 18 were waited for; matrix products, arithmetic and copies ran while one was open for 8% of the time, Pallas kernels for 0%

commit v1 on v0

v1 whole, which is shorter than its diff:
```python
import itertools

import jax
import jax.numpy as jnp
from jax import lax
from jax.sharding import Mesh, PartitionSpec as P

LOGIT_SCALE = 10.0
LOGIT_BIAS = -2.0
EPSILON = 1e-06

SIZES = (4, 2, 2, 4, 2)
AXES = ("x", "yh", "c", "z", "yl")
F32 = jnp.float32
BF16 = jnp.bfloat16


def position(coords):
    index = 0
    for size, coord in zip(SIZES, coords):
        index = index * size + coord % size
    return index


def send(block, **shift):
    step = [shift.get(name, 0) for name in AXES]
    route = [
        (position(at), position([a + s for a, s in zip(at, step)]))
        for at in itertools.product(*map(range, SIZES))
    ]
    return lax.ppermute(block, AXES, route)


def normalize(values):
    length = jnp.sqrt(jnp.sum(values * values, axis=-1, keepdims=True) + EPSILON)
    return (values / length, length)


def project(grad, norm, length):
    return (grad - norm * jnp.sum(norm * grad, axis=-1, keepdims=True)) / length


def sensor_part(feats, proj_weight, texts, diagonal):
    raw = jnp.dot(feats, proj_weight, preferred_element_type=F32)
    norm, length = normalize(raw)
    unit = norm.astype(BF16)
    logits = LOGIT_SCALE * jnp.dot(unit, texts.T, preferred_element_type=F32) + LOGIT_BIAS
    slopes = jax.nn.sigmoid(logits)
    if diagonal:
        rows = lax.broadcasted_iota(jnp.int32, slopes.shape, 0)
        columns = lax.broadcasted_iota(jnp.int32, slopes.shape, 1)
        slopes = slopes - (rows == columns).astype(F32)
    slopes = slopes.astype(BF16)
    grad = LOGIT_SCALE * jnp.dot(slopes, texts, preferred_element_type=F32)
    return unit, slopes, project(grad, norm, length).astype(BF16)


def local(sensor_feats, proj_weight, text_feats):
    rows = sensor_feats.shape[0]
    half = rows // 2
    text_y = send(text_feats, yh=1)
    text_c = send(text_feats, c=1)
    low, high = sensor_feats[:half], sensor_feats[half:]
    right_low = send(low, x=1)
    left_high = send(high, x=-1)
    right_high = send(high, x=1)
    left_low = send(low, x=-1)
    far_low = send(right_low, x=1)
    far_high = send(left_high, x=-1)
    text_yc = send(text_y, c=1)

    text_norm, text_len = normalize(text_feats.astype(F32))
    y_norm, y_len = normalize(text_y.astype(F32))
    texts = jnp.concatenate(
        [
            text_norm.astype(BF16),
            y_norm.astype(BF16),
            normalize(text_c.astype(F32))[0].astype(BF16),
            normalize(text_yc.astype(F32))[0].astype(BF16),
        ]
    )
    feats = [
        sensor_feats,
        jnp.concatenate([right_low, right_high]),
        jnp.concatenate([left_low, left_high]),
        jnp.concatenate([far_low, far_high]),
    ]
    parts = [sensor_part(f, proj_weight, texts, k == 0) for k, f in enumerate(feats)]
    units, slopes, raw_grads = (jnp.concatenate(p) for p in zip(*parts))
    feats = jnp.concatenate(feats)

    core = lax.axis_index("c")
    weight_part = jnp.dot(feats.T, raw_grads, preferred_element_type=F32)
    weight_part = weight_part.reshape(8, 2, 64, weight_part.shape[1])
    mine = jnp.where(core == 0, weight_part[:, 0], weight_part[:, 1])
    other = jnp.where(core == 0, weight_part[:, 1], weight_part[:, 0])
    weight_sum = (mine + send(other.astype(BF16), c=1).astype(F32)).astype(BF16)

    text_part = LOGIT_SCALE * jnp.dot(slopes.T, units, preferred_element_type=F32)
    text_sum = text_part[: 2 * rows] + send(text_part[2 * rows :], c=1)
    text_out = send(project(text_sum[rows:], y_norm, y_len).astype(BF16), yh=1)

    weight_all = lax.all_to_all(weight_sum, ("x", "yh"), split_axis=0, concat_axis=0, tiled=True)
    weight_sum = jnp.sum(weight_all.astype(F32), axis=0).astype(BF16)
    across = send(weight_sum, z=2)
    ahead, behind = send(weight_sum, z=1), send(weight_sum, z=-1)
    weight_sum = (
        (weight_sum.astype(F32) + across.astype(F32)) + (ahead.astype(F32) + behind.astype(F32))
    ).astype(BF16)
    weight_grad = weight_sum.astype(F32) + send(weight_sum, yl=1).astype(F32)

    text_grad = project(text_sum[:rows], text_norm, text_len) + text_out.astype(F32)
    return (text_grad, weight_grad)


def solution(mesh):
    fine = Mesh(mesh.devices.reshape(SIZES), AXES)
    return jax.shard_map(
        local,
        mesh=fine,
        in_specs=(P(AXES, None), P(), P(AXES, None)),
        out_specs=(P(AXES, None), P(("x", "yh", "c"), None)),
        check_vma=False,
    )
```

time: 725 us -> 140 us (0.19)
  waiting for transfers between devices: 542 us -> 35.1 us
  matrix products: 110 us -> 34 us
  local copies, waits for them, and re-layouts: 42.6 us -> 9.16 us
  blocking collectives: 0 us -> 21.3 us
  starting transfers between devices: 4.83 us -> 22.5 us
  between operations: 14.1 us -> 0.94 us
  other arithmetic: 8.94 us -> 16.8 us
    ppermute x32 -> x16, waiting for transfers between devices: 392 us -> 35.1 us  [send(): return lax.ppermute(block, AXES, route)]
    unnamed x3 -> x0, waiting for transfers between devices: 77.5 us -> none
    dot_general x50 -> x14, matrix products: 110 us -> 34 us  [the longest x4 15.8 us: sensor_part(): jnp.dot(unit, texts.T, preferred_element_type=F32)]
    psum x1 -> x0, waiting for transfers between devices: 73 us -> none  [local(): weight_grad = lax.psum(partial_rows, 'replica')]
    while x80 -> x0, local copies, waits for them, and re-layouts: 32.7 us -> none
    all_to_all x0 -> x1, blocking collectives: none -> 21.3 us  [local(): lax.all_to_all(weight_sum, ('x', 'yh'), split_axis=0, concat_axis=0, tile...]
    ppermute x32 -> x16, starting transfers between devices: 4.75 us -> 22.5 us  [send(): return lax.ppermute(block, AXES, route)]
  transfers between devices with their start and end apart: 34 -> 16, of which waited for: 18 -> 6; matrix products, arithmetic and copies ran while one was open for 8% -> 21% of each run, Pallas kernels for 0% -> 0%
where the time goes in v1:
time: 140 us
  waiting for transfers between devices  35.1 us (25%)
  matrix products  34 us (24%)
  starting transfers between devices  22.5 us (16%)
  blocking collectives  21.3 us (15%)
  other arithmetic  16.8 us (12%)
  local copies, waits for them, and re-layouts  9.16 us (7%)
    ppermute x16, waiting for transfers between devices, send(): return lax.ppermute(block, AXES, route)  35.1 us
    ppermute x16, starting transfers between devices, send(): return lax.ppermute(block, AXES, route)  22.5 us
    all_to_all x1, blocking collectives, local(): lax.all_to_all(weight_sum, ('x', 'yh'), split_axis=0, concat_axis=0, tile...  21.3 us
    dot_general x4, matrix products, sensor_part(): jnp.dot(unit, texts.T, preferred_element_type=F32)  15.8 us
    dot_general x4, matrix products, sensor_part(): raw = jnp.dot(feats, proj_weight, preferred_element_type=F32)  6.81 us
    unnamed x18, local copies, waits for them, and re-layouts  5.13 us
    dot_general x4, matrix products, sensor_part(): grad = LOGIT_SCALE * jnp.dot(slopes, texts, preferred_element_type=F32)  4.68 us
    dot_general x1, matrix products, local(): jnp.dot(slopes.T, units, preferred_element_type=F32)  3.64 us
  transfers between devices with their start and end apart: 16, of which 6 were waited for; matrix products, arithmetic and copies ran while one was open for 21% of the time, Pallas kernels for 0%

profile of v1, /device:TPU:0, one launch (start us, length us, event | category | flops | bytes accessed | tf_op | source)
XLA Modules:
  0.0 139.8 jit_solution(2134179523994454554)
XLA Ops:
  0.7 3.4 %collective-permute-start = (bf16[320,1024]{1,0:T(8,128)(2,1)}, bf16[320,1024]{1,0:T(8,128)(2,1)S(1)}, u32[]{:S(2)}, u32[]{:S(2)}) collective-permute-start(bf16[320,1024]{1,0:T(8,128)(2,1)} %param.5), channel_id=1, source_target_pairs={{0,16},{1,17},{2,18},{3,19},{4,20},{5,21},{6,22},{7,23},{8,24},{9,... | collective-permute-start | bytes 1966088 | tf_op jit(solution)/shard_map/ppermute | solution.py:31
  4.0 1.9 %fusion.80 = (bf16[160,1024]{1,0:T(8,128)(2,1)}, bf16[160,1024]{1,0:T(8,128)(2,1)}) fusion(bf16[320,1024]{1,0:T(8,128)(2,1)} %param.3), kind=kLoop, calls=%fused_computation.139 | loop fusion | bytes 1310720 | tf_op jit(solution)/shard_map/slice | solution.py:63
  6.0 1.5 %collective-permute-start.4 = (bf16[160,1024]{1,0:T(8,128)(2,1)}, bf16[160,1024]{1,0:T(8,128)(2,1)}, u32[]{:S(2)}, u32[]{:S(2)}) collective-permute-start(bf16[160,1024]{1,0:T(8,128)(2,1)} %get-tuple-element.5), channel_id=1, source_target_pairs={{0,32},{1,33},{2,34},{3,35},{4,36},{5,37},{6,38},{7,39},{8,40},{9,... | collective-permute-start | bytes 983048 | tf_op jit(solution)/shard_map/ppermute | solution.py:31
  7.5 1.7 %collective-permute-start.6 = (bf16[160,1024]{1,0:T(8,128)(2,1)}, bf16[160,1024]{1,0:T(8,128)(2,1)}, u32[]{:S(2)}, u32[]{:S(2)}) collective-permute-start(bf16[160,1024]{1,0:T(8,128)(2,1)} %get-tuple-element.5), channel_id=1, source_target_pairs={{0,96},{1,97},{2,98},{3,99},{4,100},{5,101},{6,102},{7,103},{8,104... | collective-permute-start | bytes 983048 | tf_op jit(solution)/shard_map/ppermute | solution.py:31
  9.5 1.3 fusion.50
  10.8 0.9 constant_dynamic-update-slice_fusion.6
  11.7 1.9 %multiply_reduce_fusion.9 = (f32[320]{0:T(512)S(1)}, f32[320,1024]{1,0:T(8,128)}) fusion(bf16[320,1024]{1,0:T(8,128)(2,1)S(1)} %copy-done.4, bf16[1024,1024]{1,0:T(8,128)(2,1)S(1)} %copy-done), kind=kOutput, calls=%fused_computation.93 | convolution fusion | flops 671743680 | bytes 4064512 | tf_op jit(solution)/shard_map/dot_general | solution.py:44
  13.6 1.7 %fusion.74 = (bf16[320,1024]{1,0:T(8,128)(2,1)S(1)}, bf16[320,1024]{1,0:T(8,128)(2,1)S(1)}) fusion(f32[320]{0:T(512)S(1)} %add_sqrt_fusion.6, bf16[320,1024]{1,0:T(8,128)(2,1)S(1)} %copy-done.1, f32[320,1024]{1,0:T(8,128)} %get-tuple-element.13, f32[320]{0:T(512)S(1)} %add_sqrt_fusion.7), kind=kLoop, calls=%fused_computation.133 | loop fusion | flops 1638400 | bytes 3279360 | tf_op jit(solution)/shard_map/convert_element_type | solution.py:76
  15.3 9.3 %collective-permute-done.3 = bf16[160,1024]{1,0:T(8,128)(2,1)} collective-permute-done((bf16[160,1024]{1,0:T(8,128)(2,1)}, bf16[160,1024]{1,0:T(8,128)(2,1)}, u32[]{:S(2)}, u32[]{:S(2)}) %collective-permute-start.3) | collective-permute-done | bytes 327712 | tf_op jit(solution)/shard_map/ppermute | solution.py:31
  24.6 1.5 %collective-permute-start.5 = (bf16[160,1024]{1,0:T(8,128)(2,1)}, bf16[160,1024]{1,0:T(8,128)(2,1)S(1)}, u32[]{:S(2)}, u32[]{:S(2)}) collective-permute-start(bf16[160,1024]{1,0:T(8,128)(2,1)} %get-tuple-element.4), channel_id=1, source_target_pairs={{0,96},{1,97},{2,98},{3,99},{4,100},{5,101},{6,102},{7,103},{8,104... | collective-permute-start | bytes 983048 | tf_op jit(solution)/shard_map/ppermute | solution.py:31
  26.2 2.0 %multiply_reduce_fusion.8 = (f32[320]{0:T(512)S(1)}, f32[320,1024]{1,0:T(8,128)S(1)}) fusion(bf16[1024,1024]{1,0:T(8,128)(2,1)S(1)} %copy-done, bf16[160,1024]{1,0:T(8,128)(2,1)} %collective-permute-done.4, bf16[160,1024]{1,0:T(8,128)(2,1)} %collective-permute-done.3), kind=kOutput, calls=%fused_computation.92 | convolution fusion | flops 673054400 | bytes 4064512 | tf_op jit(solution)/shard_map/dot_general | solution.py:44
  28.2 6.0 %collective-permute-done.5 = bf16[160,1024]{1,0:T(8,128)(2,1)S(1)} collective-permute-done((bf16[160,1024]{1,0:T(8,128)(2,1)}, bf16[160,1024]{1,0:T(8,128)(2,1)S(1)}, u32[]{:S(2)}, u32[]{:S(2)}) %collective-permute-start.5) | collective-permute-done | bytes 327712 | tf_op jit(solution)/shard_map/ppermute | solution.py:31
  34.2 1.9 %multiply_reduce_fusion.7 = (f32[320]{0:T(512)S(1)}, f32[320,1024]{1,0:T(8,128)S(1)}) fusion(bf16[1024,1024]{1,0:T(8,128)(2,1)S(1)} %copy-done, bf16[160,1024]{1,0:T(8,128)(2,1)} %collective-permute-done.6, bf16[160,1024]{1,0:T(8,128)(2,1)S(1)} %collective-permute-done.5), kind=kOutput, calls=%fused_computation.91 | convolution fusion | flops 673054400 | bytes 4064512 | tf_op jit(solution)/shard_map/dot_general | solution.py:44
  36.1 0.3 collective-permute-start.7
  36.5 3.0 %collective-permute-start.8 = (bf16[160,1024]{1,0:T(8,128)(2,1)}, bf16[160,1024]{1,0:T(8,128)(2,1)S(1)}, u32[]{:S(2)}, u32[]{:S(2)}) collective-permute-start(bf16[160,1024]{1,0:T(8,128)(2,1)} %collective-permute-done.6), channel_id=1, source_target_pairs={{0,96},{1,97},{2,98},{3,99},{4,100},{5,101},{6,102},{7,103},{8,104... | collective-permute-start | bytes 983048 | tf_op jit(solution)/shard_map/ppermute | solution.py:31
  39.4 1.0 constant_dynamic-update-slice_fusion.5
  40.4 1.0 constant_dynamic-update-slice_fusion.4
  41.7 1.0 constant_dynamic-update-slice_fusion.2
  43.1 1.3 fusion.52
  44.4 1.6 %collective-permute-done.7 = bf16[160,1024]{1,0:T(8,128)(2,1)S(1)} collective-permute-done((bf16[160,1024]{1,0:T(8,128)(2,1)}, bf16[160,1024]{1,0:T(8,128)(2,1)S(1)}, u32[]{:S(2)}, u32[]{:S(2)}) %collective-permute-start.7) | collective-permute-done | bytes 327712 | tf_op jit(solution)/shard_map/ppermute | solution.py:31
  46.1 1.0 multiply_reduce_fusion.6
  47.7 1.4 fusion.53
  49.9 4.0 %fusion.31 = bf16[320,1280]{1,0:T(8,128)(2,1)S(1)} fusion(bf16[320,1024]{1,0:T(8,128)(2,1)S(1)} %get-tuple-element.23, bf16[320,1024]{1,0:T(8,128)(2,1)S(1)} %fusion.55, bf16[320,1024]{1,0:T(8,128)(2,1)S(1)} %fusion.53, bf16[320,1024]{1,0:T(8,128)(2,1)S(1)} %fusion.75, bf16[320,1024]{1,0:T(8,128)(2,1)S(1)} %get-tuple-element.22), kind=kOutput, calls=%fused_computation.36 | convolution fusion | flops 853032960 | bytes 4096000 | tf_op jit(solution)/shard_map/dot_general | solution.py:47
  54.0 1.2 multiply_reduce_fusion.3
  55.1 3.9 %fusion.30 = bf16[320,1280]{1,0:T(8,128)(2,1)S(1)} fusion(bf16[320,1024]{1,0:T(8,128)(2,1)S(1)} %fusion.77, bf16[320,1024]{1,0:T(8,128)(2,1)S(1)} %fusion.55, bf16[320,1024]{1,0:T(8,128)(2,1)S(1)} %fusion.53, bf16[320,1024]{1,0:T(8,128)(2,1)S(1)} %fusion.75, bf16[320,1024]{1,0:T(8,128)(2,1)S(1)} %get-tuple-element.22), kind=kOutput, calls=%fused_computation.35 | convolution fusion | flops 851804160 | bytes 4096000 | tf_op jit(solution)/shard_map/dot_general | solution.py:47
  59.0 1.2 multiply_reduce_fusion.2
  60.2 3.9 %fusion.29 = bf16[320,1280]{1,0:T(8,128)(2,1)S(1)} fusion(bf16[320,1024]{1,0:T(8,128)(2,1)S(1)} %fusion.78, bf16[320,1024]{1,0:T(8,128)(2,1)S(1)} %fusion.55, bf16[320,1024]{1,0:T(8,128)(2,1)S(1)} %fusion.53, bf16[320,1024]{1,0:T(8,128)(2,1)S(1)} %fusion.75, bf16[320,1024]{1,0:T(8,128)(2,1)S(1)} %get-tuple-element.22), kind=kOutput, calls=%fused_computation.34 | convolution fusion | flops 851804160 | bytes 4096000 | tf_op jit(solution)/shard_map/dot_general | solution.py:47
  64.0 1.2 multiply_reduce_fusion.1
  65.2 4.1 %fusion.28 = bf16[320,1280]{1,0:T(8,128)(2,1)S(1)} fusion(bf16[320,1024]{1,0:T(8,128)(2,1)S(1)} %fusion.79, bf16[320,1024]{1,0:T(8,128)(2,1)S(1)} %fusion.55, bf16[320,1024]{1,0:T(8,128)(2,1)S(1)} %fusion.53, bf16[320,1024]{1,0:T(8,128)(2,1)S(1)} %fusion.75, bf16[320,1024]{1,0:T(8,128)(2,1)S(1)} %get-tuple-element.22), kind=kOutput, calls=%fused_computation.33 | convolution fusion | flops 851804160 | bytes 4096000 | tf_op jit(solution)/shard_map/dot_general | solution.py:47
  69.3 1.2 multiply_reduce_fusion
  70.5 3.6 %convolution_multiply_fusion = f32[1280,1024]{1,0:T(8,128)S(1)} fusion(bf16[320,1280]{1,0:T(8,128)(2,1)S(1)} %fusion.28, bf16[320,1280]{1,0:T(8,128)(2,1)S(1)} %fusion.29, bf16[320,1280]{1,0:T(8,128)(2,1)S(1)} %fusion.30, bf16[320,1280]{1,0:T(8,128)(2,1)S(1)} %fusion.31, bf16[320,1024]{1,0:T(8,128)(2,1)S(1)} %fusion.79, bf16[320,1024]{1,0:T(8,128)(2,1)S(1)} %fusion.78, ...), kind=kOutput, calls=%fused_computation | convolution fusion | flops 3380346880 | bytes 11141120 | tf_op jit(solution)/shard_map/dot_general | solution.py:99
  74.1 2.1 %slice.35 = f32[640,1024]{1,0:T(8,128)} slice(f32[1280,1024]{1,0:T(8,128)S(1)} %convolution_multiply_fusion), slice={[640:1280], [0:1024]} | slice | bytes 5242880 | tf_op jit(solution)/shard_map/slice | solution.py:100
  76.2 1.2 copy-done.3
  78.9 3.0 %fusion.39 = f32[1024,1024]{1,0:T(8,128)S(1)} fusion(bf16[1280,1024]{1,0:T(8,128)(2,1)S(1)} %constant_dynamic-update-slice_fusion, bf16[320,1024]{1,0:T(8,128)(2,1)S(1)} %divide_convert_fusion, bf16[320,1024]{1,0:T(8,128)(2,1)S(1)} %divide_convert_fusion.1, bf16[320,1024]{1,0:T(8,128)(2,1)S(1)} %divide_convert_fusion.2, ...), kind=kOutput, calls=%fused_computation.46 | convolution fusion | flops 2694840320 | bytes 9437184 | tf_op jit(solution)/shard_map/dot_general | solution.py:93
  82.3 2.5 %collective-permute-done.11 = bf16[8,64,1024]{2,1,0:T(8,128)(2,1)S(1)} collective-permute-done((bf16[8,64,1024]{2,1,0:T(8,128)(2,1)S(1)}, bf16[8,64,1024]{2,1,0:T(8,128)(2,1)S(1)}, u32[]{:S(2)}, u32[]{:S(2)}) %collective-permute-start.11) | collective-permute-done | bytes 1048608 | tf_op jit(solution)/shard_map/ppermute | solution.py:31
  84.8 0.6 fusion.49
  85.4 21.3 %all_to_all.5 = bf16[8,64,1024]{2,1,0:T(8,128)(2,1)} all-to-all(bf16[8,64,1024]{2,1,0:T(8,128)(2,1)S(1)} %fusion.49), channel_id=1, replica_groups=mesh['x'=4,'yh'=2,'c'=2,'z'=4,'yl'=2] {'x','yh'}, dimensions={0} | all-to-all | bytes 2097152 | tf_op jit(solution)/shard_map/all_to_all | solution.py:103
  106.7 1.4 %reduce_sum.152 = bf16[64,1024]{1,0:T(8,128)(2,1)S(1)} reduce(bf16[8,64,1024]{2,1,0:T(8,128)(2,1)} %all_to_all.5, bf16[]{:T(256)} %constant.21.clone.1), dimensions={0}, to_apply=%region_14.15 | reduce | flops 458752 | bytes 1179650 | tf_op jit(solution)/shard_map/reduce_sum | solution.py:104
  108.2 4.0 %collective-permute-start.12 = (bf16[64,1024]{1,0:T(8,128)(2,1)S(1)}, bf16[64,1024]{1,0:T(8,128)(2,1)S(1)}, u32[]{:S(2)}, u32[]{:S(2)}) collective-permute-start(bf16[64,1024]{1,0:T(8,128)(2,1)S(1)} %reduce_sum.152), channel_id=1, source_target_pairs={{0,4},{1,5},{2,6},{3,7},{4,0},{5,1},{6,2},{7,3},{8,12},{9,13},{10,... | collective-permute-start | bytes 393224 | tf_op jit(solution)/shard_map/ppermute | solution.py:31
  112.1 1.0 collective-permute-start.13
  113.1 2.2 %collective-permute-start.14 = (bf16[64,1024]{1,0:T(8,128)(2,1)S(1)}, bf16[64,1024]{1,0:T(8,128)(2,1)S(1)}, u32[]{:S(2)}, u32[]{:S(2)}) collective-permute-start(bf16[64,1024]{1,0:T(8,128)(2,1)S(1)} %reduce_sum.152), channel_id=1, source_target_pairs={{0,6},{1,7},{2,0},{3,1},{4,2},{5,3},{6,4},{7,5},{8,14},{9,15},{10,... | collective-permute-start | bytes 393224 | tf_op jit(solution)/shard_map/ppermute | solution.py:31
  115.4 3.1 %slice_add_fusion = f32[640,1024]{1,0:T(8,128)S(1)} fusion(f32[640,1024]{1,0:T(8,128)} %collective-permute-done.9, f32[1280,1024]{1,0:T(8,128)} %copy-done.3), kind=kLoop, calls=%fused_computation.37 | loop fusion | flops 655360 | bytes 7864320 | tf_op jit(solution)/shard_map/add | solution.py:100
  118.5 0.5 multiply_reduce_fusion.5
  119.4 1.3 collective-permute-start.10
  120.7 1.4 %collective-permute-start.15 = (bf16[64,1024]{1,0:T(8,128)(2,1)S(1)}, bf16[64,1024]{1,0:T(8,128)(2,1)S(1)}, u32[]{:S(2)}, u32[]{:S(2)}) collective-permute-start(bf16[64,1024]{1,0:T(8,128)(2,1)S(1)} %add_convert_fusion), channel_id=1, source_target_pairs={{0,1},{1,0},{2,3},{3,2},{4,5},{5,4},{6,7},{7,6},{8,9},{9,8},{10,11... | collective-permute-start | bytes 393224 | tf_op jit(solution)/shard_map/ppermute | solution.py:31
  122.2 15.4 %collective-permute-done.15 = bf16[64,1024]{1,0:T(8,128)(2,1)S(1)} collective-permute-done((bf16[64,1024]{1,0:T(8,128)(2,1)S(1)}, bf16[64,1024]{1,0:T(8,128)(2,1)S(1)}, u32[]{:S(2)}, u32[]{:S(2)}) %collective-permute-start.15) | collective-permute-done | bytes 131104 | tf_op jit(solution)/shard_map/ppermute | solution.py:31
  137.6 0.7 convert_add_fusion.1
  138.4 1.4 %convert_add_fusion = f32[320,1024]{1,0:T(8,128)} fusion(bf16[320,1024]{1,0:T(8,128)(2,1)S(1)} %collective-permute-done.10, f32[640,1024]{1,0:T(8,128)S(1)} %slice_add_fusion, f32[320]{0:T(512)S(1)} %get-tuple-element.2, f32[320]{0:T(512)S(1)} %add_sqrt_fusion.6, bf16[320,1024]{1,0:T(8,128)(2,1)S(1)} %copy-done.1), kind=kLoop, calls=%fused_computation.86 | loop fusion | flops 2293760 | bytes 3934720 | tf_op jit(solution)/shard_map/add | solution.py:112
  (52 shorter events, 4.8 us)
Async XLA Ops:
  0.6 11.0 %copy-start = (bf16[1024,1024]{1,0:T(8,128)(2,1)S(1)}, bf16[1024,1024]{1,0:T(8,128)(2,1)}, u32[]{:S(2)}) copy-start(bf16[1024,1024]{1,0:T(8,128)(2,1)} %param.4) | copy-start | bytes 6291460
  0.6 10.2 %copy-start.4 = (bf16[320,1024]{1,0:T(8,128)(2,1)S(1)}, bf16[320,1024]{1,0:T(8,128)(2,1)}, u32[]{:S(2)}) copy-start(bf16[320,1024]{1,0:T(8,128)(2,1)} %param.3) | copy-start | bytes 1966084
  0.7 42.2 %collective-permute-start = (bf16[320,1024]{1,0:T(8,128)(2,1)}, bf16[320,1024]{1,0:T(8,128)(2,1)S(1)}, u32[]{:S(2)}, u32[]{:S(2)}) collective-permute-start(bf16[320,1024]{1,0:T(8,128)(2,1)} %param.5), channel_id=1, source_target_pairs={{0,16},{1,17},{2,18},{3,19},{4,20},{5,21},{6,22},{7,23},{8,24},{9,... | collective-permute-start | bytes 1966088 | tf_op jit(solution)/shard_map/ppermute | solution.py:31
  4.0 39.1 %collective-permute-start.1 = (bf16[320,1024]{1,0:T(8,128)(2,1)}, bf16[320,1024]{1,0:T(8,128)(2,1)}, u32[]{:S(2)}, u32[]{:S(2)}) collective-permute-start(bf16[320,1024]{1,0:T(8,128)(2,1)} %param.5), channel_id=1, source_target_pairs={{0,8},{1,9},{2,10},{3,11},{4,12},{5,13},{6,14},{7,15},{8,0},{9,1},... | collective-permute-start | bytes 1966088 | tf_op jit(solution)/shard_map/ppermute | solution.py:31
  6.0 20.2 %collective-permute-start.4 = (bf16[160,1024]{1,0:T(8,128)(2,1)}, bf16[160,1024]{1,0:T(8,128)(2,1)}, u32[]{:S(2)}, u32[]{:S(2)}) collective-permute-start(bf16[160,1024]{1,0:T(8,128)(2,1)} %get-tuple-element.5), channel_id=1, source_target_pairs={{0,32},{1,33},{2,34},{3,35},{4,36},{5,37},{6,38},{7,39},{8,40},{9,... | collective-permute-start | bytes 983048 | tf_op jit(solution)/shard_map/ppermute | solution.py:31
  7.5 20.8 %collective-permute-start.6 = (bf16[160,1024]{1,0:T(8,128)(2,1)}, bf16[160,1024]{1,0:T(8,128)(2,1)}, u32[]{:S(2)}, u32[]{:S(2)}) collective-permute-start(bf16[160,1024]{1,0:T(8,128)(2,1)} %get-tuple-element.5), channel_id=1, source_target_pairs={{0,96},{1,97},{2,98},{3,99},{4,100},{5,101},{6,102},{7,103},{8,104... | collective-permute-start | bytes 983048 | tf_op jit(solution)/shard_map/ppermute | solution.py:31
  9.2 15.4 %collective-permute-start.3 = (bf16[160,1024]{1,0:T(8,128)(2,1)}, bf16[160,1024]{1,0:T(8,128)(2,1)}, u32[]{:S(2)}, u32[]{:S(2)}) collective-permute-start(bf16[160,1024]{1,0:T(8,128)(2,1)} %get-tuple-element.4), channel_id=1, source_target_pairs={{0,32},{1,33},{2,34},{3,35},{4,36},{5,37},{6,38},{7,39},{8,40},{9,... | collective-permute-start | bytes 983048 | tf_op jit(solution)/shard_map/ppermute | solution.py:31
  11.7 1.9 %copy-start.1 = (bf16[320,1024]{1,0:T(8,128)(2,1)S(1)}, bf16[320,1024]{1,0:T(8,128)(2,1)}, u32[]{:S(2)}) copy-start(bf16[320,1024]{1,0:T(8,128)(2,1)} %param.5) | copy-start | bytes 1966084
  24.6 9.6 %collective-permute-start.5 = (bf16[160,1024]{1,0:T(8,128)(2,1)}, bf16[160,1024]{1,0:T(8,128)(2,1)S(1)}, u32[]{:S(2)}, u32[]{:S(2)}) collective-permute-start(bf16[160,1024]{1,0:T(8,128)(2,1)} %get-tuple-element.4), channel_id=1, source_target_pairs={{0,96},{1,97},{2,98},{3,99},{4,100},{5,101},{6,102},{7,103},{8,104... | collective-permute-start | bytes 983048 | tf_op jit(solution)/shard_map/ppermute | solution.py:31
  28.2 11.2 %copy-start.5 = (bf16[1280,1024]{1,0:T(8,128)(2,1)S(1)}, bf16[1280,1024]{1,0:T(8,128)(2,1)}, u32[]{:S(2)}) copy-start(bf16[1280,1024]{1,0:T(8,128)(2,1)} %constant_dynamic-update-slice_fusion.6) | copy-start | bytes 7864324
  36.1 9.9 %collective-permute-start.7 = (bf16[160,1024]{1,0:T(8,128)(2,1)}, bf16[160,1024]{1,0:T(8,128)(2,1)S(1)}, u32[]{:S(2)}, u32[]{:S(2)}) collective-permute-start(bf16[160,1024]{1,0:T(8,128)(2,1)} %collective-permute-done.3), channel_id=1, source_target_pairs={{0,32},{1,33},{2,34},{3,35},{4,36},{5,37},{6,38},{7,39},{8,40},{9,... | collective-permute-start | bytes 983048 | tf_op jit(solution)/shard_map/ppermute | solution.py:31
  36.5 9.6 %collective-permute-start.8 = (bf16[160,1024]{1,0:T(8,128)(2,1)}, bf16[160,1024]{1,0:T(8,128)(2,1)S(1)}, u32[]{:S(2)}, u32[]{:S(2)}) collective-permute-start(bf16[160,1024]{1,0:T(8,128)(2,1)} %collective-permute-done.6), channel_id=1, source_target_pairs={{0,96},{1,97},{2,98},{3,99},{4,100},{5,101},{6,102},{7,103},{8,104... | collective-permute-start | bytes 983048 | tf_op jit(solution)/shard_map/ppermute | solution.py:31
  47.0 2.4 %collective-permute-start.2 = (bf16[320,1024]{1,0:T(8,128)(2,1)S(1)}, bf16[320,1024]{1,0:T(8,128)(2,1)S(1)}, u32[]{:S(2)}, u32[]{:S(2)}) collective-permute-start(bf16[320,1024]{1,0:T(8,128)(2,1)S(1)} %collective-permute-done), channel_id=1, source_target_pairs={{0,8},{1,9},{2,10},{3,11},{4,12},{5,13},{6,14},{7,15},{8,0},{9,1},... | collective-permute-start | bytes 1966088 | tf_op jit(solution)/shard_map/ppermute | solution.py:31
  49.9 4.0 %copy-start.2 = (f32[320,1024]{1,0:T(8,128)S(1)}, f32[320,1024]{1,0:T(8,128)}, u32[]{:S(2)}) copy-start(f32[320,1024]{1,0:T(8,128)} %get-tuple-element.13) | copy-start | bytes 3932164
  74.1 3.3 %copy-start.3 = (f32[1280,1024]{1,0:T(8,128)}, f32[1280,1024]{1,0:T(8,128)S(1)}, u32[]{:S(2)}) copy-start(f32[1280,1024]{1,0:T(8,128)S(1)} %convolution_multiply_fusion) | copy-start | bytes 15728644
  77.4 38.0 %collective-permute-start.9 = (f32[640,1024]{1,0:T(8,128)}, f32[640,1024]{1,0:T(8,128)}, u32[]{:S(2)}, u32[]{:S(2)}) collective-permute-start(f32[640,1024]{1,0:T(8,128)} %slice.35), channel_id=1, source_target_pairs={{0,8},{1,9},{2,10},{3,11},{4,12},{5,13},{6,14},{7,15},{8,0},{9,1},... | collective-permute-start | bytes 7864328 | tf_op jit(solution)/shard_map/ppermute | solution.py:31
  82.1 2.7 %collective-permute-start.11 = (bf16[8,64,1024]{2,1,0:T(8,128)(2,1)S(1)}, bf16[8,64,1024]{2,1,0:T(8,128)(2,1)S(1)}, u32[]{:S(2)}, u32[]{:S(2)}) collective-permute-start(bf16[8,64,1024]{2,1,0:T(8,128)(2,1)S(1)} %fusion.56), channel_id=1, source_target_pairs={{0,8},{1,9},{2,10},{3,11},{4,12},{5,13},{6,14},{7,15},{8,0},{9,1},... | collective-permute-start | bytes 3145736 | tf_op jit(solution)/shard_map/ppermute | solution.py:31
  108.2 12.5 %collective-permute-start.12 = (bf16[64,1024]{1,0:T(8,128)(2,1)S(1)}, bf16[64,1024]{1,0:T(8,128)(2,1)S(1)}, u32[]{:S(2)}, u32[]{:S(2)}) collective-permute-start(bf16[64,1024]{1,0:T(8,128)(2,1)S(1)} %reduce_sum.152), channel_id=1, source_target_pairs={{0,4},{1,5},{2,6},{3,7},{4,0},{5,1},{6,2},{7,3},{8,12},{9,13},{10,... | collective-permute-start | bytes 393224 | tf_op jit(solution)/shard_map/ppermute | solution.py:31
  112.1 8.5 %collective-permute-start.13 = (bf16[64,1024]{1,0:T(8,128)(2,1)S(1)}, bf16[64,1024]{1,0:T(8,128)(2,1)S(1)}, u32[]{:S(2)}, u32[]{:S(2)}) collective-permute-start(bf16[64,1024]{1,0:T(8,128)(2,1)S(1)} %reduce_sum.152), channel_id=1, source_target_pairs={{0,2},{1,3},{2,4},{3,5},{4,6},{5,7},{6,0},{7,1},{8,10},{9,11},{10,... | collective-permute-start | bytes 393224 | tf_op jit(solution)/shard_map/ppermute | solution.py:31
  113.1 7.5 %collective-permute-start.14 = (bf16[64,1024]{1,0:T(8,128)(2,1)S(1)}, bf16[64,1024]{1,0:T(8,128)(2,1)S(1)}, u32[]{:S(2)}, u32[]{:S(2)}) collective-permute-start(bf16[64,1024]{1,0:T(8,128)(2,1)S(1)} %reduce_sum.152), channel_id=1, source_target_pairs={{0,6},{1,7},{2,0},{3,1},{4,2},{5,3},{6,4},{7,5},{8,14},{9,15},{10,... | collective-permute-start | bytes 393224 | tf_op jit(solution)/shard_map/ppermute | solution.py:31
  119.4 19.0 %collective-permute-start.10 = (bf16[320,1024]{1,0:T(8,128)(2,1)S(1)}, bf16[320,1024]{1,0:T(8,128)(2,1)S(1)}, u32[]{:S(2)}, u32[]{:S(2)}) collective-permute-start(bf16[320,1024]{1,0:T(8,128)(2,1)S(1)} %divide_convert_fusion.4), channel_id=1, source_target_pairs={{0,16},{1,17},{2,18},{3,19},{4,20},{5,21},{6,22},{7,23},{8,24},{9,... | collective-permute-start | bytes 1966088 | tf_op jit(solution)/shard_map/ppermute | solution.py:31
  120.7 16.9 %collective-permute-start.15 = (bf16[64,1024]{1,0:T(8,128)(2,1)S(1)}, bf16[64,1024]{1,0:T(8,128)(2,1)S(1)}, u32[]{:S(2)}, u32[]{:S(2)}) collective-permute-start(bf16[64,1024]{1,0:T(8,128)(2,1)S(1)} %add_convert_fusion), channel_id=1, source_target_pairs={{0,1},{1,0},{2,3},{3,2},{4,5},{5,4},{6,7},{7,6},{8,9},{9,8},{10,11... | collective-permute-start | bytes 393224 | tf_op jit(solution)/shard_map/ppermute | solution.py:31

commit v2 on v1

v2 whole, which is shorter than its diff:
```python
import functools
import itertools

import jax
import jax.numpy as jnp
from jax import lax
from jax.experimental import pallas as pl
from jax.experimental.pallas import tpu as pltpu
from jax.sharding import Mesh, PartitionSpec as P

LOGIT_SCALE = 10.0
LOGIT_BIAS = -2.0
EPSILON = 1e-06

SIZES = (4, 2, 2, 4, 2)
AXES = ("x", "yh", "c", "z", "yl")
F32 = jnp.float32
BF16 = jnp.bfloat16


def position(coords):
    index = 0
    for size, coord in zip(SIZES, coords):
        index = index * size + coord % size
    return index


def send(block, **shift):
    step = [shift.get(name, 0) for name in AXES]
    route = [
        (position(at), position([a + s for a, s in zip(at, step)]))
        for at in itertools.product(*map(range, SIZES))
    ]
    return lax.ppermute(block, AXES, route)


def normalize(values):
    length = jnp.sqrt(jnp.sum(values * values, axis=-1, keepdims=True) + EPSILON)
    return (values / length, length)


def project(grad, norm, length):
    return (grad - norm * jnp.sum(norm * grad, axis=-1, keepdims=True)) / length


def sensor_kernel(diagonal, feats, proj_weight, texts, unit_out, slopes_out, raw_grad_out):
    raw = jnp.dot(feats[...], proj_weight[...], preferred_element_type=F32)
    norm, length = normalize(raw)
    unit = norm.astype(BF16)
    unit_out[...] = unit
    logits = LOGIT_SCALE * jnp.dot(unit, texts[...].T, preferred_element_type=F32) + LOGIT_BIAS
    slopes = jax.nn.sigmoid(logits)
    if diagonal:
        rows = lax.broadcasted_iota(jnp.int32, slopes.shape, 0)
        columns = lax.broadcasted_iota(jnp.int32, slopes.shape, 1)
        slopes = slopes - (rows == columns).astype(F32)
    slopes = slopes.astype(BF16)
    slopes_out[...] = slopes
    grad = LOGIT_SCALE * jnp.dot(slopes, texts[...], preferred_element_type=F32)
    raw_grad_out[...] = project(grad, norm, length).astype(BF16)


def sensor_part(feats, proj_weight, texts, diagonal):
    rows, depth = feats.shape
    width, columns = proj_weight.shape[1], texts.shape[0]
    whole = pl.BlockSpec(memory_space=pltpu.VMEM)
    return pl.pallas_call(
        functools.partial(sensor_kernel, diagonal),
        out_shape=(
            jax.ShapeDtypeStruct((rows, width), BF16),
            jax.ShapeDtypeStruct((rows, columns), BF16),
            jax.ShapeDtypeStruct((rows, width), BF16),
        ),
        in_specs=[whole] * 3,
        out_specs=(whole,) * 3,
        compiler_params=pltpu.CompilerParams(vmem_limit_bytes=40 * 1024 * 1024),
        cost_estimate=pl.CostEstimate(
            flops=2 * rows * width * (depth + 2 * columns),
            bytes_accessed=2 * (rows * (depth + 2 * width + columns) + (depth + columns) * width),
            transcendentals=rows * columns,
        ),
    )(feats, proj_weight, texts)


def local(sensor_feats, proj_weight, text_feats):
    rows = sensor_feats.shape[0]
    half = rows // 2
    right, left = send(sensor_feats, x=1), send(sensor_feats, x=-1)
    text_y, text_c = send(text_feats, yh=1), send(text_feats, c=1)
    text_norm, text_len = normalize(text_feats.astype(F32))
    c_unit = normalize(text_c.astype(F32))[0].astype(BF16)
    far_low, far_high = send(right[:half], x=1), send(left[half:], x=-1)
    text_yc = send(text_y, c=1)
    y_norm, y_len = normalize(text_y.astype(F32))
    yc_unit = normalize(text_yc.astype(F32))[0].astype(BF16)
    texts = jnp.concatenate([text_norm.astype(BF16), y_norm.astype(BF16), c_unit, yc_unit])

    feats = [sensor_feats, right, left]
    parts = [sensor_part(f, proj_weight, texts, k == 0) for k, f in enumerate(feats)]
    parts, far_low, far_high = lax.optimization_barrier((parts, far_low, far_high))
    feats.append(jnp.concatenate([far_low, far_high]))
    parts.append(sensor_part(feats[-1], proj_weight, texts, False))
    units, slopes, raw_grads = (jnp.concatenate(p) for p in zip(*parts))
    feats = jnp.concatenate(feats)

    core = lax.axis_index("c")
    weight_part = jnp.dot(feats.T, raw_grads, preferred_element_type=F32)
    weight_part = weight_part.reshape(8, 2, 64, weight_part.shape[1])
    mine = jnp.where(core == 0, weight_part[:, 0], weight_part[:, 1])
    other = jnp.where(core == 0, weight_part[:, 1], weight_part[:, 0]).astype(BF16)
    other, units, slopes = lax.optimization_barrier((other, units, slopes))
    weight_recv = send(other, c=1)
    text_part = LOGIT_SCALE * jnp.dot(slopes.T, units, preferred_element_type=F32)
    weight_recv, text_part = lax.optimization_barrier((weight_recv, text_part))
    weight_sum = (mine + weight_recv.astype(F32)).astype(BF16)

    text_recv = send(text_part[2 * rows :], c=1)
    weight_all = lax.all_to_all(weight_sum, ("x", "yh"), split_axis=0, concat_axis=0, tiled=True)
    text_sum = text_part[: 2 * rows] + text_recv
    text_send = project(text_sum[rows:], y_norm, y_len).astype(BF16)
    text_out = send(text_send, yh=1)
    weight_sum = jnp.sum(weight_all.astype(F32), axis=0).astype(BF16)
    across = send(weight_sum, z=2)
    ahead, behind = send(weight_sum, z=1), send(weight_sum, z=-1)
    weight_sum = (
        (weight_sum.astype(F32) + across.astype(F32)) + (ahead.astype(F32) + behind.astype(F32))
    ).astype(BF16)
    weight_sum, text_out = lax.optimization_barrier((weight_sum, text_out))
    weight_grad = weight_sum.astype(F32) + send(weight_sum, yl=1).astype(F32)

    text_grad = project(text_sum[:rows], text_norm, text_len) + text_out.astype(F32)
    return (text_grad, weight_grad)


def solution(mesh):
    fine = Mesh(mesh.devices.reshape(SIZES), AXES)
    return jax.shard_map(
        local,
        mesh=fine,
        in_specs=(P(AXES, None), P(), P(AXES, None)),
        out_specs=(P(AXES, None), P(("x", "yh", "c"), None)),
        check_vma=False,
    )
```

time: 140 us -> 96.5 us (0.69)
  matrix products: 34 us -> 6.77 us
  blocking collectives: 21.3 us -> 0 us
  Pallas kernels: 0 us -> 13.2 us
  waiting for transfers between devices: 35.1 us -> 24.5 us
  starting transfers between devices: 22.5 us -> 27.9 us
  local copies, waits for them, and re-layouts: 9.16 us -> 5.72 us
    dot_general x12 -> x0, matrix products: 27.3 us -> none  [the longest x4 15.8 us: sensor_part(): jnp.dot(unit, texts.T, preferred_element_type=F32)]
    all_to_all x1 -> x0, blocking collectives: 21.3 us -> none  [local(): lax.all_to_all(weight_sum, ('x', 'yh'), split_axis=0, concat_axis=0, tile...]
    ppermute x16 -> x14, waiting for transfers between devices: 35.1 us -> 16.3 us  [send(): return lax.ppermute(block, AXES, route)]
    pallas_call x0 -> x4, Pallas kernels: none -> 13.2 us  [sensor_part(): pl.pallas_call(functools.partial(sensor_kernel, diagonal), out_shape=(jax...]
    all_to_all x0 -> x1, waiting for transfers between devices: none -> 8.24 us  [local(): lax.all_to_all(weight_sum, ('x', 'yh'), split_axis=0, concat_axis=0, tile...]
    all_to_all x0 -> x1, starting transfers between devices: none -> 7.15 us  [local(): lax.all_to_all(weight_sum, ('x', 'yh'), split_axis=0, concat_axis=0, tile...]
    slice x2 -> x3, local copies, waits for them, and re-layouts: 4.01 us -> 0.36 us  [the longest x1 0.32 us: local(): text_recv = send(text_part[2 * rows:], c=1)]
    ppermute x16 -> x14, starting transfers between devices: 22.5 us -> 20.8 us  [send(): return lax.ppermute(block, AXES, route)]
  transfers between devices with their start and end apart: 16 -> 15, of which waited for: 6 -> 7; matrix products, arithmetic and copies ran while one was open for 21% -> 22% of each run, Pallas kernels for 0% -> 10%
where the time goes in v2:
time: 96.5 us; the launch traced here: 96.1 us
  starting transfers between devices  27.9 us (29%)
  waiting for transfers between devices  24.5 us (25%)
  other arithmetic  17 us (18%)
  Pallas kernels  13.2 us (14%)
  matrix products  6.77 us (7%)
  local copies, waits for them, and re-layouts  5.72 us (6%)
    ppermute x14, starting transfers between devices, send(): return lax.ppermute(block, AXES, route)  20.8 us
    ppermute x14, waiting for transfers between devices, send(): return lax.ppermute(block, AXES, route)  16.3 us
    pallas_call x4, Pallas kernels, sensor_part(): pl.pallas_call(functools.partial(sensor_kernel, diagonal), out_shape=(jax...  13.2 us
    all_to_all x1, waiting for transfers between devices, local(): lax.all_to_all(weight_sum, ('x', 'yh'), split_axis=0, concat_axis=0, tile...  8.24 us
    all_to_all x1, starting transfers between devices, local(): lax.all_to_all(weight_sum, ('x', 'yh'), split_axis=0, concat_axis=0, tile...  7.15 us
    unnamed x14, local copies, waits for them, and re-layouts  5.33 us
    dot_general x1, matrix products, local(): jnp.dot(slopes.T, units, preferred_element_type=F32)  3.6 us
    dot_general x1, matrix products, local(): weight_part = jnp.dot(feats.T, raw_grads, preferred_element_type=F32)  3.17 us
  transfers between devices with their start and end apart: 15, of which 7 were waited for; matrix products, arithmetic and copies ran while one was open for 22% of the time, Pallas kernels for 10%

profile of v2, /device:TPU:0, one launch (start us, length us, event | category | flops | bytes accessed | tf_op | source)
XLA Modules:
  0.0 96.1 jit_solution(12872188333838331564)
XLA Ops:
  0.6 2.9 %collective-permute-start.1 = (bf16[320,1024]{1,0:T(8,128)(2,1)}, bf16[320,1024]{1,0:T(8,128)(2,1)S(1)}, u32[]{:S(2)}, u32[]{:S(2)}) collective-permute-start(bf16[320,1024]{1,0:T(8,128)(2,1)} %feats.1), channel_id=1, source_target_pairs={{0,96},{1,97},{2,98},{3,99},{4,100},{5,101},{6,102},{7,103},{8,104... | collective-permute-start | bytes 1966088 | tf_op jit(solution)/shard_map/ppermute | solution.py:34
  3.5 3.2 %collective-permute-start.2 = (bf16[320,1024]{1,0:T(8,128)(2,1)}, bf16[320,1024]{1,0:T(8,128)(2,1)S(1)}, u32[]{:S(2)}, u32[]{:S(2)}) collective-permute-start(bf16[320,1024]{1,0:T(8,128)(2,1)} %param.5), channel_id=1, source_target_pairs={{0,16},{1,17},{2,18},{3,19},{4,20},{5,21},{6,22},{7,23},{8,24},{9,... | collective-permute-start | bytes 1966088 | tf_op jit(solution)/shard_map/ppermute | solution.py:34
  6.7 1.3 %fusion.10 = f32[320]{0:T(512)S(1)} fusion(bf16[320,1024]{1,0:T(8,128)(2,1)} %param.5), kind=kLoop, calls=%fused_computation.25 | loop fusion | flops 982720 | bytes 656640 | tf_op jit(solution)/shard_map/reduce_sum | solution.py:38
  8.1 2.0 %constant_dynamic-update-slice_fusion.4 = bf16[1280,1024]{1,0:T(8,128)(2,1)} fusion(bf16[320,1024]{1,0:T(8,128)(2,1)} %feats.1), kind=kLoop, calls=%fused_computation.43 | loop fusion | bytes 1310720
  10.1 1.5 %fusion.18 = bf16[320,1024]{1,0:T(8,128)(2,1)S(1)} fusion(f32[320]{0:T(512)S(1)} %add_sqrt_fusion.3, bf16[320,1024]{1,0:T(8,128)(2,1)} %param.5), kind=kLoop, calls=%fused_computation.49 | loop fusion | flops 983040 | bytes 1312000 | tf_op jit(solution)/shard_map/convert_element_type | solution.py:96
  11.6 6.3 %collective-permute-done.1.feats = bf16[320,1024]{1,0:T(8,128)(2,1)S(1)} collective-permute-done((bf16[320,1024]{1,0:T(8,128)(2,1)}, bf16[320,1024]{1,0:T(8,128)(2,1)S(1)}, u32[]{:S(2)}, u32[]{:S(2)}) %collective-permute-start.1) | collective-permute-done | bytes 655392 | tf_op jit(solution)/shard_map/ppermute | solution.py:34
  17.9 3.7 %collective-permute-start.6 = (bf16[160,1024]{1,0:T(8,128)(2,1)S(1)}, bf16[160,1024]{1,0:T(8,128)(2,1)S(1)}, u32[]{:S(2)}, u32[]{:S(2)}) collective-permute-start(bf16[160,1024]{1,0:T(8,128)(2,1)S(1)} %slice.35), channel_id=1, source_target_pairs={{0,96},{1,97},{2,98},{3,99},{4,100},{5,101},{6,102},{7,103},{8,104... | collective-permute-start | bytes 983048 | tf_op jit(solution)/shard_map/ppermute | solution.py:34
  21.7 0.2 fusion.12
  21.9 0.5 collective-permute-done.2
  22.4 0.2 fusion.11
  22.6 0.1 collective-permute-start.4
  22.8 0.3 fusion.13
  23.1 0.3 fusion.19
  23.4 1.4 %collective-permute-done.4 = bf16[320,1024]{1,0:T(8,128)(2,1)S(1)} collective-permute-done((bf16[320,1024]{1,0:T(8,128)(2,1)S(1)}, bf16[320,1024]{1,0:T(8,128)(2,1)S(1)}, u32[]{:S(2)}, u32[]{:S(2)}) %collective-permute-start.4) | collective-permute-done | bytes 655392 | tf_op jit(solution)/shard_map/ppermute | solution.py:34
  24.8 0.2 fusion.14
  25.1 0.3 fusion.15
  25.4 0.5 pad_maximum_fusion.1.texts
  25.9 0.6 copy-done
  26.4 0.7 copy-done.1
  27.2 3.3 %shard_map.50 = (bf16[320,1024]{1,0:T(8,128)(2,1)S(1)}, bf16[320,1280]{1,0:T(8,128)(2,1)S(1)}, bf16[320,1024]{1,0:T(8,128)(2,1)S(1)}) custom-call(bf16[320,1024]{1,0:T(8,128)(2,1)S(1)} %copy-done, bf16[1024,1024]{1,0:T(8,128)(2,1)S(1)} %copy-done.1, bf16[1280,1024]{1,0:T(8,128)(2,1)S(1)} %pad_maximum_fusion.1.texts), custom_call_target="tpu_custom_call" | custom-call | flops 2348810240 | bytes 7503872 | tf_op jit(solution)/shard_map/pallas_call | solution.py:67
  30.5 3.3 %shard_map.52 = (bf16[320,1024]{1,0:T(8,128)(2,1)S(1)}, bf16[320,1280]{1,0:T(8,128)(2,1)S(1)}, bf16[320,1024]{1,0:T(8,128)(2,1)S(1)}) custom-call(bf16[320,1024]{1,0:T(8,128)(2,1)S(1)} %collective-permute-done.1.feats, bf16[1024,1024]{1,0:T(8,128)(2,1)S(1)} %copy-done.1, bf16[1280,1024]{1,0:T(8,128)(2,1)S(1)} %pad_maximum_fusion.1.texts), custom_call_target="tpu_custom_call" | custom-call | flops 2348810240 | bytes 7503872 | tf_op jit(solution)/shard_map/pallas_call | solution.py:67
  33.8 3.3 %shard_map.51 = (bf16[320,1024]{1,0:T(8,128)(2,1)S(1)}, bf16[320,1280]{1,0:T(8,128)(2,1)S(1)}, bf16[320,1024]{1,0:T(8,128)(2,1)S(1)}) custom-call(bf16[320,1024]{1,0:T(8,128)(2,1)S(1)} %collective-permute-done.feats, bf16[1024,1024]{1,0:T(8,128)(2,1)S(1)} %copy-done.1, bf16[1280,1024]{1,0:T(8,128)(2,1)S(1)} %pad_maximum_fusion.1.texts), custom_call_target="tpu_custom_call" | custom-call | flops 2348810240 | bytes 7503872 | tf_op jit(solution)/shard_map/pallas_call | solution.py:67
  37.2 3.3 %shard_map.53 = (bf16[320,1024]{1,0:T(8,128)(2,1)S(1)}, bf16[320,1280]{1,0:T(8,128)(2,1)S(1)}, bf16[320,1024]{1,0:T(8,128)(2,1)S(1)}) custom-call(bf16[320,1024]{1,0:T(8,128)(2,1)S(1)} %pad_maximum_fusion.3.feats, bf16[1024,1024]{1,0:T(8,128)(2,1)S(1)} %copy-done.1, bf16[1280,1024]{1,0:T(8,128)(2,1)S(1)} %pad_maximum_fusion.1.texts), custom_call_target="tpu_custom_call" | custom-call | flops 2348810240 | bytes 7503872 | tf_op jit(solution)/shard_map/pallas_call | solution.py:67
  40.5 3.2 %fusion = f32[1024,1024]{1,0:T(8,128)S(1)} fusion(bf16[1280,1024]{1,0:T(8,128)(2,1)S(1)} %constant_dynamic-update-slice_fusion, bf16[320,1024]{1,0:T(8,128)(2,1)S(1)} %get-tuple-element.46, bf16[320,1024]{1,0:T(8,128)(2,1)S(1)} %get-tuple-element.45, bf16[320,1024]{1,0:T(8,128)(2,1)S(1)} %get-tuple-element.44, bf16[320,1024]{1,0:T(8,128)(2,1)S(1)} %get-tuple-element.43), kind=kOutput, calls=%fused_computation.3 | convolution fusion | flops 2694840320 | bytes 9437184 | tf_op jit(solution)/shard_map/dot_general | solution.py:107
  43.7 0.2 fusion.16
  43.9 0.3 pad_maximum_fusion.2
  44.3 0.3 pad_maximum_fusion
  44.6 0.2 collective-permute-start.7
  44.8 3.6 %convolution_multiply_fusion = f32[1280,1024]{1,0:T(8,128)S(1)} fusion(bf16[1280,1280]{1,0:T(8,128)(2,1)S(1)} %pad_maximum_fusion, bf16[1280,1024]{1,0:T(8,128)(2,1)S(1)} %pad_maximum_fusion.2), kind=kOutput, calls=%fused_computation | convolution fusion | flops 3356753920 | bytes 11141120 | tf_op jit(solution)/shard_map/dot_general | solution.py:113
  48.4 0.3 slice.31
  48.8 1.9 %copy-done.3 = f32[1280,1024]{1,0:T(8,128)} copy-done((f32[1280,1024]{1,0:T(8,128)}, f32[1280,1024]{1,0:T(8,128)S(1)}, u32[]{:S(2)}) %copy-start.3) | copy-done | bytes 5242904
  50.7 0.4 collective-permute-start.8
  51.1 1.6 %fusion.9 = bf16[8,64,1024]{2,1,0:T(8,128)(2,1)} fusion(bf16[8,64,1024]{2,1,0:T(8,128)(2,1)S(1)} %collective-permute-done.7, f32[8,2,64,1024]{3,2,1,0:T(8,128)S(1)} %bitcast.25, pred[]{:T(512)S(6)} %eq.4), kind=kLoop, calls=%fused_computation.16 | loop fusion | flops 2097152 | bytes 6291457 | tf_op jit(solution)/shard_map/convert_element_type | solution.py:115
  52.7 7.1 %all-to-all-start = ((bf16[8,64,1024]{2,1,0:T(8,128)(2,1)}), bf16[8,64,1024]{2,1,0:T(8,128)(2,1)}, u32[]{:S(2)}, u32[]{:S(2)}) async-start(bf16[8,64,1024]{2,1,0:T(8,128)(2,1)} %fusion.9), calls=%async_computation | async-start | bytes 2097152 | tf_op jit(solution)/shard_map/all_to_all | solution.py:118
  59.9 3.1 %slice_add_fusion = f32[640,1024]{1,0:T(8,128)S(1)} fusion(f32[640,1024]{1,0:T(8,128)} %collective-permute-done.8, f32[1280,1024]{1,0:T(8,128)} %copy-done.3), kind=kLoop, calls=%fused_computation.12 | loop fusion | flops 655360 | bytes 7864320 | tf_op jit(solution)/shard_map/add | solution.py:119
  63.0 0.5 multiply_reduce_fusion.1
  63.5 1.2 %divide_convert_fusion = bf16[320,1024]{1,0:T(8,128)(2,1)} fusion(f32[640,1024]{1,0:T(8,128)S(1)} %slice_add_fusion, f32[320]{0:T(512)S(1)} %get-tuple-element.63, f32[320]{0:T(512)S(1)} %add_sqrt_fusion.2, bf16[320,1024]{1,0:T(8,128)(2,1)S(1)} %collective-permute-done.2), kind=kLoop, calls=%fused_computation.32 | loop fusion | flops 1966080 | bytes 2624000 | tf_op jit(solution)/shard_map/convert_element_type | solution.py:120
  64.7 3.5 %collective-permute-start.12 = (bf16[320,1024]{1,0:T(8,128)(2,1)}, bf16[320,1024]{1,0:T(8,128)(2,1)S(1)}, u32[]{:S(2)}, u32[]{:S(2)}) collective-permute-start(bf16[320,1024]{1,0:T(8,128)(2,1)} %divide_convert_fusion), channel_id=1, source_target_pairs={{0,16},{1,17},{2,18},{3,19},{4,20},{5,21},{6,22},{7,23},{8,24},{9,... | collective-permute-start | bytes 1966088 | tf_op jit(solution)/shard_map/ppermute | solution.py:34
  68.2 8.2 %all-to-all-done = bf16[8,64,1024]{2,1,0:T(8,128)(2,1)} async-done(((bf16[8,64,1024]{2,1,0:T(8,128)(2,1)}), bf16[8,64,1024]{2,1,0:T(8,128)(2,1)}, u32[]{:S(2)}, u32[]{:S(2)}) %all-to-all-start) | async-done | bytes 1048608 | tf_op jit(solution)/shard_map/all_to_all | solution.py:118
  76.5 1.4 %reduce_sum.71 = bf16[64,1024]{1,0:T(8,128)(2,1)S(1)} reduce(bf16[8,64,1024]{2,1,0:T(8,128)(2,1)} %all-to-all-done, bf16[]{:T(256)} %constant.15.clone.1), dimensions={0}, to_apply=%region_5.6 | reduce | flops 458752 | bytes 1179650 | tf_op jit(solution)/shard_map/reduce_sum | solution.py:122
  77.9 4.1 %collective-permute-start.11 = (bf16[64,1024]{1,0:T(8,128)(2,1)S(1)}, bf16[64,1024]{1,0:T(8,128)(2,1)S(1)}, u32[]{:S(2)}, u32[]{:S(2)}) collective-permute-start(bf16[64,1024]{1,0:T(8,128)(2,1)S(1)} %reduce_sum.71), channel_id=1, source_target_pairs={{0,6},{1,7},{2,0},{3,1},{4,2},{5,3},{6,4},{7,5},{8,14},{9,15},{10,... | collective-permute-start | bytes 393224 | tf_op jit(solution)/shard_map/ppermute | solution.py:34
  82.0 1.9 %collective-permute-start.9 = (bf16[64,1024]{1,0:T(8,128)(2,1)S(1)}, bf16[64,1024]{1,0:T(8,128)(2,1)S(1)}, u32[]{:S(2)}, u32[]{:S(2)}) collective-permute-start(bf16[64,1024]{1,0:T(8,128)(2,1)S(1)} %reduce_sum.71), channel_id=1, source_target_pairs={{0,4},{1,5},{2,6},{3,7},{4,0},{5,1},{6,2},{7,3},{8,12},{9,13},{10,... | collective-permute-start | bytes 393224 | tf_op jit(solution)/shard_map/ppermute | solution.py:34
  83.9 2.0 %collective-permute-done.11 = bf16[64,1024]{1,0:T(8,128)(2,1)S(1)} collective-permute-done((bf16[64,1024]{1,0:T(8,128)(2,1)S(1)}, bf16[64,1024]{1,0:T(8,128)(2,1)S(1)}, u32[]{:S(2)}, u32[]{:S(2)}) %collective-permute-start.11) | collective-permute-done | bytes 131104 | tf_op jit(solution)/shard_map/ppermute | solution.py:34
  85.9 4.3 %collective-permute-done.10 = bf16[64,1024]{1,0:T(8,128)(2,1)S(1)} collective-permute-done((bf16[64,1024]{1,0:T(8,128)(2,1)S(1)}, bf16[64,1024]{1,0:T(8,128)(2,1)S(1)}, u32[]{:S(2)}, u32[]{:S(2)}) %collective-permute-start.10) | collective-permute-done | bytes 131104 | tf_op jit(solution)/shard_map/ppermute | solution.py:34
  90.3 0.8 collective-permute-start.13
  91.1 2.5 %convert_add_fusion = f32[320,1024]{1,0:T(8,128)} fusion(bf16[320,1024]{1,0:T(8,128)(2,1)S(1)} %collective-permute-done.12, f32[640,1024]{1,0:T(8,128)S(1)} %slice_add_fusion, f32[320]{0:T(512)S(1)} %get-tuple-element.62, f32[320]{0:T(512)S(1)} %add_sqrt_fusion.3, bf16[320,1024]{1,0:T(8,128)(2,1)} %param.5), kind=kLoop, calls=%fused_computation.31 | loop fusion | flops 2293760 | bytes 3934720 | tf_op jit(solution)/shard_map/add | solution.py:131
  93.6 1.8 %collective-permute-done.13 = bf16[64,1024]{1,0:T(8,128)(2,1)S(1)} collective-permute-done((bf16[64,1024]{1,0:T(8,128)(2,1)S(1)}, bf16[64,1024]{1,0:T(8,128)(2,1)S(1)}, u32[]{:S(2)}, u32[]{:S(2)}) %collective-permute-start.13) | collective-permute-done | bytes 131104 | tf_op jit(solution)/shard_map/ppermute | solution.py:34
  95.4 0.7 convert_add_fusion.1
  (31 shorter events, 0.5 us)
Async XLA Ops:
  0.6 17.2 %collective-permute-start.1 = (bf16[320,1024]{1,0:T(8,128)(2,1)}, bf16[320,1024]{1,0:T(8,128)(2,1)S(1)}, u32[]{:S(2)}, u32[]{:S(2)}) collective-permute-start(bf16[320,1024]{1,0:T(8,128)(2,1)} %feats.1), channel_id=1, source_target_pairs={{0,96},{1,97},{2,98},{3,99},{4,100},{5,101},{6,102},{7,103},{8,104... | collective-permute-start | bytes 1966088 | tf_op jit(solution)/shard_map/ppermute | solution.py:34
  3.5 18.0 %collective-permute-start = (bf16[320,1024]{1,0:T(8,128)(2,1)}, bf16[320,1024]{1,0:T(8,128)(2,1)S(1)}, u32[]{:S(2)}, u32[]{:S(2)}) collective-permute-start(bf16[320,1024]{1,0:T(8,128)(2,1)} %feats.1), channel_id=1, source_target_pairs={{0,32},{1,33},{2,34},{3,35},{4,36},{5,37},{6,38},{7,39},{8,40},{9,... | collective-permute-start | bytes 1966088 | tf_op jit(solution)/shard_map/ppermute | solution.py:34
  3.5 18.1 %collective-permute-start.3 = (bf16[320,1024]{1,0:T(8,128)(2,1)}, bf16[320,1024]{1,0:T(8,128)(2,1)S(1)}, u32[]{:S(2)}, u32[]{:S(2)}) collective-permute-start(bf16[320,1024]{1,0:T(8,128)(2,1)} %param.5), channel_id=1, source_target_pairs={{0,8},{1,9},{2,10},{3,11},{4,12},{5,13},{6,14},{7,15},{8,0},{9,1},... | collective-permute-start | bytes 1966088 | tf_op jit(solution)/shard_map/ppermute | solution.py:34
  3.5 18.9 %collective-permute-start.2 = (bf16[320,1024]{1,0:T(8,128)(2,1)}, bf16[320,1024]{1,0:T(8,128)(2,1)S(1)}, u32[]{:S(2)}, u32[]{:S(2)}) collective-permute-start(bf16[320,1024]{1,0:T(8,128)(2,1)} %param.5), channel_id=1, source_target_pairs={{0,16},{1,17},{2,18},{3,19},{4,20},{5,21},{6,22},{7,23},{8,24},{9,... | collective-permute-start | bytes 1966088 | tf_op jit(solution)/shard_map/ppermute | solution.py:34
  10.1 12.7 %copy-start.4 = (bf16[1280,1024]{1,0:T(8,128)(2,1)S(1)}, bf16[1280,1024]{1,0:T(8,128)(2,1)}, u32[]{:S(2)}) copy-start(bf16[1280,1024]{1,0:T(8,128)(2,1)} %constant_dynamic-update-slice_fusion.4) | copy-start | bytes 7864324
  17.9 19.2 %collective-permute-start.6 = (bf16[160,1024]{1,0:T(8,128)(2,1)S(1)}, bf16[160,1024]{1,0:T(8,128)(2,1)S(1)}, u32[]{:S(2)}, u32[]{:S(2)}) collective-permute-start(bf16[160,1024]{1,0:T(8,128)(2,1)S(1)} %slice.35), channel_id=1, source_target_pairs={{0,96},{1,97},{2,98},{3,99},{4,100},{5,101},{6,102},{7,103},{8,104... | collective-permute-start | bytes 983048 | tf_op jit(solution)/shard_map/ppermute | solution.py:34
  21.6 15.6 %collective-permute-start.5 = (bf16[160,1024]{1,0:T(8,128)(2,1)S(1)}, bf16[160,1024]{1,0:T(8,128)(2,1)S(1)}, u32[]{:S(2)}, u32[]{:S(2)}) collective-permute-start(bf16[160,1024]{1,0:T(8,128)(2,1)S(1)} %slice.34), channel_id=1, source_target_pairs={{0,32},{1,33},{2,34},{3,35},{4,36},{5,37},{6,38},{7,39},{8,40},{9,... | collective-permute-start | bytes 983048 | tf_op jit(solution)/shard_map/ppermute | solution.py:34
  22.6 2.2 %collective-permute-start.4 = (bf16[320,1024]{1,0:T(8,128)(2,1)S(1)}, bf16[320,1024]{1,0:T(8,128)(2,1)S(1)}, u32[]{:S(2)}, u32[]{:S(2)}) collective-permute-start(bf16[320,1024]{1,0:T(8,128)(2,1)S(1)} %collective-permute-done.2), channel_id=1, source_target_pairs={{0,8},{1,9},{2,10},{3,11},{4,12},{5,13},{6,14},{7,15},{8,0},{9,1},... | collective-permute-start | bytes 1966088 | tf_op jit(solution)/shard_map/ppermute | solution.py:34
  25.3 1.1 %copy-start = (bf16[320,1024]{1,0:T(8,128)(2,1)S(1)}, bf16[320,1024]{1,0:T(8,128)(2,1)}, u32[]{:S(2)}) copy-start(bf16[320,1024]{1,0:T(8,128)(2,1)} %feats.1) | copy-start | bytes 1966084
  25.4 1.8 %copy-start.1 = (bf16[1024,1024]{1,0:T(8,128)(2,1)S(1)}, bf16[1024,1024]{1,0:T(8,128)(2,1)}, u32[]{:S(2)}) copy-start(bf16[1024,1024]{1,0:T(8,128)(2,1)} %proj_weight.7) | copy-start | bytes 6291460
  44.6 3.8 %collective-permute-start.7 = (bf16[8,64,1024]{2,1,0:T(8,128)(2,1)S(1)}, bf16[8,64,1024]{2,1,0:T(8,128)(2,1)S(1)}, u32[]{:S(2)}, u32[]{:S(2)}) collective-permute-start(bf16[8,64,1024]{2,1,0:T(8,128)(2,1)S(1)} %fusion.16), channel_id=1, source_target_pairs={{0,8},{1,9},{2,10},{3,11},{4,12},{5,13},{6,14},{7,15},{8,0},{9,1},... | collective-permute-start | bytes 3145736 | tf_op jit(solution)/shard_map/ppermute | solution.py:34
  48.4 2.3 %copy-start.3 = (f32[1280,1024]{1,0:T(8,128)}, f32[1280,1024]{1,0:T(8,128)S(1)}, u32[]{:S(2)}) copy-start(f32[1280,1024]{1,0:T(8,128)S(1)} %convolution_multiply_fusion) | copy-start | bytes 15728644
  50.7 9.2 %collective-permute-start.8 = (f32[640,1024]{1,0:T(8,128)S(1)}, f32[640,1024]{1,0:T(8,128)}, u32[]{:S(2)}, u32[]{:S(2)}) collective-permute-start(f32[640,1024]{1,0:T(8,128)S(1)} %slice.31), channel_id=1, source_target_pairs={{0,8},{1,9},{2,10},{3,11},{4,12},{5,13},{6,14},{7,15},{8,0},{9,1},... | collective-permute-start | bytes 7864328 | tf_op jit(solution)/shard_map/ppermute | solution.py:34
  52.7 23.7 %all-to-all-start = ((bf16[8,64,1024]{2,1,0:T(8,128)(2,1)}), bf16[8,64,1024]{2,1,0:T(8,128)(2,1)}, u32[]{:S(2)}, u32[]{:S(2)}) async-start(bf16[8,64,1024]{2,1,0:T(8,128)(2,1)} %fusion.9), calls=%async_computation | async-start | bytes 2097152 | tf_op jit(solution)/shard_map/all_to_all | solution.py:118
  59.9 3.1 %copy-start.2 = (bf16[320,1024]{1,0:T(8,128)(2,1)S(1)}, bf16[320,1024]{1,0:T(8,128)(2,1)}, u32[]{:S(2)}) copy-start(bf16[320,1024]{1,0:T(8,128)(2,1)} %param.5) | copy-start | bytes 1966084
  64.7 25.6 %collective-permute-start.12 = (bf16[320,1024]{1,0:T(8,128)(2,1)}, bf16[320,1024]{1,0:T(8,128)(2,1)S(1)}, u32[]{:S(2)}, u32[]{:S(2)}) collective-permute-start(bf16[320,1024]{1,0:T(8,128)(2,1)} %divide_convert_fusion), channel_id=1, source_target_pairs={{0,16},{1,17},{2,18},{3,19},{4,20},{5,21},{6,22},{7,23},{8,24},{9,... | collective-permute-start | bytes 1966088 | tf_op jit(solution)/shard_map/ppermute | solution.py:34
  77.9 8.0 %collective-permute-start.11 = (bf16[64,1024]{1,0:T(8,128)(2,1)S(1)}, bf16[64,1024]{1,0:T(8,128)(2,1)S(1)}, u32[]{:S(2)}, u32[]{:S(2)}) collective-permute-start(bf16[64,1024]{1,0:T(8,128)(2,1)S(1)} %reduce_sum.71), channel_id=1, source_target_pairs={{0,6},{1,7},{2,0},{3,1},{4,2},{5,3},{6,4},{7,5},{8,14},{9,15},{10,... | collective-permute-start | bytes 393224 | tf_op jit(solution)/shard_map/ppermute | solution.py:34
  82.0 8.2 %collective-permute-start.10 = (bf16[64,1024]{1,0:T(8,128)(2,1)S(1)}, bf16[64,1024]{1,0:T(8,128)(2,1)S(1)}, u32[]{:S(2)}, u32[]{:S(2)}) collective-permute-start(bf16[64,1024]{1,0:T(8,128)(2,1)S(1)} %reduce_sum.71), channel_id=1, source_target_pairs={{0,2},{1,3},{2,4},{3,5},{4,6},{5,7},{6,0},{7,1},{8,10},{9,11},{10,... | collective-permute-start | bytes 393224 | tf_op jit(solution)/shard_map/ppermute | solution.py:34
  82.0 8.2 %collective-permute-start.9 = (bf16[64,1024]{1,0:T(8,128)(2,1)S(1)}, bf16[64,1024]{1,0:T(8,128)(2,1)S(1)}, u32[]{:S(2)}, u32[]{:S(2)}) collective-permute-start(bf16[64,1024]{1,0:T(8,128)(2,1)S(1)} %reduce_sum.71), channel_id=1, source_target_pairs={{0,4},{1,5},{2,6},{3,7},{4,0},{5,1},{6,2},{7,3},{8,12},{9,13},{10,... | collective-permute-start | bytes 393224 | tf_op jit(solution)/shard_map/ppermute | solution.py:34
  90.3 5.0 %collective-permute-start.13 = (bf16[64,1024]{1,0:T(8,128)(2,1)S(1)}, bf16[64,1024]{1,0:T(8,128)(2,1)S(1)}, u32[]{:S(2)}, u32[]{:S(2)}) collective-permute-start(bf16[64,1024]{1,0:T(8,128)(2,1)S(1)} %add_convert_fusion), channel_id=1, source_target_pairs={{0,1},{1,0},{2,3},{3,2},{4,5},{5,4},{6,7},{7,6},{8,9},{9,8},{10,11... | collective-permute-start | bytes 393224 | tf_op jit(solution)/shard_map/ppermute | solution.py:34

commit v3 on v1

v3 whole, which is shorter than its diff:
```python
import functools
import itertools

import jax
import jax.numpy as jnp
from jax import lax
from jax.experimental import pallas as pl
from jax.experimental.pallas import tpu as pltpu
from jax.sharding import Mesh, PartitionSpec as P

LOGIT_SCALE = 10.0
LOGIT_BIAS = -2.0
EPSILON = 1e-06

SIZES = (4, 2, 2, 4, 2)
AXES = ("x", "yh", "c", "z", "yl")
F32 = jnp.float32
BF16 = jnp.bfloat16


def position(coords):
    index = 0
    for size, coord in zip(SIZES, coords):
        index = index * size + coord % size
    return index


def send(block, **shift):
    step = [shift.get(name, 0) for name in AXES]
    route = [
        (position(at), position([a + s for a, s in zip(at, step)]))
        for at in itertools.product(*map(range, SIZES))
    ]
    return lax.ppermute(block, AXES, route)


def normalize(values):
    length = jnp.sqrt(jnp.sum(values * values, axis=-1, keepdims=True) + EPSILON)
    return (values / length, length)


def project(grad, norm, length):
    return (grad - norm * jnp.sum(norm * grad, axis=-1, keepdims=True)) / length


def slopes_of(unit, texts, diagonal):
    logits = LOGIT_SCALE * jnp.dot(unit, texts.T, preferred_element_type=F32) + LOGIT_BIAS
    slopes = jax.nn.sigmoid(logits)
    if diagonal:
        rows = lax.broadcasted_iota(jnp.int32, slopes.shape, 0)
        columns = lax.broadcasted_iota(jnp.int32, slopes.shape, 1)
        slopes = slopes - (rows == columns).astype(F32)
    return slopes.astype(BF16)


def unit_kernel(first, second, out):
    rows = first.shape[0]
    out[:rows] = normalize(first[...].astype(F32))[0].astype(BF16)
    out[rows:] = normalize(second[...].astype(F32))[0].astype(BF16)


def stacked(refs):
    blocks = [ref[...] for ref in refs]
    return blocks[0] if len(blocks) == 1 else jnp.concatenate(blocks)


def early_kernel(count, diagonal, *refs):
    feats, (proj_weight, texts) = refs[:count], refs[count : count + 2]
    unit_out, norm_out, length_out, slopes_out, grad_out = refs[count + 2 :]
    raw = jnp.dot(stacked(feats), proj_weight[...], preferred_element_type=F32)
    norm, length = normalize(raw)
    unit = norm.astype(BF16)
    unit_out[...], norm_out[...], length_out[...] = unit, norm, length
    slopes = slopes_of(unit, texts[...], diagonal)
    slopes_out[...] = slopes
    grad_out[...] = jnp.dot(slopes, texts[...], preferred_element_type=F32)


def whole_block(feats, proj_weight, texts_a, texts_b):
    raw = jnp.dot(feats, proj_weight[...], preferred_element_type=F32)
    norm, length = normalize(raw)
    unit = norm.astype(BF16)
    slopes_a = slopes_of(unit, texts_a[...], False)
    slopes_b = slopes_of(unit, texts_b[...], False)
    grad = jnp.dot(slopes_a, texts_a[...], preferred_element_type=F32)
    grad = grad + jnp.dot(slopes_b, texts_b[...], preferred_element_type=F32)
    return unit, slopes_a, slopes_b, project(LOGIT_SCALE * grad, norm, length).astype(BF16)


def middle_kernel(*refs):
    own, near, (high, low, proj_weight, texts_a, texts_b) = refs[:4], refs[4:8], refs[8:13]
    outs = refs[13:]
    for k, (unit, norm, length, grad) in enumerate((own, near)):
        slopes = slopes_of(unit[...], texts_b[...], False)
        outs[2 * k][...] = slopes
        total = grad[...] + jnp.dot(slopes, texts_b[...], preferred_element_type=F32)
        total = project(LOGIT_SCALE * total, norm[...], length[...])
        outs[2 * k + 1][...] = total.astype(BF16)
    block = whole_block(stacked((high, low)), proj_weight, texts_a, texts_b)
    for out, value in zip(outs[4:], block):
        out[...] = value


def late_kernel(*refs):
    core = lax.axis_index("c")
    feats, grads, (proj_weight, texts_a, texts_b) = refs[:7], refs[7:10], refs[10:13]
    unit_out, slopes_a, slopes_b, mine_out, other_out, weight = refs[13:]
    unit_out[...], slopes_a[...], slopes_b[...], far_grad = whole_block(
        stacked(feats[5:]), proj_weight, texts_a, texts_b
    )
    grads = jnp.concatenate([stacked(grads), far_grad])
    weight[...] = jnp.dot(stacked(feats).T, grads, preferred_element_type=F32)
    slices, rows = mine_out.shape[0], mine_out.shape[1]
    for k in range(slices):
        start = 2 * k * rows
        mine = pl.ds(pl.multiple_of(start + core * rows, rows), rows)
        other = pl.ds(pl.multiple_of(start + (1 - core) * rows, rows), rows)
        mine_out[k] = weight[mine]
        other_out[k] = weight[other].astype(BF16)


def add_kernel(mine, received, out):
    out[...] = (mine[...] + received[...].astype(F32)).astype(BF16)


def text_rows(units, slopes, start, stop):
    return LOGIT_SCALE * sum(
        jnp.dot(s[...].T[start:stop], u[...], preferred_element_type=F32)
        for s, u in zip(slopes, units)
    )


def text_kernel(count, *refs):
    units, slopes, (home, away) = refs[:count], refs[count : 2 * count], refs[2 * count :]
    rows = home.shape[0]
    total = text_rows(units, slopes, 0, 2 * rows)
    home[...], away[...] = total[:rows], total[rows:]


def away_kernel(count, *refs):
    units, slopes, away = refs[:count], refs[count : 2 * count], refs[2 * count]
    rows = away.shape[0]
    away[...] = text_rows(units, slopes, rows, 2 * rows)


def home_kernel(count, *refs):
    units, slopes, (received, feats, out) = refs[:count], refs[count : 2 * count], refs[2 * count :]
    total = received[...] + text_rows(units, slopes, 0, out.shape[0])
    out[...] = project(total, *normalize(feats[...].astype(F32))).astype(out.dtype)


def final_kernel(home, received, rest, feats, out):
    norm, length = normalize(feats[...].astype(F32))
    out[...] = project(home[...] + received[...], norm, length) + rest[...].astype(F32)


def call(kernel, outs, operands, mib, scratch=()):
    vmem = pl.BlockSpec(memory_space=pltpu.VMEM)
    shapes = tuple(jax.ShapeDtypeStruct(*out) for out in outs)
    return pl.pallas_call(
        kernel,
        out_shape=shapes,
        in_specs=[vmem] * len(operands),
        out_specs=(vmem,) * len(shapes),
        scratch_shapes=scratch,
        compiler_params=pltpu.CompilerParams(vmem_limit_bytes=mib * 1024 * 1024),
        cost_estimate=pl.CostEstimate(flops=1, bytes_accessed=1, transcendentals=0),
    )(*operands)


def local(sensor_feats, proj_weight, text_feats):
    rows, depth = sensor_feats.shape
    width = proj_weight.shape[1]
    half, texts = rows // 2, 2 * rows
    unit_like, grad_like = ((rows, width), BF16), ((rows, width), F32)
    slopes_like = ((rows, texts), BF16)

    text_c, text_y = send(text_feats, c=1), send(text_feats, yh=1)
    low, high = sensor_feats[:half], sensor_feats[half:]
    right_low, left_high = send(low, x=1), send(high, x=-1)
    right_high, left_low = send(high, x=1), send(low, x=-1)

    def units(first, second):
        return call(unit_kernel, [((texts, width), BF16)], [first, second], 12)[0]

    def early(feats, diagonal):
        return call(
            functools.partial(early_kernel, len(feats), diagonal),
            [unit_like, grad_like, ((rows, 1), F32), slopes_like, grad_like],
            [*feats, proj_weight, texts_a],
            16,
        )

    texts_a = units(text_feats, text_c)
    unit, norm, length, slopes_a, grad = early([sensor_feats], True)
    right_low, left_high, grad = lax.optimization_barrier((right_low, left_high, grad))
    far_low, far_high = send(right_low, x=1), send(left_high, x=-1)
    near_unit, near_norm, near_length, near_a, near = early([right_low, left_high], False)
    text_y, right_high, left_low, near = lax.optimization_barrier(
        (text_y, right_high, left_low, near)
    )
    texts_b = units(text_y, send(text_y, c=1))
    slopes_b, raw_grad, near_b, near_grad, next_unit, next_a, next_b, next_grad = call(
        middle_kernel,
        [
            slopes_like, unit_like, slopes_like, unit_like,
            unit_like, slopes_like, slopes_like, unit_like,
        ],
        [
            unit, norm, length, grad, near_unit, near_norm, near_length, near,
            right_high, left_low, proj_weight, texts_a, texts_b,
        ],
        30,
    )
    next_grad, far_low, far_high = lax.optimization_barrier((next_grad, far_low, far_high))
    share = (8, depth // 16, width)
    far_unit, far_a, far_b, mine, other = call(
        late_kernel,
        [unit_like, slopes_like, slopes_like, (share, F32), (share, BF16)],
        [
            sensor_feats, right_low, left_high, right_high, left_low,
            far_low, far_high, raw_grad, near_grad, next_grad, proj_weight, texts_a, texts_b,
        ],
        30,
        scratch=[pltpu.VMEM((depth, width), F32)],
    )

    def text_sums(kernel, outs, mib, slopes, *others):
        operands = [unit, near_unit, next_unit, far_unit, *slopes, *others]
        return call(functools.partial(kernel, 4), outs, operands, mib)

    weight_recv = send(other, c=1)
    half_b = [slopes_b, near_b, next_b, far_b]
    away_b = text_sums(away_kernel, [grad_like], 20, half_b)[0]
    weight_recv, away_b = lax.optimization_barrier((weight_recv, away_b))
    weight_sum = call(add_kernel, [(share, BF16)], [mine, weight_recv], 12)[0]
    weight_all = lax.all_to_all(weight_sum, ("x", "yh"), split_axis=0, concat_axis=0, tiled=True)
    text_send = text_sums(home_kernel, [unit_like], 58, half_b, send(away_b, c=1), text_y)[0]
    text_out = send(text_send, yh=1)
    slopes_a, text_send = lax.optimization_barrier((slopes_a, text_send))
    home_a, away_a = text_sums(text_kernel, [grad_like] * 2, 58, [slopes_a, near_a, next_a, far_a])
    away_a = send(away_a, c=1)

    weight_sum = jnp.sum(weight_all.astype(F32), axis=0).astype(BF16)
    across = send(weight_sum, z=2)
    ahead, behind = send(weight_sum, z=1), send(weight_sum, z=-1)
    weight_sum = (
        (weight_sum.astype(F32) + across.astype(F32)) + (ahead.astype(F32) + behind.astype(F32))
    ).astype(BF16)
    weight_sum, text_out = lax.optimization_barrier((weight_sum, text_out))
    across = send(weight_sum, yl=1)
    text_grad = call(final_kernel, [grad_like], [home_a, away_a, text_out, text_feats], 16)[0]
    across, text_grad = lax.optimization_barrier((across, text_grad))
    return (text_grad, weight_sum.astype(F32) + across.astype(F32))


def solution(mesh):
    fine = Mesh(mesh.devices.reshape(SIZES), AXES)
    return jax.shard_map(
        local,
        mesh=fine,
        in_specs=(P(AXES, None), P(), P(AXES, None)),
        out_specs=(P(AXES, None), P(("x", "yh", "c"), None)),
        check_vma=False,
    )
```

time: 140 us -> 89.2 us (0.64)
  Pallas kernels: 0 us -> 37 us
  matrix products: 34 us -> 0 us
  blocking collectives: 21.3 us -> 0 us
  waiting for transfers between devices: 35.1 us -> 15.4 us
  other arithmetic: 16.8 us -> 2.21 us
  starting transfers between devices: 22.5 us -> 30.6 us
  local copies, waits for them, and re-layouts: 9.16 us -> 2.3 us
    pallas_call x0 -> x11, Pallas kernels: none -> 37 us  [call(): pl.pallas_call(kernel, out_shape=shapes, in_specs=[vmem] * len(operands),...]
    dot_general x14 -> x0, matrix products: 34 us -> none  [the longest x4 15.8 us: sensor_part(): jnp.dot(unit, texts.T, preferred_element_type=F32)]
    all_to_all x1 -> x0, blocking collectives: 21.3 us -> none  [local(): lax.all_to_all(weight_sum, ('x', 'yh'), split_axis=0, concat_axis=0, tile...]
    ppermute x16 -> x17, waiting for transfers between devices: 35.1 us -> 15.2 us  [send(): return lax.ppermute(block, AXES, route)]
    convert_element_type x14 -> x0, other arithmetic: 6.37 us -> none  [the longest x1 1.67 us: local(): text_norm.astype(BF16)]
    add x3 -> x1, other arithmetic: 5.29 us -> 0.73 us  [local(): return (text_grad, weight_sum.astype(F32) + across.astype(F32))]
    all_to_all x0 -> x1, starting transfers between devices: none -> 4.24 us  [local(): lax.all_to_all(weight_sum, ('x', 'yh'), split_axis=0, concat_axis=0, tile...]
    unnamed x18 -> x36, local copies, waits for them, and re-layouts: 5.13 us -> 1.12 us
  transfers between devices with their start and end apart: 16 -> 18, of which waited for: 6 -> 10; matrix products, arithmetic and copies ran while one was open for 21% -> 3% of each run, Pallas kernels for 0% -> 35%
where the time goes in v3:
time: 89.2 us; the launch traced here: 88.4 us
  Pallas kernels  37 us (41%)
  starting transfers between devices  30.6 us (34%)
  waiting for transfers between devices  15.4 us (17%)
  local copies, waits for them, and re-layouts  2.3 us (3%)
  other arithmetic  2.21 us (2%)
  between operations  0.95 us (1%)
    pallas_call x11, Pallas kernels, call(): pl.pallas_call(kernel, out_shape=shapes, in_specs=[vmem] * len(operands),...  37 us
    ppermute x17, starting transfers between devices, send(): return lax.ppermute(block, AXES, route)  26.4 us
    ppermute x17, waiting for transfers between devices, send(): return lax.ppermute(block, AXES, route)  15.2 us
    all_to_all x1, starting transfers between devices, local(): lax.all_to_all(weight_sum, ('x', 'yh'), split_axis=0, concat_axis=0, tile...  4.24 us
  transfers between devices with their start and end apart: 18, of which 10 were waited for; matrix products, arithmetic and copies ran while one was open for 3% of the time, Pallas kernels for 35%

profile of v3, /device:TPU:0, one launch (start us, length us, event | category | flops | bytes accessed | tf_op | source)
XLA Modules:
  0.0 88.4 jit_solution(1147795269079254709)
XLA Ops:
  0.6 0.1 collective-permute-start.2
  0.7 3.4 %collective-permute-start.3 = (bf16[320,1024]{1,0:T(8,128)(2,1)}, bf16[320,1024]{1,0:T(8,128)(2,1)S(1)}, u32[]{:S(2)}, u32[]{:S(2)}) collective-permute-start(bf16[320,1024]{1,0:T(8,128)(2,1)} %feats.1), channel_id=1, source_target_pairs={{0,16},{1,17},{2,18},{3,19},{4,20},{5,21},{6,22},{7,23},{8,24},{9,... | collective-permute-start | bytes 1966088 | tf_op jit(solution)/shard_map/ppermute | solution.py:34
  4.1 1.2 %fusion = (bf16[160,1024]{1,0:T(8,128)(2,1)S(1)}, bf16[160,1024]{1,0:T(8,128)(2,1)S(1)}) fusion(bf16[320,1024]{1,0:T(8,128)(2,1)} %refs_0_.3), kind=kLoop, calls=%fused_computation.2 | loop fusion | bytes 1310720 | tf_op jit(solution)/shard_map/slice | solution.py:179
  5.3 1.6 %collective-permute-start = (bf16[160,1024]{1,0:T(8,128)(2,1)S(1)}, bf16[160,1024]{1,0:T(8,128)(2,1)S(1)}, u32[]{:S(2)}, u32[]{:S(2)}) collective-permute-start(bf16[160,1024]{1,0:T(8,128)(2,1)S(1)} %get-tuple-element.87), channel_id=1, source_target_pairs={{0,32},{1,33},{2,34},{3,35},{4,36},{5,37},{6,38},{7,39},{8,40},{9,... | collective-permute-start | bytes 983048 | tf_op jit(solution)/shard_map/ppermute | solution.py:34
  6.8 1.7 %collective-permute-start.1 = (bf16[160,1024]{1,0:T(8,128)(2,1)S(1)}, bf16[160,1024]{1,0:T(8,128)(2,1)S(1)}, u32[]{:S(2)}, u32[]{:S(2)}) collective-permute-start(bf16[160,1024]{1,0:T(8,128)(2,1)S(1)} %get-tuple-element.86), channel_id=1, source_target_pairs={{0,96},{1,97},{2,98},{3,99},{4,100},{5,101},{6,102},{7,103},{8,104... | collective-permute-start | bytes 983048 | tf_op jit(solution)/shard_map/ppermute | solution.py:34
  8.6 0.3 collective-permute-start.4
  8.9 0.0 collective-permute-done.2.second
  8.9 3.0 %collective-permute-start.5 = (bf16[160,1024]{1,0:T(8,128)(2,1)S(1)}, bf16[160,1024]{1,0:T(8,128)(2,1)S(1)}, u32[]{:S(2)}, u32[]{:S(2)}) collective-permute-start(bf16[160,1024]{1,0:T(8,128)(2,1)S(1)} %get-tuple-element.87), channel_id=1, source_target_pairs={{0,96},{1,97},{2,98},{3,99},{4,100},{5,101},{6,102},{7,103},{8,104... | collective-permute-start | bytes 983048 | tf_op jit(solution)/shard_map/ppermute | solution.py:34
  11.8 0.5 shard_map.50.refs_2_.refs_3_.refs_11_
  12.3 2.5 %shard_map.51 = (bf16[320,1024]{1,0:T(8,128)(2,1)S(1)}, f32[320,1024]{1,0:T(8,128)S(1)}, f32[320,1]{1,0:T(8,128)S(1)}, bf16[320,640]{1,0:T(8,128)(2,1)S(1)}, f32[320,1024]{1,0:T(8,128)S(1)}) custom-call(bf16[320,1024]{1,0:T(8,128)(2,1)S(1)} %copy-done.3, bf16[1024,1024]{1,0:T(8,128)(2,1)S(1)} %copy-done, bf16[640,1024]{1,0:T(8,128)(2,1)S(1)} %shard_map.50.refs_2_.refs_3_.refs_11_), custom_call_target="tpu_custom_call" | custom-call | flops 1 | bytes 1 | tf_op jit(solution)/shard_map/pallas_call | solution.py:160
  14.9 2.2 %collective-permute-done.refs_0_.refs_1_ = bf16[160,1024]{1,0:T(8,128)(2,1)S(1)} collective-permute-done((bf16[160,1024]{1,0:T(8,128)(2,1)S(1)}, bf16[160,1024]{1,0:T(8,128)(2,1)S(1)}, u32[]{:S(2)}, u32[]{:S(2)}) %collective-permute-start) | collective-permute-done | bytes 327712 | tf_op jit(solution)/shard_map/ppermute | solution.py:34
  17.1 0.3 collective-permute-done.1.refs_1_.refs_2_
  17.4 2.5 %shard_map.52 = (bf16[320,1024]{1,0:T(8,128)(2,1)S(1)}, f32[320,1024]{1,0:T(8,128)S(1)}, f32[320,1]{1,0:T(8,128)S(1)}, bf16[320,640]{1,0:T(8,128)(2,1)S(1)}, f32[320,1024]{1,0:T(8,128)S(1)}) custom-call(bf16[160,1024]{1,0:T(8,128)(2,1)S(1)} %collective-permute-done.refs_0_.refs_1_, bf16[160,1024]{1,0:T(8,128)(2,1)S(1)} %collective-permute-done.1.refs_1_.refs_2_, ...), custom_call_target="tpu_custom_call" | custom-call | flops 1 | bytes 1 | tf_op jit(solution)/shard_map/pallas_call | solution.py:160
  20.0 3.4 %collective-permute-done.4.refs_8_.refs_3_ = bf16[160,1024]{1,0:T(8,128)(2,1)S(1)} collective-permute-done((bf16[160,1024]{1,0:T(8,128)(2,1)S(1)}, bf16[160,1024]{1,0:T(8,128)(2,1)S(1)}, u32[]{:S(2)}, u32[]{:S(2)}) %collective-permute-start.4) | collective-permute-done | bytes 327712 | tf_op jit(solution)/shard_map/ppermute | solution.py:34
  23.3 0.0 collective-permute-done.5.refs_9_.refs_4_
  23.3 0.0 collective-permute-done.3.first.refs_9_
  23.4 0.1 collective-permute-start.6
  23.4 1.5 %collective-permute-start.7 = (bf16[160,1024]{1,0:T(8,128)(2,1)S(1)}, bf16[160,1024]{1,0:T(8,128)(2,1)S(1)}, u32[]{:S(2)}, u32[]{:S(2)}) collective-permute-start(bf16[160,1024]{1,0:T(8,128)(2,1)S(1)} %collective-permute-done.refs_0_.refs_1_), channel_id=1, source_target_pairs={{0,32},{1,33},{2,34},{3,35},{4,36},{5,37},{6,38},{7,39},{8,40},{9,... | collective-permute-start | bytes 983048 | tf_op jit(solution)/shard_map/ppermute | solution.py:34
  24.9 1.8 %collective-permute-start.8 = (bf16[160,1024]{1,0:T(8,128)(2,1)S(1)}, bf16[160,1024]{1,0:T(8,128)(2,1)S(1)}, u32[]{:S(2)}, u32[]{:S(2)}) collective-permute-start(bf16[160,1024]{1,0:T(8,128)(2,1)S(1)} %collective-permute-done.1.refs_1_.refs_2_), channel_id=1, source_target_pairs={{0,96},{1,97},{2,98},{3,99},{4,100},{5,101},{6,102},{7,103},{8,104... | collective-permute-start | bytes 983048 | tf_op jit(solution)/shard_map/ppermute | solution.py:34
  26.8 0.5 shard_map.53.refs_12_
  27.3 6.0 %shard_map.54 = (bf16[320,640]{1,0:T(8,128)(2,1)S(1)}, bf16[320,1024]{1,0:T(8,128)(2,1)S(1)}, bf16[320,640]{1,0:T(8,128)(2,1)S(1)}, bf16[320,1024]{1,0:T(8,128)(...) custom-call(bf16[320,1024]{1,0:T(8,128)(2,1)S(1)} %get-tuple-element, ...), custom_call_target="tpu_custom_call" | custom-call | flops 1 | bytes 1 | tf_op jit(solution)/shard_map/pallas_call | solution.py:160
  33.4 1.4 %collective-permute-done.7.refs_5_ = bf16[160,1024]{1,0:T(8,128)(2,1)S(1)} collective-permute-done((bf16[160,1024]{1,0:T(8,128)(2,1)S(1)}, bf16[160,1024]{1,0:T(8,128)(2,1)S(1)}, u32[]{:S(2)}, u32[]{:S(2)}) %collective-permute-start.7) | collective-permute-done | bytes 327712 | tf_op jit(solution)/shard_map/ppermute | solution.py:34
  34.8 6.4 %shard_map.55 = (bf16[320,1024]{1,0:T(8,128)(2,1)S(1)}, bf16[320,640]{1,0:T(8,128)(2,1)S(1)}, bf16[320,640]{1,0:T(8,128)(2,1)S(1)}, f32[8,64,1024]{2,1,0:T(8,128)S(1)}, bf16[8,64,1024]{2,1,0:T(8,128)(2,1)S(1)}) custom-call(bf16[320,1024]{1,0:T(8,128)(2,1)S(1)} %copy-done.3, bf16[160,1024]{1,0:T(8,128)(2,1)S(1)} %collective-permute-done.refs_0_.refs_1_, ...), custom_call_target="tpu_custom_call" | custom-call | flops 1 | bytes 1 | tf_op jit(solution)/shard_map/pallas_call | solution.py:160
  41.3 0.1 collective-permute-start.9
  41.4 2.6 %shard_map.56 = f32[320,1024]{1,0:T(8,128)} custom-call(bf16[320,1024]{1,0:T(8,128)(2,1)S(1)} %get-tuple-element.50.refs_0_, bf16[320,1024]{1,0:T(8,128)(2,1)S(1)} %get-tuple-element.54.refs_4_.refs_1_, bf16[320,1024]{1,0:T(8,128)(2,1)S(1)} %get-tuple-element.67.refs_2_, bf16[320,1024]{1,0:T(8,128)(2,1)S(1)} %get-tuple-element.68.refs_3_, ...), custom_call_target="tpu_custom_call" | custom-call | flops 1 | bytes 1 | tf_op jit(solution)/shard_map/pallas_call | solution.py:160
  44.0 0.8 collective-permute-start.13
  44.8 1.2 %shard_map.57 = bf16[8,64,1024]{2,1,0:T(8,128)(2,1)} custom-call(f32[8,64,1024]{2,1,0:T(8,128)S(1)} %get-tuple-element.65.mine, bf16[8,64,1024]{2,1,0:T(8,128)(2,1)S(1)} %collective-permute-done.9.received), custom_call_target="tpu_custom_call" | custom-call | flops 1 | bytes 1 | tf_op jit(solution)/shard_map/pallas_call | solution.py:160
  46.0 4.2 %all-to-all-start = ((bf16[8,64,1024]{2,1,0:T(8,128)(2,1)}), bf16[8,64,1024]{2,1,0:T(8,128)(2,1)}, u32[]{:S(2)}, u32[]{:S(2)}) async-start(bf16[8,64,1024]{2,1,0:T(8,128)(2,1)} %shard_map.57), calls=%async_computation | async-start | bytes 2097152 | tf_op jit(solution)/shard_map/all_to_all | solution.py:237
  50.2 0.0 copy-start.17
  50.2 1.0 %copy-done.17 = f32[320,1024]{1,0:T(8,128)} copy-done((f32[320,1024]{1,0:T(8,128)}, f32[320,1024]{1,0:T(8,128)S(1)}, u32[]{:S(2)}) %copy-start.17) | copy-done | bytes 1310744
  51.3 5.4 %shard_map.58 = bf16[320,1024]{1,0:T(8,128)(2,1)} custom-call(bf16[320,1024]{1,0:T(8,128)(2,1)} %copy-done.1, bf16[320,1024]{1,0:T(8,128)(2,1)} %copy-done.2, bf16[320,1024]{1,0:T(8,128)(2,1)} %copy-done.4, bf16[320,1024]{1,0:T(8,128)(2,1)} %copy-done.5, bf16[320,640]{1,0:T(8,128)(2,1)} %copy-done.8, bf16[320,640]{1,0:T(8,128)(2,1)} %copy-done.9, ...), custom_call_target="tpu_custom_call" | custom-call | flops 1 | bytes 1 | tf_op jit(solution)/shard_map/pallas_call | solution.py:160
  56.7 6.6 %shard_map.59 = (f32[320,1024]{1,0:T(8,128)}, f32[320,1024]{1,0:T(8,128)}) custom-call(bf16[320,1024]{1,0:T(8,128)(2,1)} %copy-done.1, bf16[320,1024]{1,0:T(8,128)(2,1)} %copy-done.2, bf16[320,1024]{1,0:T(8,128)(2,1)} %copy-done.4, bf16[320,1024]{1,0:T(8,128)(2,1)} %copy-done.5, bf16[320,640]{1,0:T(8,128)(2,1)} %copy-done.13, bf16[320,640]{1,0:T(8,128)(2,1)} %copy-done.14, ...), custom_call_target="tpu_custom_call" | custom-call | flops 1 | bytes 1 | tf_op jit(solution)/shard_map/pallas_call | solution.py:160
  63.3 0.0 collective-permute-start.16
  63.3 3.5 %collective-permute-start.14 = (bf16[320,1024]{1,0:T(8,128)(2,1)}, bf16[320,1024]{1,0:T(8,128)(2,1)}, u32[]{:S(2)}, u32[]{:S(2)}) collective-permute-start(bf16[320,1024]{1,0:T(8,128)(2,1)} %shard_map.58), channel_id=1, source_target_pairs={{0,16},{1,17},{2,18},{3,19},{4,20},{5,21},{6,22},{7,23},{8,24},{9,... | collective-permute-start | bytes 1966088 | tf_op jit(solution)/shard_map/ppermute | solution.py:34
  66.9 0.2 all-to-all-done
  67.0 1.4 %reduce_sum.12 = bf16[64,1024]{1,0:T(8,128)(2,1)S(1)} reduce(bf16[8,64,1024]{2,1,0:T(8,128)(2,1)} %all-to-all-done, bf16[]{:T(256)} %constant.2.clone.1), dimensions={0}, to_apply=%region_0.0 | reduce | flops 458752 | bytes 1179650 | tf_op jit(solution)/shard_map/reduce_sum | solution.py:244
  68.5 4.0 %collective-permute-start.10 = (bf16[64,1024]{1,0:T(8,128)(2,1)S(1)}, bf16[64,1024]{1,0:T(8,128)(2,1)S(1)}, u32[]{:S(2)}, u32[]{:S(2)}) collective-permute-start(bf16[64,1024]{1,0:T(8,128)(2,1)S(1)} %reduce_sum.12), channel_id=1, source_target_pairs={{0,4},{1,5},{2,6},{3,7},{4,0},{5,1},{6,2},{7,3},{8,12},{9,13},{10,... | collective-permute-start | bytes 393224 | tf_op jit(solution)/shard_map/ppermute | solution.py:34
  72.4 1.0 %collective-permute-start.11 = (bf16[64,1024]{1,0:T(8,128)(2,1)S(1)}, bf16[64,1024]{1,0:T(8,128)(2,1)S(1)}, u32[]{:S(2)}, u32[]{:S(2)}) collective-permute-start(bf16[64,1024]{1,0:T(8,128)(2,1)S(1)} %reduce_sum.12), channel_id=1, source_target_pairs={{0,2},{1,3},{2,4},{3,5},{4,6},{5,7},{6,0},{7,1},{8,10},{9,11},{10,... | collective-permute-start | bytes 393224 | tf_op jit(solution)/shard_map/ppermute | solution.py:34
  73.4 2.2 %collective-permute-start.12 = (bf16[64,1024]{1,0:T(8,128)(2,1)S(1)}, bf16[64,1024]{1,0:T(8,128)(2,1)S(1)}, u32[]{:S(2)}, u32[]{:S(2)}) collective-permute-start(bf16[64,1024]{1,0:T(8,128)(2,1)S(1)} %reduce_sum.12), channel_id=1, source_target_pairs={{0,6},{1,7},{2,0},{3,1},{4,2},{5,3},{6,4},{7,5},{8,14},{9,15},{10,... | collective-permute-start | bytes 393224 | tf_op jit(solution)/shard_map/ppermute | solution.py:34
  75.6 1.1 %collective-permute-done.10 = bf16[64,1024]{1,0:T(8,128)(2,1)S(1)} collective-permute-done((bf16[64,1024]{1,0:T(8,128)(2,1)S(1)}, bf16[64,1024]{1,0:T(8,128)(2,1)S(1)}, u32[]{:S(2)}, u32[]{:S(2)}) %collective-permute-start.10) | collective-permute-done | bytes 131104 | tf_op jit(solution)/shard_map/ppermute | solution.py:34
  76.7 2.4 %collective-permute-done.11 = bf16[64,1024]{1,0:T(8,128)(2,1)S(1)} collective-permute-done((bf16[64,1024]{1,0:T(8,128)(2,1)S(1)}, bf16[64,1024]{1,0:T(8,128)(2,1)S(1)}, u32[]{:S(2)}, u32[]{:S(2)}) %collective-permute-start.11) | collective-permute-done | bytes 131104 | tf_op jit(solution)/shard_map/ppermute | solution.py:34
  79.1 0.5 collective-permute-done.12
  79.6 0.1 add_convert_fusion
  79.7 2.8 %collective-permute-done.14.rest = bf16[320,1024]{1,0:T(8,128)(2,1)} collective-permute-done((bf16[320,1024]{1,0:T(8,128)(2,1)}, bf16[320,1024]{1,0:T(8,128)(2,1)}, u32[]{:S(2)}, u32[]{:S(2)}) %collective-permute-start.14) | collective-permute-done | bytes 655392 | tf_op jit(solution)/shard_map/ppermute | solution.py:34
  82.5 1.3 %collective-permute-start.15 = (bf16[64,1024]{1,0:T(8,128)(2,1)S(1)}, bf16[64,1024]{1,0:T(8,128)(2,1)S(1)}, u32[]{:S(2)}, u32[]{:S(2)}) collective-permute-start(bf16[64,1024]{1,0:T(8,128)(2,1)S(1)} %add_convert_fusion), channel_id=1, source_target_pairs={{0,1},{1,0},{2,3},{3,2},{4,5},{5,4},{6,7},{7,6},{8,9},{9,8},{10,11... | collective-permute-start | bytes 393224 | tf_op jit(solution)/shard_map/ppermute | solution.py:34
  83.8 2.7 %shard_map.60 = f32[320,1024]{1,0:T(8,128)} custom-call(f32[320,1024]{1,0:T(8,128)S(1)} %copy-done.12, f32[320,1024]{1,0:T(8,128)S(1)} %collective-permute-done.16.received, bf16[320,1024]{1,0:T(8,128)(2,1)} %collective-permute-done.14.rest, bf16[320,1024]{1,0:T(8,128)(2,1)S(1)} %copy-done.6), custom_call_target="tpu_custom_call" | custom-call | flops 1 | bytes 1 | tf_op jit(solution)/shard_map/pallas_call | solution.py:160
  86.6 1.1 %collective-permute-done.15 = bf16[64,1024]{1,0:T(8,128)(2,1)S(1)} collective-permute-done((bf16[64,1024]{1,0:T(8,128)(2,1)S(1)}, bf16[64,1024]{1,0:T(8,128)(2,1)S(1)}, u32[]{:S(2)}, u32[]{:S(2)}) %collective-permute-start.15) | collective-permute-done | bytes 131104 | tf_op jit(solution)/shard_map/ppermute | solution.py:34
  87.7 0.7 convert_add_fusion
  (39 shorter events, 0.1 us)
Async XLA Ops:
  0.6 11.2 %copy-start.6 = (bf16[320,1024]{1,0:T(8,128)(2,1)S(1)}, bf16[320,1024]{1,0:T(8,128)(2,1)}, u32[]{:S(2)}) copy-start(bf16[320,1024]{1,0:T(8,128)(2,1)} %feats.1) | copy-start | bytes 1966084
  0.6 8.2 %collective-permute-start.2 = (bf16[320,1024]{1,0:T(8,128)(2,1)}, bf16[320,1024]{1,0:T(8,128)(2,1)S(1)}, u32[]{:S(2)}, u32[]{:S(2)}) collective-permute-start(bf16[320,1024]{1,0:T(8,128)(2,1)} %feats.1), channel_id=1, source_target_pairs={{0,8},{1,9},{2,10},{3,11},{4,12},{5,13},{6,14},{7,15},{8,0},{9,1},... | collective-permute-start | bytes 1966088 | tf_op jit(solution)/shard_map/ppermute | solution.py:34
  0.7 22.6 %collective-permute-start.3 = (bf16[320,1024]{1,0:T(8,128)(2,1)}, bf16[320,1024]{1,0:T(8,128)(2,1)S(1)}, u32[]{:S(2)}, u32[]{:S(2)}) collective-permute-start(bf16[320,1024]{1,0:T(8,128)(2,1)} %feats.1), channel_id=1, source_target_pairs={{0,16},{1,17},{2,18},{3,19},{4,20},{5,21},{6,22},{7,23},{8,24},{9,... | collective-permute-start | bytes 1966088 | tf_op jit(solution)/shard_map/ppermute | solution.py:34
  4.1 8.2 %copy-start.3 = (bf16[320,1024]{1,0:T(8,128)(2,1)S(1)}, bf16[320,1024]{1,0:T(8,128)(2,1)}, u32[]{:S(2)}) copy-start(bf16[320,1024]{1,0:T(8,128)(2,1)} %refs_0_.3) | copy-start | bytes 1966084
  5.3 11.8 %collective-permute-start = (bf16[160,1024]{1,0:T(8,128)(2,1)S(1)}, bf16[160,1024]{1,0:T(8,128)(2,1)S(1)}, u32[]{:S(2)}, u32[]{:S(2)}) collective-permute-start(bf16[160,1024]{1,0:T(8,128)(2,1)S(1)} %get-tuple-element.87), channel_id=1, source_target_pairs={{0,32},{1,33},{2,34},{3,35},{4,36},{5,37},{6,38},{7,39},{8,40},{9,... | collective-permute-start | bytes 983048 | tf_op jit(solution)/shard_map/ppermute | solution.py:34
  6.8 5.5 %copy-start = (bf16[1024,1024]{1,0:T(8,128)(2,1)S(1)}, bf16[1024,1024]{1,0:T(8,128)(2,1)}, u32[]{:S(2)}) copy-start(bf16[1024,1024]{1,0:T(8,128)(2,1)} %refs_10_.3) | copy-start | bytes 6291460
  6.8 10.6 %collective-permute-start.1 = (bf16[160,1024]{1,0:T(8,128)(2,1)S(1)}, bf16[160,1024]{1,0:T(8,128)(2,1)S(1)}, u32[]{:S(2)}, u32[]{:S(2)}) collective-permute-start(bf16[160,1024]{1,0:T(8,128)(2,1)S(1)} %get-tuple-element.86), channel_id=1, source_target_pairs={{0,96},{1,97},{2,98},{3,99},{4,100},{5,101},{6,102},{7,103},{8,104... | collective-permute-start | bytes 983048 | tf_op jit(solution)/shard_map/ppermute | solution.py:34
  8.6 14.8 %collective-permute-start.4 = (bf16[160,1024]{1,0:T(8,128)(2,1)S(1)}, bf16[160,1024]{1,0:T(8,128)(2,1)S(1)}, u32[]{:S(2)}, u32[]{:S(2)}) collective-permute-start(bf16[160,1024]{1,0:T(8,128)(2,1)S(1)} %get-tuple-element.86), channel_id=1, source_target_pairs={{0,32},{1,33},{2,34},{3,35},{4,36},{5,37},{6,38},{7,39},{8,40},{9,... | collective-permute-start | bytes 983048 | tf_op jit(solution)/shard_map/ppermute | solution.py:34
  8.9 14.5 %collective-permute-start.5 = (bf16[160,1024]{1,0:T(8,128)(2,1)S(1)}, bf16[160,1024]{1,0:T(8,128)(2,1)S(1)}, u32[]{:S(2)}, u32[]{:S(2)}) collective-permute-start(bf16[160,1024]{1,0:T(8,128)(2,1)S(1)} %get-tuple-element.87), channel_id=1, source_target_pairs={{0,96},{1,97},{2,98},{3,99},{4,100},{5,101},{6,102},{7,103},{8,104... | collective-permute-start | bytes 983048 | tf_op jit(solution)/shard_map/ppermute | solution.py:34
  14.9 5.1 %copy-start.13 = (bf16[320,640]{1,0:T(8,128)(2,1)}, bf16[320,640]{1,0:T(8,128)(2,1)S(1)}, u32[]{:S(2)}) copy-start(bf16[320,640]{1,0:T(8,128)(2,1)S(1)} %get-tuple-element.77.refs_4_) | copy-start | bytes 1228804
  14.9 26.5 %copy-start.1 = (bf16[320,1024]{1,0:T(8,128)(2,1)}, bf16[320,1024]{1,0:T(8,128)(2,1)S(1)}, u32[]{:S(2)}) copy-start(bf16[320,1024]{1,0:T(8,128)(2,1)S(1)} %get-tuple-element.50.refs_0_) | copy-start | bytes 1966084
  20.0 7.3 %copy-start.14 = (bf16[320,640]{1,0:T(8,128)(2,1)}, bf16[320,640]{1,0:T(8,128)(2,1)S(1)}, u32[]{:S(2)}) copy-start(bf16[320,640]{1,0:T(8,128)(2,1)S(1)} %get-tuple-element.78.refs_5_) | copy-start | bytes 1228804
  20.0 21.4 %copy-start.2 = (bf16[320,1024]{1,0:T(8,128)(2,1)}, bf16[320,1024]{1,0:T(8,128)(2,1)S(1)}, u32[]{:S(2)}) copy-start(bf16[320,1024]{1,0:T(8,128)(2,1)S(1)} %get-tuple-element.54.refs_4_.refs_1_) | copy-start | bytes 1966084
  23.4 3.9 %copy-start.7 = (bf16[320,1024]{1,0:T(8,128)(2,1)}, bf16[320,1024]{1,0:T(8,128)(2,1)S(1)}, u32[]{:S(2)}) copy-start(bf16[320,1024]{1,0:T(8,128)(2,1)S(1)} %collective-permute-done.3.first.refs_9_) | copy-start | bytes 1966084
  23.4 3.4 %collective-permute-start.6 = (bf16[320,1024]{1,0:T(8,128)(2,1)S(1)}, bf16[320,1024]{1,0:T(8,128)(2,1)S(1)}, u32[]{:S(2)}, u32[]{:S(2)}) collective-permute-start(bf16[320,1024]{1,0:T(8,128)(2,1)S(1)} %collective-permute-done.3.first.refs_9_), channel_id=1, source_target_pairs={{0,8},{1,9},{2,10},{3,11},{4,12},{5,13},{6,14},{7,15},{8,0},{9,1},... | collective-permute-start | bytes 1966088 | tf_op jit(solution)/shard_map/ppermute | solution.py:34
  23.4 11.3 %collective-permute-start.7 = (bf16[160,1024]{1,0:T(8,128)(2,1)S(1)}, bf16[160,1024]{1,0:T(8,128)(2,1)S(1)}, u32[]{:S(2)}, u32[]{:S(2)}) collective-permute-start(bf16[160,1024]{1,0:T(8,128)(2,1)S(1)} %collective-permute-done.refs_0_.refs_1_), channel_id=1, source_target_pairs={{0,32},{1,33},{2,34},{3,35},{4,36},{5,37},{6,38},{7,39},{8,40},{9,... | collective-permute-start | bytes 983048 | tf_op jit(solution)/shard_map/ppermute | solution.py:34
  24.9 9.9 %collective-permute-start.8 = (bf16[160,1024]{1,0:T(8,128)(2,1)S(1)}, bf16[160,1024]{1,0:T(8,128)(2,1)S(1)}, u32[]{:S(2)}, u32[]{:S(2)}) collective-permute-start(bf16[160,1024]{1,0:T(8,128)(2,1)S(1)} %collective-permute-done.1.refs_1_.refs_2_), channel_id=1, source_target_pairs={{0,96},{1,97},{2,98},{3,99},{4,100},{5,101},{6,102},{7,103},{8,104... | collective-permute-start | bytes 983048 | tf_op jit(solution)/shard_map/ppermute | solution.py:34
  33.3 7.9 %copy-start.15 = (bf16[320,640]{1,0:T(8,128)(2,1)}, bf16[320,640]{1,0:T(8,128)(2,1)S(1)}, u32[]{:S(2)}) copy-start(bf16[320,640]{1,0:T(8,128)(2,1)S(1)} %get-tuple-element.79.refs_6_) | copy-start | bytes 1228804
  33.3 8.1 %copy-start.4 = (bf16[320,1024]{1,0:T(8,128)(2,1)}, bf16[320,1024]{1,0:T(8,128)(2,1)S(1)}, u32[]{:S(2)}) copy-start(bf16[320,1024]{1,0:T(8,128)(2,1)S(1)} %get-tuple-element.67.refs_2_) | copy-start | bytes 1966084
  33.3 8.1 %copy-start.8 = (bf16[320,640]{1,0:T(8,128)(2,1)}, bf16[320,640]{1,0:T(8,128)(2,1)S(1)}, u32[]{:S(2)}) copy-start(bf16[320,640]{1,0:T(8,128)(2,1)S(1)} %get-tuple-element.69.refs_4_) | copy-start | bytes 1228804
  33.3 8.1 %copy-start.9 = (bf16[320,640]{1,0:T(8,128)(2,1)}, bf16[320,640]{1,0:T(8,128)(2,1)S(1)}, u32[]{:S(2)}) copy-start(bf16[320,640]{1,0:T(8,128)(2,1)S(1)} %get-tuple-element.70.refs_5_) | copy-start | bytes 1228804
  33.3 8.1 %copy-start.10 = (bf16[320,640]{1,0:T(8,128)(2,1)}, bf16[320,640]{1,0:T(8,128)(2,1)S(1)}, u32[]{:S(2)}) copy-start(bf16[320,640]{1,0:T(8,128)(2,1)S(1)} %get-tuple-element.71.refs_6_) | copy-start | bytes 1228804
  41.2 2.8 %copy-start.5 = (bf16[320,1024]{1,0:T(8,128)(2,1)}, bf16[320,1024]{1,0:T(8,128)(2,1)S(1)}, u32[]{:S(2)}) copy-start(bf16[320,1024]{1,0:T(8,128)(2,1)S(1)} %get-tuple-element.68.refs_3_) | copy-start | bytes 1966084
  41.2 2.8 %copy-start.11 = (bf16[320,640]{1,0:T(8,128)(2,1)}, bf16[320,640]{1,0:T(8,128)(2,1)S(1)}, u32[]{:S(2)}) copy-start(bf16[320,640]{1,0:T(8,128)(2,1)S(1)} %get-tuple-element.72.refs_7_) | copy-start | bytes 1228804
  41.3 2.8 %copy-start.16 = (bf16[320,640]{1,0:T(8,128)(2,1)}, bf16[320,640]{1,0:T(8,128)(2,1)S(1)}, u32[]{:S(2)}) copy-start(bf16[320,640]{1,0:T(8,128)(2,1)S(1)} %get-tuple-element.80.refs_7_) | copy-start | bytes 1228804
  41.3 2.8 %collective-permute-start.9 = (bf16[8,64,1024]{2,1,0:T(8,128)(2,1)S(1)}, bf16[8,64,1024]{2,1,0:T(8,128)(2,1)S(1)}, u32[]{:S(2)}, u32[]{:S(2)}) collective-permute-start(bf16[8,64,1024]{2,1,0:T(8,128)(2,1)S(1)} %get-tuple-element.66), channel_id=1, source_target_pairs={{0,8},{1,9},{2,10},{3,11},{4,12},{5,13},{6,14},{7,15},{8,0},{9,1},... | collective-permute-start | bytes 3145736 | tf_op jit(solution)/shard_map/ppermute | solution.py:34
  44.0 6.2 %collective-permute-start.13 = (f32[320,1024]{1,0:T(8,128)}, f32[320,1024]{1,0:T(8,128)S(1)}, u32[]{:S(2)}, u32[]{:S(2)}) collective-permute-start(f32[320,1024]{1,0:T(8,128)} %shard_map.56), channel_id=1, source_target_pairs={{0,8},{1,9},{2,10},{3,11},{4,12},{5,13},{6,14},{7,15},{8,0},{9,1},... | collective-permute-start | bytes 3932168 | tf_op jit(solution)/shard_map/ppermute | solution.py:34
  46.0 21.1 %all-to-all-start = ((bf16[8,64,1024]{2,1,0:T(8,128)(2,1)}), bf16[8,64,1024]{2,1,0:T(8,128)(2,1)}, u32[]{:S(2)}, u32[]{:S(2)}) async-start(bf16[8,64,1024]{2,1,0:T(8,128)(2,1)} %shard_map.57), calls=%async_computation | async-start | bytes 2097152 | tf_op jit(solution)/shard_map/all_to_all | solution.py:237
  50.2 1.1 %copy-start.17 = (f32[320,1024]{1,0:T(8,128)}, f32[320,1024]{1,0:T(8,128)S(1)}, u32[]{:S(2)}) copy-start(f32[320,1024]{1,0:T(8,128)S(1)} %collective-permute-done.13.refs_8_) | copy-start | bytes 3932164
  63.3 20.6 %copy-start.12 = (f32[320,1024]{1,0:T(8,128)S(1)}, f32[320,1024]{1,0:T(8,128)}, u32[]{:S(2)}) copy-start(f32[320,1024]{1,0:T(8,128)} %get-tuple-element.81.home) | copy-start | bytes 3932164
  63.3 20.6 %collective-permute-start.16 = (f32[320,1024]{1,0:T(8,128)}, f32[320,1024]{1,0:T(8,128)S(1)}, u32[]{:S(2)}, u32[]{:S(2)}) collective-permute-start(f32[320,1024]{1,0:T(8,128)} %get-tuple-element.82), channel_id=1, source_target_pairs={{0,8},{1,9},{2,10},{3,11},{4,12},{5,13},{6,14},{7,15},{8,0},{9,1},... | collective-permute-start | bytes 3932168 | tf_op jit(solution)/shard_map/ppermute | solution.py:34
  63.3 19.2 %collective-permute-start.14 = (bf16[320,1024]{1,0:T(8,128)(2,1)}, bf16[320,1024]{1,0:T(8,128)(2,1)}, u32[]{:S(2)}, u32[]{:S(2)}) collective-permute-start(bf16[320,1024]{1,0:T(8,128)(2,1)} %shard_map.58), channel_id=1, source_target_pairs={{0,16},{1,17},{2,18},{3,19},{4,20},{5,21},{6,22},{7,23},{8,24},{9,... | collective-permute-start | bytes 1966088 | tf_op jit(solution)/shard_map/ppermute | solution.py:34
  68.5 8.3 %collective-permute-start.10 = (bf16[64,1024]{1,0:T(8,128)(2,1)S(1)}, bf16[64,1024]{1,0:T(8,128)(2,1)S(1)}, u32[]{:S(2)}, u32[]{:S(2)}) collective-permute-start(bf16[64,1024]{1,0:T(8,128)(2,1)S(1)} %reduce_sum.12), channel_id=1, source_target_pairs={{0,4},{1,5},{2,6},{3,7},{4,0},{5,1},{6,2},{7,3},{8,12},{9,13},{10,... | collective-permute-start | bytes 393224 | tf_op jit(solution)/shard_map/ppermute | solution.py:34
  72.4 6.7 %collective-permute-start.11 = (bf16[64,1024]{1,0:T(8,128)(2,1)S(1)}, bf16[64,1024]{1,0:T(8,128)(2,1)S(1)}, u32[]{:S(2)}, u32[]{:S(2)}) collective-permute-start(bf16[64,1024]{1,0:T(8,128)(2,1)S(1)} %reduce_sum.12), channel_id=1, source_target_pairs={{0,2},{1,3},{2,4},{3,5},{4,6},{5,7},{6,0},{7,1},{8,10},{9,11},{10,... | collective-permute-start | bytes 393224 | tf_op jit(solution)/shard_map/ppermute | solution.py:34
  73.4 6.2 %collective-permute-start.12 = (bf16[64,1024]{1,0:T(8,128)(2,1)S(1)}, bf16[64,1024]{1,0:T(8,128)(2,1)S(1)}, u32[]{:S(2)}, u32[]{:S(2)}) collective-permute-start(bf16[64,1024]{1,0:T(8,128)(2,1)S(1)} %reduce_sum.12), channel_id=1, source_target_pairs={{0,6},{1,7},{2,0},{3,1},{4,2},{5,3},{6,4},{7,5},{8,14},{9,15},{10,... | collective-permute-start | bytes 393224 | tf_op jit(solution)/shard_map/ppermute | solution.py:34
  82.5 5.2 %collective-permute-start.15 = (bf16[64,1024]{1,0:T(8,128)(2,1)S(1)}, bf16[64,1024]{1,0:T(8,128)(2,1)S(1)}, u32[]{:S(2)}, u32[]{:S(2)}) collective-permute-start(bf16[64,1024]{1,0:T(8,128)(2,1)S(1)} %add_convert_fusion), channel_id=1, source_target_pairs={{0,1},{1,0},{2,3},{3,2},{4,5},{5,4},{6,7},{7,6},{8,9},{9,8},{10,11... | collective-permute-start | bytes 393224 | tf_op jit(solution)/shard_map/ppermute | solution.py:34

commit v4 on v3

--- a/solution.py
+++ b/solution.py
@@ -53,7 +53,7 @@
     return slopes.astype(BF16)
 
 
-def unit_kernel(first, second, out):
+def text_units(first, second, out):
     rows = first.shape[0]
     out[:rows] = normalize(first[...].astype(F32))[0].astype(BF16)
     out[rows:] = normalize(second[...].astype(F32))[0].astype(BF16)
@@ -62,6 +62,11 @@
 def stacked(refs):
     blocks = [ref[...] for ref in refs]
     return blocks[0] if len(blocks) == 1 else jnp.concatenate(blocks)
+
+
+def first_kernel(feats, proj_weight, text, text_c, *outs):
+    text_units(text, text_c, outs[0])
+    early_kernel(1, True, feats, proj_weight, *outs)
 
 
 def early_kernel(count, diagonal, *refs):
@@ -88,8 +93,9 @@
 
 
 def middle_kernel(*refs):
-    own, near, (high, low, proj_weight, texts_a, texts_b) = refs[:4], refs[4:8], refs[8:13]
-    outs = refs[13:]
+    own, near, (high, low, proj_weight, texts_a) = refs[:4], refs[4:8], refs[8:12]
+    (text_y, text_yc, texts_b), outs = refs[12:15], refs[15:]
+    text_units(text_y, text_yc, texts_b)
     for k, (unit, norm, length, grad) in enumerate((own, near)):
         slopes = slopes_of(unit[...], texts_b[...], False)
         outs[2 * k][...] = slopes
@@ -130,13 +136,6 @@
     )
 
 
-def text_kernel(count, *refs):
-    units, slopes, (home, away) = refs[:count], refs[count : 2 * count], refs[2 * count :]
-    rows = home.shape[0]
-    total = text_rows(units, slopes, 0, 2 * rows)
-    home[...], away[...] = total[:rows], total[rows:]
-
-
 def away_kernel(count, *refs):
     units, slopes, away = refs[:count], refs[count : 2 * count], refs[2 * count]
     rows = away.shape[0]
@@ -144,9 +143,13 @@
 
 
 def home_kernel(count, *refs):
-    units, slopes, (received, feats, out) = refs[:count], refs[count : 2 * count], refs[2 * count :]
-    total = received[...] + text_rows(units, slopes, 0, out.shape[0])
-    out[...] = project(total, *normalize(feats[...].astype(F32))).astype(out.dtype)
+    units, slopes_a, slopes_b = (refs[k * count : (k + 1) * count] for k in range(3))
+    received, feats, y_out, home, away = refs[3 * count :]
+    rows = feats.shape[0]
+    total = received[...] + text_rows(units, slopes_b, 0, rows)
+    y_out[...] = project(total, *normalize(feats[...].astype(F32))).astype(BF16)
+    total = text_rows(units, slopes_a, 0, 2 * rows)
+    home[...], away[...] = total[:rows], total[rows:]
 
 
 def final_kernel(home, received, rest, feats, out):
@@ -175,40 +178,36 @@
     unit_like, grad_like = ((rows, width), BF16), ((rows, width), F32)
     slopes_like = ((rows, texts), BF16)
 
-    text_c, text_y = send(text_feats, c=1), send(text_feats, yh=1)
-    low, high = sensor_feats[:half], sensor_feats[half:]
+    low, high, text = lax.optimization_barrier(
+        (sensor_feats[:half], sensor_feats[half:], text_feats)
+    )
+    text_c, text_y = send(text, c=1), send(text, yh=1)
     right_low, left_high = send(low, x=1), send(high, x=-1)
     right_high, left_low = send(high, x=1), send(low, x=-1)
 
-    def units(first, second):
-        return call(unit_kernel, [((texts, width), BF16)], [first, second], 12)[0]
-
-    def early(feats, diagonal):
-        return call(
-            functools.partial(early_kernel, len(feats), diagonal),
-            [unit_like, grad_like, ((rows, 1), F32), slopes_like, grad_like],
-            [*feats, proj_weight, texts_a],
-            16,
-        )
-
-    texts_a = units(text_feats, text_c)
-    unit, norm, length, slopes_a, grad = early([sensor_feats], True)
+    texts_like = ((texts, width), BF16)
+    early_like = [unit_like, grad_like, ((rows, 1), F32), slopes_like, grad_like]
+    texts_a, unit, norm, length, slopes_a, grad = call(
+        first_kernel, [texts_like, *early_like], [sensor_feats, proj_weight, text_feats, text_c], 18
+    )
     right_low, left_high, grad = lax.optimization_barrier((right_low, left_high, grad))
     far_low, far_high = send(right_low, x=1), send(left_high, x=-1)
-    near_unit, near_norm, near_length, near_a, near = early([right_low, left_high], False)
+    near_unit, near_norm, near_length, near_a, near = call(
+        functools.partial(early_kernel, 2, False),
+        early_like, [right_low, left_high, proj_weight, texts_a], 16,
+    )
     text_y, right_high, left_low, near = lax.optimization_barrier(
         (text_y, right_high, left_low, near)
     )
-    texts_b = units(text_y, send(text_y, c=1))
-    slopes_b, raw_grad, near_b, near_grad, next_unit, next_a, next_b, next_grad = call(
+    texts_b, slopes_b, raw_grad, near_b, near_grad, next_unit, next_a, next_b, next_grad = call(
         middle_kernel,
         [
-            slopes_like, unit_like, slopes_like, unit_like,
+            texts_like, slopes_like, unit_like, slopes_like, unit_like,
             unit_like, slopes_like, slopes_like, unit_like,
         ],
         [
             unit, norm, length, grad, near_unit, near_norm, near_length, near,
-            right_high, left_low, proj_weight, texts_a, texts_b,
+            right_high, left_low, proj_weight, texts_a, text_y, send(text_y, c=1),
         ],
         30,
     )
@@ -235,11 +234,15 @@
     weight_recv, away_b = lax.optimization_barrier((weight_recv, away_b))
     weight_sum = call(add_kernel, [(share, BF16)], [mine, weight_recv], 12)[0]
     weight_all = lax.all_to_all(weight_sum, ("x", "yh"), split_axis=0, concat_axis=0, tiled=True)
-    text_send = text_sums(home_kernel, [unit_like], 58, half_b, send(away_b, c=1), text_y)[0]
-    text_out = send(text_send, yh=1)
-    slopes_a, text_send = lax.optimization_barrier((slopes_a, text_send))
-    home_a, away_a = text_sums(text_kernel, [grad_like] * 2, 58, [slopes_a, near_a, next_a, far_a])
-    away_a = send(away_a, c=1)
+    text_send, home_a, away_a = text_sums(
+        home_kernel,
+        [unit_like, grad_like, grad_like],
+        58,
+        [slopes_a, near_a, next_a, far_a, *half_b],
+        send(away_b, c=1),
+        text_y,
+    )
+    text_out, away_a = send(text_send, yh=1), send(away_a, c=1)
 
     weight_sum = jnp.sum(weight_all.astype(F32), axis=0).astype(BF16)
     across = send(weight_sum, z=2)
@@ -247,7 +250,6 @@
     weight_sum = (
         (weight_sum.astype(F32) + across.astype(F32)) + (ahead.astype(F32) + behind.astype(F32))
     ).astype(BF16)
-    weight_sum, text_out = lax.optimization_barrier((weight_sum, text_out))
     across = send(weight_sum, yl=1)
     text_grad = call(final_kernel, [grad_like], [home_a, away_a, text_out, text_feats], 16)[0]
     across, text_grad = lax.optimization_barrier((across, text_grad))

time: 89.2 us -> 85.5 us (0.959)
  Pallas kernels: 37 us -> 33.4 us
  local copies, waits for them, and re-layouts: 2.3 us -> 5.56 us
  waiting for transfers between devices: 15.4 us -> 12.5 us
    ppermute x17, waiting for transfers between devices: 15.2 us -> 9.33 us  [send(): return lax.ppermute(block, AXES, route)]
    pallas_call x11 -> x8, Pallas kernels: 37 us -> 33.4 us  [call(): pl.pallas_call(kernel, out_shape=shapes, in_specs=[vmem] * len(operands),...]
    unnamed x36 -> x38, local copies, waits for them, and re-layouts: 1.12 us -> 4.34 us
    all_to_all x1, waiting for transfers between devices: 0.19 us -> 3.17 us  [local(): lax.all_to_all(weight_sum, ('x', 'yh'), split_axis=0, concat_axis=0, tile...]
  transfers between devices with their start and end apart: 18 -> 18, of which waited for: 10 -> 10; matrix products, arithmetic and copies ran while one was open for 3% -> 2% of each run, Pallas kernels for 35% -> 32%
where the time goes in v4:
time: 85.5 us; the launch traced here: 84.6 us
  Pallas kernels  33.4 us (39%)
  starting transfers between devices  30 us (35%)
  waiting for transfers between devices  12.5 us (15%)
  local copies, waits for them, and re-layouts  5.56 us (7%)
  other arithmetic  2.21 us (3%)
  between operations  0.9 us (1%)
    pallas_call x8, Pallas kernels, call(): pl.pallas_call(kernel, out_shape=shapes, in_specs=[vmem] * len(operands),...  33.4 us
    ppermute x17, starting transfers between devices, send(): return lax.ppermute(block, AXES, route)  25.8 us
    ppermute x17, waiting for transfers between devices, send(): return lax.ppermute(block, AXES, route)  9.33 us
    unnamed x38, local copies, waits for them, and re-layouts  4.34 us
    all_to_all x1, starting transfers between devices, local(): lax.all_to_all(weight_sum, ('x', 'yh'), split_axis=0, concat_axis=0, tile...  4.24 us
    all_to_all x1, waiting for transfers between devices, local(): lax.all_to_all(weight_sum, ('x', 'yh'), split_axis=0, concat_axis=0, tile...  3.17 us
  transfers between devices with their start and end apart: 18, of which 10 were waited for; matrix products, arithmetic and copies ran while one was open for 2% of the time, Pallas kernels for 32%

profile of v4, /device:TPU:0, one launch (start us, length us, event | category | flops | bytes accessed | tf_op | source)
XLA Modules:
  0.0 84.6 jit_solution(1504103888519966516)
XLA Ops:
  0.6 1.2 %fusion = (bf16[160,1024]{1,0:T(8,128)(2,1)S(1)}, bf16[160,1024]{1,0:T(8,128)(2,1)S(1)}) fusion(bf16[320,1024]{1,0:T(8,128)(2,1)} %refs_0_.1), kind=kLoop, calls=%fused_computation.2 | loop fusion | bytes 1310720 | tf_op jit(solution)/shard_map/slice | solution.py:182
  1.9 0.1 copy-done.5
  2.0 0.0 collective-permute-start.2
  2.0 3.3 %collective-permute-start.3 = (bf16[320,1024]{1,0:T(8,128)(2,1)S(1)}, bf16[320,1024]{1,0:T(8,128)(2,1)S(1)}, u32[]{:S(2)}, u32[]{:S(2)}) collective-permute-start(bf16[320,1024]{1,0:T(8,128)(2,1)S(1)} %copy-done.5), channel_id=1, source_target_pairs={{0,16},{1,17},{2,18},{3,19},{4,20},{5,21},{6,22},{7,23},{8,24},{9,... | collective-permute-start | bytes 1966088 | tf_op jit(solution)/shard_map/ppermute | solution.py:34
  5.3 1.5 %collective-permute-start = (bf16[160,1024]{1,0:T(8,128)(2,1)S(1)}, bf16[160,1024]{1,0:T(8,128)(2,1)S(1)}, u32[]{:S(2)}, u32[]{:S(2)}) collective-permute-start(bf16[160,1024]{1,0:T(8,128)(2,1)S(1)} %get-tuple-element.47), channel_id=1, source_target_pairs={{0,32},{1,33},{2,34},{3,35},{4,36},{5,37},{6,38},{7,39},{8,40},{9,... | collective-permute-start | bytes 983048 | tf_op jit(solution)/shard_map/ppermute | solution.py:34
  6.8 1.7 %collective-permute-start.1 = (bf16[160,1024]{1,0:T(8,128)(2,1)S(1)}, bf16[160,1024]{1,0:T(8,128)(2,1)S(1)}, u32[]{:S(2)}, u32[]{:S(2)}) collective-permute-start(bf16[160,1024]{1,0:T(8,128)(2,1)S(1)} %get-tuple-element.48), channel_id=1, source_target_pairs={{0,96},{1,97},{2,98},{3,99},{4,100},{5,101},{6,102},{7,103},{8,104... | collective-permute-start | bytes 983048 | tf_op jit(solution)/shard_map/ppermute | solution.py:34
  8.6 0.3 collective-permute-start.4
  8.8 0.0 collective-permute-done.2.text_c
  8.9 3.0 %collective-permute-start.5 = (bf16[160,1024]{1,0:T(8,128)(2,1)S(1)}, bf16[160,1024]{1,0:T(8,128)(2,1)S(1)}, u32[]{:S(2)}, u32[]{:S(2)}) collective-permute-start(bf16[160,1024]{1,0:T(8,128)(2,1)S(1)} %get-tuple-element.47), channel_id=1, source_target_pairs={{0,96},{1,97},{2,98},{3,99},{4,100},{5,101},{6,102},{7,103},{8,104... | collective-permute-start | bytes 983048 | tf_op jit(solution)/shard_map/ppermute | solution.py:34
  11.8 1.6 %copy-done = bf16[1024,1024]{1,0:T(8,128)(2,1)S(1)} copy-done((bf16[1024,1024]{1,0:T(8,128)(2,1)S(1)}, bf16[1024,1024]{1,0:T(8,128)(2,1)}, u32[]{:S(2)}) %copy-start) | copy-done | bytes 2097176
  13.4 2.6 %shard_map.50 = (bf16[640,1024]{1,0:T(8,128)(2,1)S(1)}, bf16[320,1024]{1,0:T(8,128)(2,1)S(1)}, f32[320,1024]{1,0:T(8,128)S(1)}, f32[320,1]{1,0:T(8,128)S(1)}, bf...) custom-call(bf16[320,1024]{1,0:T(8,128)(2,1)S(1)} %copy-done.2, bf16[1024,1024]{1,0:T(8,128)(2,1)S(1)} %copy-done, ...), custom_call_target="tpu_custom_call" | custom-call | flops 1 | bytes 1 | tf_op jit(solution)/shard_map/pallas_call | solution.py:163
  16.0 0.8 copy-done.14
  16.8 0.3 collective-permute-done.refs_0_.refs_1_
  17.1 0.3 collective-permute-done.1.refs_1_.refs_2_
  17.4 2.5 %shard_map.51 = (bf16[320,1024]{1,0:T(8,128)(2,1)S(1)}, f32[320,1024]{1,0:T(8,128)S(1)}, f32[320,1]{1,0:T(8,128)S(1)}, bf16[320,640]{1,0:T(8,128)(2,1)S(1)}, f32[320,1024]{1,0:T(8,128)S(1)}) custom-call(bf16[160,1024]{1,0:T(8,128)(2,1)S(1)} %collective-permute-done.refs_0_.refs_1_, bf16[160,1024]{1,0:T(8,128)(2,1)S(1)} %collective-permute-done.1.refs_1_.refs_2_, ...), custom_call_target="tpu_custom_call" | custom-call | flops 1 | bytes 1 | tf_op jit(solution)/shard_map/pallas_call | solution.py:163
  19.9 0.8 copy-done.15
  20.7 2.6 %collective-permute-done.4.refs_8_.refs_3_ = bf16[160,1024]{1,0:T(8,128)(2,1)S(1)} collective-permute-done((bf16[160,1024]{1,0:T(8,128)(2,1)S(1)}, bf16[160,1024]{1,0:T(8,128)(2,1)S(1)}, u32[]{:S(2)}, u32[]{:S(2)}) %collective-permute-start.4) | collective-permute-done | bytes 327712 | tf_op jit(solution)/shard_map/ppermute | solution.py:34
  23.4 0.1 collective-permute-start.6
  23.5 1.5 %collective-permute-start.7 = (bf16[160,1024]{1,0:T(8,128)(2,1)S(1)}, bf16[160,1024]{1,0:T(8,128)(2,1)S(1)}, u32[]{:S(2)}, u32[]{:S(2)}) collective-permute-start(bf16[160,1024]{1,0:T(8,128)(2,1)S(1)} %collective-permute-done.refs_0_.refs_1_), channel_id=1, source_target_pairs={{0,32},{1,33},{2,34},{3,35},{4,36},{5,37},{6,38},{7,39},{8,40},{9,... | collective-permute-start | bytes 983048 | tf_op jit(solution)/shard_map/ppermute | solution.py:34
  24.9 1.8 %collective-permute-start.8 = (bf16[160,1024]{1,0:T(8,128)(2,1)S(1)}, bf16[160,1024]{1,0:T(8,128)(2,1)S(1)}, u32[]{:S(2)}, u32[]{:S(2)}) collective-permute-start(bf16[160,1024]{1,0:T(8,128)(2,1)S(1)} %collective-permute-done.1.refs_1_.refs_2_), channel_id=1, source_target_pairs={{0,96},{1,97},{2,98},{3,99},{4,100},{5,101},{6,102},{7,103},{8,104... | collective-permute-start | bytes 983048 | tf_op jit(solution)/shard_map/ppermute | solution.py:34
  26.8 0.0 collective-permute-done.6.refs_13_
  26.8 6.4 %shard_map.52 = (bf16[640,1024]{1,0:T(8,128)(2,1)S(1)}, bf16[320,640]{1,0:T(8,128)(2,1)S(1)}, bf16[320,1024]{1,0:T(8,128)(2,1)S(1)}, bf16[320,640]{1,0:T(8,128)(...) custom-call(bf16[320,1024]{1,0:T(8,128)(2,1)S(1)} %get-tuple-element, ...), custom_call_target="tpu_custom_call" | custom-call | flops 1 | bytes 1 | tf_op jit(solution)/shard_map/pallas_call | solution.py:163
  33.2 1.6 %collective-permute-done.7.refs_5_ = bf16[160,1024]{1,0:T(8,128)(2,1)S(1)} collective-permute-done((bf16[160,1024]{1,0:T(8,128)(2,1)S(1)}, bf16[160,1024]{1,0:T(8,128)(2,1)S(1)}, u32[]{:S(2)}, u32[]{:S(2)}) %collective-permute-start.7) | collective-permute-done | bytes 327712 | tf_op jit(solution)/shard_map/ppermute | solution.py:34
  34.8 6.4 %shard_map.53 = (bf16[320,1024]{1,0:T(8,128)(2,1)S(1)}, bf16[320,640]{1,0:T(8,128)(2,1)S(1)}, bf16[320,640]{1,0:T(8,128)(2,1)S(1)}, f32[8,64,1024]{2,1,0:T(8,128)S(1)}, bf16[8,64,1024]{2,1,0:T(8,128)(2,1)S(1)}) custom-call(bf16[320,1024]{1,0:T(8,128)(2,1)S(1)} %copy-done.2, bf16[160,1024]{1,0:T(8,128)(2,1)S(1)} %collective-permute-done.refs_0_.refs_1_, ...), custom_call_target="tpu_custom_call" | custom-call | flops 1 | bytes 1 | tf_op jit(solution)/shard_map/pallas_call | solution.py:163
  41.3 0.1 collective-permute-start.9
  41.4 2.6 %shard_map.54 = f32[320,1024]{1,0:T(8,128)} custom-call(bf16[320,1024]{1,0:T(8,128)(2,1)S(1)} %get-tuple-element.57.refs_0_, bf16[320,1024]{1,0:T(8,128)(2,1)S(1)} %get-tuple-element.61.refs_4_.refs_1_, bf16[320,1024]{1,0:T(8,128)(2,1)S(1)} %get-tuple-element.75.refs_2_, bf16[320,1024]{1,0:T(8,128)(2,1)S(1)} %get-tuple-element.76.refs_3_, ...), custom_call_target="tpu_custom_call" | custom-call | flops 1 | bytes 1 | tf_op jit(solution)/shard_map/pallas_call | solution.py:163
  44.1 0.8 collective-permute-start.14
  44.8 1.1 %shard_map.55 = bf16[8,64,1024]{2,1,0:T(8,128)(2,1)} custom-call(f32[8,64,1024]{2,1,0:T(8,128)S(1)} %get-tuple-element.73.mine, bf16[8,64,1024]{2,1,0:T(8,128)(2,1)S(1)} %collective-permute-done.9.received), custom_call_target="tpu_custom_call" | custom-call | flops 1 | bytes 1 | tf_op jit(solution)/shard_map/pallas_call | solution.py:163
  46.0 4.2 %all-to-all-start = ((bf16[8,64,1024]{2,1,0:T(8,128)(2,1)}), bf16[8,64,1024]{2,1,0:T(8,128)(2,1)}, u32[]{:S(2)}, u32[]{:S(2)}) async-start(bf16[8,64,1024]{2,1,0:T(8,128)(2,1)} %shard_map.55), calls=%async_computation | async-start | bytes 2097152 | tf_op jit(solution)/shard_map/all_to_all | solution.py:236
  50.2 0.0 copy-start.18
  50.2 1.0 %copy-done.18 = f32[320,1024]{1,0:T(8,128)} copy-done((f32[320,1024]{1,0:T(8,128)}, f32[320,1024]{1,0:T(8,128)S(1)}, u32[]{:S(2)}) %copy-start.18) | copy-done | bytes 1310744
  51.3 9.0 %shard_map.56 = (bf16[320,1024]{1,0:T(8,128)(2,1)}, f32[320,1024]{1,0:T(8,128)}, f32[320,1024]{1,0:T(8,128)}) custom-call(bf16[320,1024]{1,0:T(8,128)(2,1)} %copy-done.3, bf16[320,1024]{1,0:T(8,128)(2,1)} %copy-done.4, bf16[320,1024]{1,0:T(8,128)(2,1)} %copy-done.7, bf16[320,1024]{1,0:T(8,128)(2,1)} %copy-done.8, bf16[320,640]{1,0:T(8,128)(2,1)} %copy-done.14, ...), custom_call_target="tpu_custom_call" | custom-call | flops 1 | bytes 1 | tf_op jit(solution)/shard_map/pallas_call | solution.py:163
  60.3 0.0 collective-permute-start.15
  60.3 3.5 %collective-permute-start.16 = (bf16[320,1024]{1,0:T(8,128)(2,1)}, bf16[320,1024]{1,0:T(8,128)(2,1)}, u32[]{:S(2)}, u32[]{:S(2)}) collective-permute-start(bf16[320,1024]{1,0:T(8,128)(2,1)} %get-tuple-element.89), channel_id=1, source_target_pairs={{0,16},{1,17},{2,18},{3,19},{4,20},{5,21},{6,22},{7,23},{8,24},{9,... | collective-permute-start | bytes 1966088 | tf_op jit(solution)/shard_map/ppermute | solution.py:34
  63.9 3.2 %all-to-all-done = bf16[8,64,1024]{2,1,0:T(8,128)(2,1)} async-done(((bf16[8,64,1024]{2,1,0:T(8,128)(2,1)}), bf16[8,64,1024]{2,1,0:T(8,128)(2,1)}, u32[]{:S(2)}, u32[]{:S(2)}) %all-to-all-start) | async-done | bytes 1048608 | tf_op jit(solution)/shard_map/all_to_all | solution.py:236
  67.0 1.4 %reduce_sum.12 = bf16[64,1024]{1,0:T(8,128)(2,1)S(1)} reduce(bf16[8,64,1024]{2,1,0:T(8,128)(2,1)} %all-to-all-done, bf16[]{:T(256)} %constant.2.clone.1), dimensions={0}, to_apply=%region_0.0 | reduce | flops 458752 | bytes 1179650 | tf_op jit(solution)/shard_map/reduce_sum | solution.py:247
  68.4 3.9 %collective-permute-start.10 = (bf16[64,1024]{1,0:T(8,128)(2,1)S(1)}, bf16[64,1024]{1,0:T(8,128)(2,1)S(1)}, u32[]{:S(2)}, u32[]{:S(2)}) collective-permute-start(bf16[64,1024]{1,0:T(8,128)(2,1)S(1)} %reduce_sum.12), channel_id=1, source_target_pairs={{0,4},{1,5},{2,6},{3,7},{4,0},{5,1},{6,2},{7,3},{8,12},{9,13},{10,... | collective-permute-start | bytes 393224 | tf_op jit(solution)/shard_map/ppermute | solution.py:34
  72.4 1.0 %collective-permute-start.11 = (bf16[64,1024]{1,0:T(8,128)(2,1)S(1)}, bf16[64,1024]{1,0:T(8,128)(2,1)S(1)}, u32[]{:S(2)}, u32[]{:S(2)}) collective-permute-start(bf16[64,1024]{1,0:T(8,128)(2,1)S(1)} %reduce_sum.12), channel_id=1, source_target_pairs={{0,2},{1,3},{2,4},{3,5},{4,6},{5,7},{6,0},{7,1},{8,10},{9,11},{10,... | collective-permute-start | bytes 393224 | tf_op jit(solution)/shard_map/ppermute | solution.py:34
  73.4 2.2 %collective-permute-start.12 = (bf16[64,1024]{1,0:T(8,128)(2,1)S(1)}, bf16[64,1024]{1,0:T(8,128)(2,1)S(1)}, u32[]{:S(2)}, u32[]{:S(2)}) collective-permute-start(bf16[64,1024]{1,0:T(8,128)(2,1)S(1)} %reduce_sum.12), channel_id=1, source_target_pairs={{0,6},{1,7},{2,0},{3,1},{4,2},{5,3},{6,4},{7,5},{8,14},{9,15},{10,... | collective-permute-start | bytes 393224 | tf_op jit(solution)/shard_map/ppermute | solution.py:34
  75.6 1.1 %collective-permute-done.10 = bf16[64,1024]{1,0:T(8,128)(2,1)S(1)} collective-permute-done((bf16[64,1024]{1,0:T(8,128)(2,1)S(1)}, bf16[64,1024]{1,0:T(8,128)(2,1)S(1)}, u32[]{:S(2)}, u32[]{:S(2)}) %collective-permute-start.10) | collective-permute-done | bytes 131104 | tf_op jit(solution)/shard_map/ppermute | solution.py:34
  76.7 2.0 %collective-permute-done.11 = bf16[64,1024]{1,0:T(8,128)(2,1)S(1)} collective-permute-done((bf16[64,1024]{1,0:T(8,128)(2,1)S(1)}, bf16[64,1024]{1,0:T(8,128)(2,1)S(1)}, u32[]{:S(2)}, u32[]{:S(2)}) %collective-permute-start.11) | collective-permute-done | bytes 131104 | tf_op jit(solution)/shard_map/ppermute | solution.py:34
  78.7 0.1 collective-permute-done.12
  78.8 0.1 add_convert_fusion
  78.8 1.0 %collective-permute-start.13 = (bf16[64,1024]{1,0:T(8,128)(2,1)S(1)}, bf16[64,1024]{1,0:T(8,128)(2,1)S(1)}, u32[]{:S(2)}, u32[]{:S(2)}) collective-permute-start(bf16[64,1024]{1,0:T(8,128)(2,1)S(1)} %add_convert_fusion), channel_id=1, source_target_pairs={{0,1},{1,0},{2,3},{3,2},{4,5},{5,4},{6,7},{7,6},{8,9},{9,8},{10,11... | collective-permute-start | bytes 393224 | tf_op jit(solution)/shard_map/ppermute | solution.py:34
  79.8 0.9 %collective-permute-done.16.rest = bf16[320,1024]{1,0:T(8,128)(2,1)} collective-permute-done((bf16[320,1024]{1,0:T(8,128)(2,1)}, bf16[320,1024]{1,0:T(8,128)(2,1)}, u32[]{:S(2)}, u32[]{:S(2)}) %collective-permute-start.16) | collective-permute-done | bytes 655392 | tf_op jit(solution)/shard_map/ppermute | solution.py:34
  80.7 2.7 %shard_map.57 = f32[320,1024]{1,0:T(8,128)} custom-call(f32[320,1024]{1,0:T(8,128)S(1)} %copy-done.13, f32[320,1024]{1,0:T(8,128)S(1)} %collective-permute-done.15.received, bf16[320,1024]{1,0:T(8,128)(2,1)} %collective-permute-done.16.rest, bf16[320,1024]{1,0:T(8,128)(2,1)S(1)} %copy-done.5), custom_call_target="tpu_custom_call" | custom-call | flops 1 | bytes 1 | tf_op jit(solution)/shard_map/pallas_call | solution.py:163
  83.4 0.5 collective-permute-done.13
  83.9 0.7 convert_add_fusion
  (38 shorter events, 0.1 us)
Async XLA Ops:
  0.6 11.2 %copy-start.2 = (bf16[320,1024]{1,0:T(8,128)(2,1)S(1)}, bf16[320,1024]{1,0:T(8,128)(2,1)}, u32[]{:S(2)}) copy-start(bf16[320,1024]{1,0:T(8,128)(2,1)} %refs_0_.1) | copy-start | bytes 1966084
  0.6 1.4 %copy-start.5 = (bf16[320,1024]{1,0:T(8,128)(2,1)S(1)}, bf16[320,1024]{1,0:T(8,128)(2,1)}, u32[]{:S(2)}) copy-start(bf16[320,1024]{1,0:T(8,128)(2,1)} %feats.3) | copy-start | bytes 1966084
  2.0 6.9 %collective-permute-start.2 = (bf16[320,1024]{1,0:T(8,128)(2,1)S(1)}, bf16[320,1024]{1,0:T(8,128)(2,1)S(1)}, u32[]{:S(2)}, u32[]{:S(2)}) collective-permute-start(bf16[320,1024]{1,0:T(8,128)(2,1)S(1)} %copy-done.5), channel_id=1, source_target_pairs={{0,8},{1,9},{2,10},{3,11},{4,12},{5,13},{6,14},{7,15},{8,0},{9,1},... | collective-permute-start | bytes 1966088 | tf_op jit(solution)/shard_map/ppermute | solution.py:34
  2.0 21.4 %collective-permute-start.3 = (bf16[320,1024]{1,0:T(8,128)(2,1)S(1)}, bf16[320,1024]{1,0:T(8,128)(2,1)S(1)}, u32[]{:S(2)}, u32[]{:S(2)}) collective-permute-start(bf16[320,1024]{1,0:T(8,128)(2,1)S(1)} %copy-done.5), channel_id=1, source_target_pairs={{0,16},{1,17},{2,18},{3,19},{4,20},{5,21},{6,22},{7,23},{8,24},{9,... | collective-permute-start | bytes 1966088 | tf_op jit(solution)/shard_map/ppermute | solution.py:34
  5.3 11.8 %collective-permute-start = (bf16[160,1024]{1,0:T(8,128)(2,1)S(1)}, bf16[160,1024]{1,0:T(8,128)(2,1)S(1)}, u32[]{:S(2)}, u32[]{:S(2)}) collective-permute-start(bf16[160,1024]{1,0:T(8,128)(2,1)S(1)} %get-tuple-element.47), channel_id=1, source_target_pairs={{0,32},{1,33},{2,34},{3,35},{4,36},{5,37},{6,38},{7,39},{8,40},{9,... | collective-permute-start | bytes 983048 | tf_op jit(solution)/shard_map/ppermute | solution.py:34
  6.8 10.6 %collective-permute-start.1 = (bf16[160,1024]{1,0:T(8,128)(2,1)S(1)}, bf16[160,1024]{1,0:T(8,128)(2,1)S(1)}, u32[]{:S(2)}, u32[]{:S(2)}) collective-permute-start(bf16[160,1024]{1,0:T(8,128)(2,1)S(1)} %get-tuple-element.48), channel_id=1, source_target_pairs={{0,96},{1,97},{2,98},{3,99},{4,100},{5,101},{6,102},{7,103},{8,104... | collective-permute-start | bytes 983048 | tf_op jit(solution)/shard_map/ppermute | solution.py:34
  8.6 14.8 %collective-permute-start.4 = (bf16[160,1024]{1,0:T(8,128)(2,1)S(1)}, bf16[160,1024]{1,0:T(8,128)(2,1)S(1)}, u32[]{:S(2)}, u32[]{:S(2)}) collective-permute-start(bf16[160,1024]{1,0:T(8,128)(2,1)S(1)} %get-tuple-element.48), channel_id=1, source_target_pairs={{0,32},{1,33},{2,34},{3,35},{4,36},{5,37},{6,38},{7,39},{8,40},{9,... | collective-permute-start | bytes 983048 | tf_op jit(solution)/shard_map/ppermute | solution.py:34
  8.9 14.5 %collective-permute-start.5 = (bf16[160,1024]{1,0:T(8,128)(2,1)S(1)}, bf16[160,1024]{1,0:T(8,128)(2,1)S(1)}, u32[]{:S(2)}, u32[]{:S(2)}) collective-permute-start(bf16[160,1024]{1,0:T(8,128)(2,1)S(1)} %get-tuple-element.47), channel_id=1, source_target_pairs={{0,96},{1,97},{2,98},{3,99},{4,100},{5,101},{6,102},{7,103},{8,104... | collective-permute-start | bytes 983048 | tf_op jit(solution)/shard_map/ppermute | solution.py:34
  11.8 1.6 %copy-start = (bf16[1024,1024]{1,0:T(8,128)(2,1)S(1)}, bf16[1024,1024]{1,0:T(8,128)(2,1)}, u32[]{:S(2)}) copy-start(bf16[1024,1024]{1,0:T(8,128)(2,1)} %refs_10_.3) | copy-start | bytes 6291460
  13.4 4.0 %copy-start.1 = (bf16[1024,1024]{1,0:T(8,128)(2,1)S(1)}, bf16[1024,1024]{1,0:T(8,128)(2,1)}, u32[]{:S(2)}) copy-start(bf16[1024,1024]{1,0:T(8,128)(2,1)} %refs_10_.3) | copy-start | bytes 6291460
  16.0 0.8 copy-start.14
  16.8 24.6 %copy-start.3 = (bf16[320,1024]{1,0:T(8,128)(2,1)}, bf16[320,1024]{1,0:T(8,128)(2,1)S(1)}, u32[]{:S(2)}) copy-start(bf16[320,1024]{1,0:T(8,128)(2,1)S(1)} %get-tuple-element.57.refs_0_) | copy-start | bytes 1966084
  19.9 0.8 copy-start.15
  20.7 20.7 %copy-start.4 = (bf16[320,1024]{1,0:T(8,128)(2,1)}, bf16[320,1024]{1,0:T(8,128)(2,1)S(1)}, u32[]{:S(2)}) copy-start(bf16[320,1024]{1,0:T(8,128)(2,1)S(1)} %get-tuple-element.61.refs_4_.refs_1_) | copy-start | bytes 1966084
  23.4 9.8 %copy-start.6 = (bf16[320,1024]{1,0:T(8,128)(2,1)}, bf16[320,1024]{1,0:T(8,128)(2,1)S(1)}, u32[]{:S(2)}) copy-start(bf16[320,1024]{1,0:T(8,128)(2,1)S(1)} %collective-permute-done.3.refs_12_.refs_13_) | copy-start | bytes 1966084
  23.4 3.4 %collective-permute-start.6 = (bf16[320,1024]{1,0:T(8,128)(2,1)S(1)}, bf16[320,1024]{1,0:T(8,128)(2,1)S(1)}, u32[]{:S(2)}, u32[]{:S(2)}) collective-permute-start(bf16[320,1024]{1,0:T(8,128)(2,1)S(1)} %collective-permute-done.3.refs_12_.refs_13_), channel_id=1, source_target_pairs={{0,8},{1,9},{2,10},{3,11},{4,12},{5,13},{6,14},{7,15},{8,0},{9,1},... | collective-permute-start | bytes 1966088 | tf_op jit(solution)/shard_map/ppermute | solution.py:34
  23.5 11.3 %collective-permute-start.7 = (bf16[160,1024]{1,0:T(8,128)(2,1)S(1)}, bf16[160,1024]{1,0:T(8,128)(2,1)S(1)}, u32[]{:S(2)}, u32[]{:S(2)}) collective-permute-start(bf16[160,1024]{1,0:T(8,128)(2,1)S(1)} %collective-permute-done.refs_0_.refs_1_), channel_id=1, source_target_pairs={{0,32},{1,33},{2,34},{3,35},{4,36},{5,37},{6,38},{7,39},{8,40},{9,... | collective-permute-start | bytes 983048 | tf_op jit(solution)/shard_map/ppermute | solution.py:34
  24.9 9.9 %collective-permute-start.8 = (bf16[160,1024]{1,0:T(8,128)(2,1)S(1)}, bf16[160,1024]{1,0:T(8,128)(2,1)S(1)}, u32[]{:S(2)}, u32[]{:S(2)}) collective-permute-start(bf16[160,1024]{1,0:T(8,128)(2,1)S(1)} %collective-permute-done.1.refs_1_.refs_2_), channel_id=1, source_target_pairs={{0,96},{1,97},{2,98},{3,99},{4,100},{5,101},{6,102},{7,103},{8,104... | collective-permute-start | bytes 983048 | tf_op jit(solution)/shard_map/ppermute | solution.py:34
  33.2 8.1 %copy-start.16 = (bf16[320,640]{1,0:T(8,128)(2,1)}, bf16[320,640]{1,0:T(8,128)(2,1)S(1)}, u32[]{:S(2)}) copy-start(bf16[320,640]{1,0:T(8,128)(2,1)S(1)} %get-tuple-element.84.refs_6_) | copy-start | bytes 1228804
  33.2 8.2 %copy-start.7 = (bf16[320,1024]{1,0:T(8,128)(2,1)}, bf16[320,1024]{1,0:T(8,128)(2,1)S(1)}, u32[]{:S(2)}) copy-start(bf16[320,1024]{1,0:T(8,128)(2,1)S(1)} %get-tuple-element.75.refs_2_) | copy-start | bytes 1966084
  33.2 8.2 %copy-start.9 = (bf16[320,640]{1,0:T(8,128)(2,1)}, bf16[320,640]{1,0:T(8,128)(2,1)S(1)}, u32[]{:S(2)}) copy-start(bf16[320,640]{1,0:T(8,128)(2,1)S(1)} %get-tuple-element.77.refs_4_.refs_8_) | copy-start | bytes 1228804
  33.2 8.2 %copy-start.10 = (bf16[320,640]{1,0:T(8,128)(2,1)}, bf16[320,640]{1,0:T(8,128)(2,1)S(1)}, u32[]{:S(2)}) copy-start(bf16[320,640]{1,0:T(8,128)(2,1)S(1)} %get-tuple-element.78.refs_5_.refs_9_) | copy-start | bytes 1228804
  33.2 8.2 %copy-start.11 = (bf16[320,640]{1,0:T(8,128)(2,1)}, bf16[320,640]{1,0:T(8,128)(2,1)S(1)}, u32[]{:S(2)}) copy-start(bf16[320,640]{1,0:T(8,128)(2,1)S(1)} %get-tuple-element.79.refs_6_.refs_10_) | copy-start | bytes 1228804
  41.3 2.8 %copy-start.8 = (bf16[320,1024]{1,0:T(8,128)(2,1)}, bf16[320,1024]{1,0:T(8,128)(2,1)S(1)}, u32[]{:S(2)}) copy-start(bf16[320,1024]{1,0:T(8,128)(2,1)S(1)} %get-tuple-element.76.refs_3_) | copy-start | bytes 1966084
  41.3 2.8 %copy-start.12 = (bf16[320,640]{1,0:T(8,128)(2,1)}, bf16[320,640]{1,0:T(8,128)(2,1)S(1)}, u32[]{:S(2)}) copy-start(bf16[320,640]{1,0:T(8,128)(2,1)S(1)} %get-tuple-element.80.refs_7_.refs_11_) | copy-start | bytes 1228804
  41.3 2.8 %copy-start.17 = (bf16[320,640]{1,0:T(8,128)(2,1)}, bf16[320,640]{1,0:T(8,128)(2,1)S(1)}, u32[]{:S(2)}) copy-start(bf16[320,640]{1,0:T(8,128)(2,1)S(1)} %get-tuple-element.85.refs_7_) | copy-start | bytes 1228804
  41.3 2.8 %collective-permute-start.9 = (bf16[8,64,1024]{2,1,0:T(8,128)(2,1)S(1)}, bf16[8,64,1024]{2,1,0:T(8,128)(2,1)S(1)}, u32[]{:S(2)}, u32[]{:S(2)}) collective-permute-start(bf16[8,64,1024]{2,1,0:T(8,128)(2,1)S(1)} %get-tuple-element.74), channel_id=1, source_target_pairs={{0,8},{1,9},{2,10},{3,11},{4,12},{5,13},{6,14},{7,15},{8,0},{9,1},... | collective-permute-start | bytes 3145736 | tf_op jit(solution)/shard_map/ppermute | solution.py:34
  44.1 6.2 %collective-permute-start.14 = (f32[320,1024]{1,0:T(8,128)}, f32[320,1024]{1,0:T(8,128)S(1)}, u32[]{:S(2)}, u32[]{:S(2)}) collective-permute-start(f32[320,1024]{1,0:T(8,128)} %shard_map.54), channel_id=1, source_target_pairs={{0,8},{1,9},{2,10},{3,11},{4,12},{5,13},{6,14},{7,15},{8,0},{9,1},... | collective-permute-start | bytes 3932168 | tf_op jit(solution)/shard_map/ppermute | solution.py:34
  46.0 21.1 %all-to-all-start = ((bf16[8,64,1024]{2,1,0:T(8,128)(2,1)}), bf16[8,64,1024]{2,1,0:T(8,128)(2,1)}, u32[]{:S(2)}, u32[]{:S(2)}) async-start(bf16[8,64,1024]{2,1,0:T(8,128)(2,1)} %shard_map.55), calls=%async_computation | async-start | bytes 2097152 | tf_op jit(solution)/shard_map/all_to_all | solution.py:236
  50.2 1.1 %copy-start.18 = (f32[320,1024]{1,0:T(8,128)}, f32[320,1024]{1,0:T(8,128)S(1)}, u32[]{:S(2)}) copy-start(f32[320,1024]{1,0:T(8,128)S(1)} %collective-permute-done.14.refs_12_) | copy-start | bytes 3932164
  60.3 20.4 %copy-start.13 = (f32[320,1024]{1,0:T(8,128)S(1)}, f32[320,1024]{1,0:T(8,128)}, u32[]{:S(2)}) copy-start(f32[320,1024]{1,0:T(8,128)} %get-tuple-element.87.home) | copy-start | bytes 3932164
  60.3 20.4 %collective-permute-start.15 = (f32[320,1024]{1,0:T(8,128)}, f32[320,1024]{1,0:T(8,128)S(1)}, u32[]{:S(2)}, u32[]{:S(2)}) collective-permute-start(f32[320,1024]{1,0:T(8,128)} %get-tuple-element.88), channel_id=1, source_target_pairs={{0,8},{1,9},{2,10},{3,11},{4,12},{5,13},{6,14},{7,15},{8,0},{9,1},... | collective-permute-start | bytes 3932168 | tf_op jit(solution)/shard_map/ppermute | solution.py:34
  60.3 20.4 %collective-permute-start.16 = (bf16[320,1024]{1,0:T(8,128)(2,1)}, bf16[320,1024]{1,0:T(8,128)(2,1)}, u32[]{:S(2)}, u32[]{:S(2)}) collective-permute-start(bf16[320,1024]{1,0:T(8,128)(2,1)} %get-tuple-element.89), channel_id=1, source_target_pairs={{0,16},{1,17},{2,18},{3,19},{4,20},{5,21},{6,22},{7,23},{8,24},{9,... | collective-permute-start | bytes 1966088 | tf_op jit(solution)/shard_map/ppermute | solution.py:34
  68.4 8.3 %collective-permute-start.10 = (bf16[64,1024]{1,0:T(8,128)(2,1)S(1)}, bf16[64,1024]{1,0:T(8,128)(2,1)S(1)}, u32[]{:S(2)}, u32[]{:S(2)}) collective-permute-start(bf16[64,1024]{1,0:T(8,128)(2,1)S(1)} %reduce_sum.12), channel_id=1, source_target_pairs={{0,4},{1,5},{2,6},{3,7},{4,0},{5,1},{6,2},{7,3},{8,12},{9,13},{10,... | collective-permute-start | bytes 393224 | tf_op jit(solution)/shard_map/ppermute | solution.py:34
  72.4 6.3 %collective-permute-start.11 = (bf16[64,1024]{1,0:T(8,128)(2,1)S(1)}, bf16[64,1024]{1,0:T(8,128)(2,1)S(1)}, u32[]{:S(2)}, u32[]{:S(2)}) collective-permute-start(bf16[64,1024]{1,0:T(8,128)(2,1)S(1)} %reduce_sum.12), channel_id=1, source_target_pairs={{0,2},{1,3},{2,4},{3,5},{4,6},{5,7},{6,0},{7,1},{8,10},{9,11},{10,... | collective-permute-start | bytes 393224 | tf_op jit(solution)/shard_map/ppermute | solution.py:34
  73.4 5.4 %collective-permute-start.12 = (bf16[64,1024]{1,0:T(8,128)(2,1)S(1)}, bf16[64,1024]{1,0:T(8,128)(2,1)S(1)}, u32[]{:S(2)}, u32[]{:S(2)}) collective-permute-start(bf16[64,1024]{1,0:T(8,128)(2,1)S(1)} %reduce_sum.12), channel_id=1, source_target_pairs={{0,6},{1,7},{2,0},{3,1},{4,2},{5,3},{6,4},{7,5},{8,14},{9,15},{10,... | collective-permute-start | bytes 393224 | tf_op jit(solution)/shard_map/ppermute | solution.py:34
  78.8 5.0 %collective-permute-start.13 = (bf16[64,1024]{1,0:T(8,128)(2,1)S(1)}, bf16[64,1024]{1,0:T(8,128)(2,1)S(1)}, u32[]{:S(2)}, u32[]{:S(2)}) collective-permute-start(bf16[64,1024]{1,0:T(8,128)(2,1)S(1)} %add_convert_fusion), channel_id=1, source_target_pairs={{0,1},{1,0},{2,3},{3,2},{4,5},{5,4},{6,7},{7,6},{8,9},{9,8},{10,11... | collective-permute-start | bytes 393224 | tf_op jit(solution)/shard_map/ppermute | solution.py:34

commit v5 on v4

--- a/solution.py
+++ b/solution.py
@@ -55,8 +55,8 @@
 
 def text_units(first, second, out):
     rows = first.shape[0]
-    out[:rows] = normalize(first[...].astype(F32))[0].astype(BF16)
-    out[rows:] = normalize(second[...].astype(F32))[0].astype(BF16)
+    out[:rows] = normalize(first.astype(F32))[0].astype(BF16)
+    out[rows:] = normalize(second.astype(F32))[0].astype(BF16)
 
 
 def stacked(refs):
@@ -65,7 +65,7 @@
 
 
 def first_kernel(feats, proj_weight, text, text_c, *outs):
-    text_units(text, text_c, outs[0])
+    text_units(text[...], text_c[...], outs[0])
     early_kernel(1, True, feats, proj_weight, *outs)
 
 
@@ -92,30 +92,33 @@
     return unit, slopes_a, slopes_b, project(LOGIT_SCALE * grad, norm, length).astype(BF16)
 
 
-def middle_kernel(*refs):
-    own, near, (high, low, proj_weight, texts_a) = refs[:4], refs[4:8], refs[8:12]
-    (text_y, text_yc, texts_b), outs = refs[12:15], refs[15:]
-    text_units(text_y, text_yc, texts_b)
-    for k, (unit, norm, length, grad) in enumerate((own, near)):
-        slopes = slopes_of(unit[...], texts_b[...], False)
+def middle_kernel(count, *refs):
+    early, (text_y, *text_yc), (texts, *outs) = (
+        refs[: 4 * count], refs[4 * count : 4 * count + 3], refs[4 * count + 3 :]
+    )
+    text_units(text_y[...], stacked(text_yc), texts)
+    for k in range(count):
+        unit, norm, length, grad = early[4 * k : 4 * k + 4]
+        slopes = slopes_of(unit[...], texts[...], False)
         outs[2 * k][...] = slopes
-        total = grad[...] + jnp.dot(slopes, texts_b[...], preferred_element_type=F32)
+        total = grad[...] + jnp.dot(slopes, texts[...], preferred_element_type=F32)
         total = project(LOGIT_SCALE * total, norm[...], length[...])
         outs[2 * k + 1][...] = total.astype(BF16)
-    block = whole_block(stacked((high, low)), proj_weight, texts_a, texts_b)
-    for out, value in zip(outs[4:], block):
-        out[...] = value
 
 
 def late_kernel(*refs):
     core = lax.axis_index("c")
-    feats, grads, (proj_weight, texts_a, texts_b) = refs[:7], refs[7:10], refs[10:13]
-    unit_out, slopes_a, slopes_b, mine_out, other_out, weight = refs[13:]
+    feats, (low, high), grads = refs[:5], refs[5:7], refs[7:10]
+    (proj_weight, texts_a, texts_b), outs = refs[10:13], refs[13:]
+    unit_out, slopes_a, slopes_b, mine_out, other_out, weight = outs
+    half = unit_out.shape[0] // 2
+    far = jnp.concatenate([low[:half], high[high.shape[0] - half :]])
     unit_out[...], slopes_a[...], slopes_b[...], far_grad = whole_block(
-        stacked(feats[5:]), proj_weight, texts_a, texts_b
-    )
+        far, proj_weight, texts_a, texts_b
+    )
+    feats = jnp.concatenate([stacked(feats), far])
     grads = jnp.concatenate([stacked(grads), far_grad])
-    weight[...] = jnp.dot(stacked(feats).T, grads, preferred_element_type=F32)
+    weight[...] = jnp.dot(feats.T, grads, preferred_element_type=F32)
     slices, rows = mine_out.shape[0], mine_out.shape[1]
     for k in range(slices):
         start = 2 * k * rows
@@ -175,41 +178,53 @@
     rows, depth = sensor_feats.shape
     width = proj_weight.shape[1]
     half, texts = rows // 2, 2 * rows
-    unit_like, grad_like = ((rows, width), BF16), ((rows, width), F32)
-    slopes_like = ((rows, texts), BF16)
+    more, less = half + 16, half - 16
+
+    def early_like(rows):
+        return [
+            ((rows, width), BF16), ((rows, width), F32), ((rows, 1), F32),
+            ((rows, texts), BF16), ((rows, width), F32),
+        ]
+
+    def early(*feats):
+        return call(
+            functools.partial(early_kernel, 2, False),
+            early_like(sum(f.shape[0] for f in feats)), [*feats, proj_weight, texts_a], 18,
+        )
 
     low, high, text = lax.optimization_barrier(
-        (sensor_feats[:half], sensor_feats[half:], text_feats)
+        (sensor_feats[:more], sensor_feats[less:], text_feats)
     )
     text_c, text_y = send(text, c=1), send(text, yh=1)
     right_low, left_high = send(low, x=1), send(high, x=-1)
-    right_high, left_low = send(high, x=1), send(low, x=-1)
+    right_rest = send(sensor_feats[more:], x=1)
+    left_rest = send(sensor_feats[:less], x=-1)
 
     texts_like = ((texts, width), BF16)
-    early_like = [unit_like, grad_like, ((rows, 1), F32), slopes_like, grad_like]
+    unit_like, grad_like, _, slopes_like, _ = early_like(rows)
     texts_a, unit, norm, length, slopes_a, grad = call(
-        first_kernel, [texts_like, *early_like], [sensor_feats, proj_weight, text_feats, text_c], 18
+        first_kernel,
+        [texts_like, *early_like(rows)], [sensor_feats, proj_weight, text_feats, text_c], 18,
     )
     right_low, left_high, grad = lax.optimization_barrier((right_low, left_high, grad))
     far_low, far_high = send(right_low, x=1), send(left_high, x=-1)
-    near_unit, near_norm, near_length, near_a, near = call(
-        functools.partial(early_kernel, 2, False),
-        early_like, [right_low, left_high, proj_weight, texts_a], 16,
-    )
-    text_y, right_high, left_low, near = lax.optimization_barrier(
-        (text_y, right_high, left_low, near)
-    )
-    texts_b, slopes_b, raw_grad, near_b, near_grad, next_unit, next_a, next_b, next_grad = call(
-        middle_kernel,
-        [
-            texts_like, slopes_like, unit_like, slopes_like, unit_like,
-            unit_like, slopes_like, slopes_like, unit_like,
-        ],
-        [
-            unit, norm, length, grad, near_unit, near_norm, near_length, near,
-            right_high, left_low, proj_weight, texts_a, text_y, send(text_y, c=1),
-        ],
-        30,
+    near_unit, near_norm, near_length, near_a, near = early(right_low, left_high)
+    text_y, right_rest, left_rest, near = lax.optimization_barrier(
+        (text_y, right_rest, left_rest, near)
+    )
+    text_yc = [send(text_y[:half], c=1), send(text_y[half:], c=1)]
+    next_unit, next_norm, next_length, next_a, next_ = early(right_rest, left_rest)
+    groups = [
+        (unit, norm, length, grad),
+        (near_unit, near_norm, near_length, near),
+        (next_unit, next_norm, next_length, next_),
+    ]
+    outs = [[((g[0].shape[0], texts), BF16), ((g[0].shape[0], width), BF16)] for g in groups]
+    texts_b, slopes_b, raw_grad, near_b, near_grad, next_b, next_grad = call(
+        functools.partial(middle_kernel, 3),
+        [texts_like, *itertools.chain(*outs)],
+        [*itertools.chain(*groups), text_y, *text_yc],
+        32,
     )
     next_grad, far_low, far_high = lax.optimization_barrier((next_grad, far_low, far_high))
     share = (8, depth // 16, width)
@@ -217,8 +232,8 @@
         late_kernel,
         [unit_like, slopes_like, slopes_like, (share, F32), (share, BF16)],
         [
-            sensor_feats, right_low, left_high, right_high, left_low,
-            far_low, far_high, raw_grad, near_grad, next_grad, proj_weight, texts_a, texts_b,
+            sensor_feats, right_low, left_high, right_rest, left_rest, far_low, far_high,
+            raw_grad, near_grad, next_grad, proj_weight, texts_a, texts_b,
         ],
         30,
         scratch=[pltpu.VMEM((depth, width), F32)],

time: 85.5 us -> 83.5 us (0.977)
  waiting for transfers between devices: 12.5 us -> 9.62 us
  local copies, waits for them, and re-layouts: 5.56 us -> 7.03 us
    ppermute x17 -> x18, waiting for transfers between devices: 9.33 us -> 5.69 us  [send(): return lax.ppermute(block, AXES, route)]
    slice x1 -> x3, local copies, waits for them, and re-layouts: 1.22 us -> 2.42 us  [the longest x1 1.29 us: local(): sensor_feats[less:]]
    pallas_call x8 -> x9, Pallas kernels: 33.4 us -> 33.1 us  [call(): pl.pallas_call(kernel, out_shape=shapes, in_specs=[vmem] * len(operands),...]
    unnamed x38 -> x40, local copies, waits for them, and re-layouts: 4.34 us -> 4.61 us
    ppermute x17 -> x18, starting transfers between devices: 25.8 us -> 26 us  [send(): return lax.ppermute(block, AXES, route)]
  transfers between devices with their start and end apart: 18 -> 19, of which waited for: 10 -> 8; matrix products, arithmetic and copies ran while one was open for 2% -> 3% of each run, Pallas kernels for 32% -> 32%
where the time goes in v5:
time: 83.5 us; the launch traced here: 83.1 us
  Pallas kernels  33.1 us (40%)
  starting transfers between devices  30.2 us (36%)
  waiting for transfers between devices  9.62 us (12%)
  local copies, waits for them, and re-layouts  7.03 us (8%)
  other arithmetic  2.21 us (3%)
  between operations  0.95 us (1%)
    pallas_call x9, Pallas kernels, call(): pl.pallas_call(kernel, out_shape=shapes, in_specs=[vmem] * len(operands),...  33.1 us
    ppermute x18, starting transfers between devices, send(): return lax.ppermute(block, AXES, route)  26 us
    ppermute x18, waiting for transfers between devices, send(): return lax.ppermute(block, AXES, route)  5.69 us
    unnamed x40, local copies, waits for them, and re-layouts  4.61 us
    all_to_all x1, starting transfers between devices, local(): lax.all_to_all(weight_sum, ('x', 'yh'), split_axis=0, concat_axis=0, tile...  4.25 us
    all_to_all x1, waiting for transfers between devices, local(): lax.all_to_all(weight_sum, ('x', 'yh'), split_axis=0, concat_axis=0, tile...  3.93 us
  transfers between devices with their start and end apart: 19, of which 8 were waited for; matrix products, arithmetic and copies ran while one was open for 3% of the time, Pallas kernels for 32%

profile of v5, /device:TPU:0, one launch (start us, length us, event | category | flops | bytes accessed | tf_op | source)
XLA Modules:
  0.0 83.1 jit_solution(14326608181054674518)
XLA Ops:
  0.6 1.3 %fusion.2 = (bf16[176,1024]{1,0:T(8,128)(2,1)S(1)}, bf16[176,1024]{1,0:T(8,128)(2,1)S(1)}) fusion(bf16[320,1024]{1,0:T(8,128)(2,1)} %refs_0_.1), kind=kLoop, calls=%fused_computation.4 | loop fusion | bytes 1441792 | tf_op jit(solution)/shard_map/slice | solution.py:196
  1.9 0.1 collective-permute-start.2
  2.0 3.4 %collective-permute-start.3 = (bf16[320,1024]{1,0:T(8,128)(2,1)}, bf16[320,1024]{1,0:T(8,128)(2,1)S(1)}, u32[]{:S(2)}, u32[]{:S(2)}) collective-permute-start(bf16[320,1024]{1,0:T(8,128)(2,1)} %feats.3), channel_id=1, source_target_pairs={{0,16},{1,17},{2,18},{3,19},{4,20},{5,21},{6,22},{7,23},{8,24},{9,... | collective-permute-start | bytes 1966088 | tf_op jit(solution)/shard_map/ppermute | solution.py:34
  5.4 1.5 %collective-permute-start = (bf16[176,1024]{1,0:T(8,128)(2,1)S(1)}, bf16[176,1024]{1,0:T(8,128)(2,1)S(1)}, u32[]{:S(2)}, u32[]{:S(2)}) collective-permute-start(bf16[176,1024]{1,0:T(8,128)(2,1)S(1)} %get-tuple-element.50), channel_id=1, source_target_pairs={{0,32},{1,33},{2,34},{3,35},{4,36},{5,37},{6,38},{7,39},{8,40},{9,... | collective-permute-start | bytes 1081352 | tf_op jit(solution)/shard_map/ppermute | solution.py:34
  6.9 1.7 %collective-permute-start.1 = (bf16[176,1024]{1,0:T(8,128)(2,1)S(1)}, bf16[176,1024]{1,0:T(8,128)(2,1)S(1)}, u32[]{:S(2)}, u32[]{:S(2)}) collective-permute-start(bf16[176,1024]{1,0:T(8,128)(2,1)S(1)} %get-tuple-element.51), channel_id=1, source_target_pairs={{0,96},{1,97},{2,98},{3,99},{4,100},{5,101},{6,102},{7,103},{8,104... | collective-permute-start | bytes 1081352 | tf_op jit(solution)/shard_map/ppermute | solution.py:34
  8.6 1.1 %fusion.1 = (bf16[144,1024]{1,0:T(8,128)(2,1)S(1)}, bf16[144,1024]{1,0:T(8,128)(2,1)S(1)}) fusion(bf16[320,1024]{1,0:T(8,128)(2,1)} %refs_0_.1), kind=kLoop, calls=%fused_computation.3 | loop fusion | bytes 1179648 | tf_op jit(solution)/shard_map/slice | solution.py:201
  9.7 0.3 collective-permute-start.4
  10.1 3.0 %collective-permute-start.5 = (bf16[144,1024]{1,0:T(8,128)(2,1)S(1)}, bf16[144,1024]{1,0:T(8,128)(2,1)S(1)}, u32[]{:S(2)}, u32[]{:S(2)}) collective-permute-start(bf16[144,1024]{1,0:T(8,128)(2,1)S(1)} %get-tuple-element.100), channel_id=1, source_target_pairs={{0,96},{1,97},{2,98},{3,99},{4,100},{5,101},{6,102},{7,103},{8,104... | collective-permute-start | bytes 884744 | tf_op jit(solution)/shard_map/ppermute | solution.py:34
  13.0 1.1 %copy-done.1 = bf16[320,1024]{1,0:T(8,128)(2,1)S(1)} copy-done((bf16[320,1024]{1,0:T(8,128)(2,1)S(1)}, bf16[320,1024]{1,0:T(8,128)(2,1)}, u32[]{:S(2)}) %copy-start.1) | copy-done | bytes 655384
  14.1 1.1 %copy-done.7 = bf16[320,1024]{1,0:T(8,128)(2,1)S(1)} copy-done((bf16[320,1024]{1,0:T(8,128)(2,1)S(1)}, bf16[320,1024]{1,0:T(8,128)(2,1)}, u32[]{:S(2)}) %copy-start.7) | copy-done | bytes 655384
  15.2 2.6 %shard_map.50 = (bf16[640,1024]{1,0:T(8,128)(2,1)S(1)}, bf16[320,1024]{1,0:T(8,128)(2,1)S(1)}, f32[320,1024]{1,0:T(8,128)S(1)}, f32[320,1]{1,0:T(8,128)S(1)}, bf...) custom-call(bf16[320,1024]{1,0:T(8,128)(2,1)S(1)} %copy-done.1, bf16[1024,1024]{1,0:T(8,128)(2,1)S(1)} %copy-done, ...), custom_call_target="tpu_custom_call" | custom-call | flops 1 | bytes 1 | tf_op jit(solution)/shard_map/pallas_call | solution.py:166
  17.8 0.0 collective-permute-done.refs_0_.refs_1_
  17.9 0.3 collective-permute-done.1.refs_1_.refs_2_
  18.2 1.5 %collective-permute-start.8 = (bf16[176,1024]{1,0:T(8,128)(2,1)S(1)}, bf16[176,1024]{1,0:T(8,128)(2,1)S(1)}, u32[]{:S(2)}, u32[]{:S(2)}) collective-permute-start(bf16[176,1024]{1,0:T(8,128)(2,1)S(1)} %collective-permute-done.refs_0_.refs_1_), channel_id=1, source_target_pairs={{0,32},{1,33},{2,34},{3,35},{4,36},{5,37},{6,38},{7,39},{8,40},{9,... | collective-permute-start | bytes 1081352 | tf_op jit(solution)/shard_map/ppermute | solution.py:34
  19.7 1.7 %collective-permute-start.9 = (bf16[176,1024]{1,0:T(8,128)(2,1)S(1)}, bf16[176,1024]{1,0:T(8,128)(2,1)S(1)}, u32[]{:S(2)}, u32[]{:S(2)}) collective-permute-start(bf16[176,1024]{1,0:T(8,128)(2,1)S(1)} %collective-permute-done.1.refs_1_.refs_2_), channel_id=1, source_target_pairs={{0,96},{1,97},{2,98},{3,99},{4,100},{5,101},{6,102},{7,103},{8,104... | collective-permute-start | bytes 1081352 | tf_op jit(solution)/shard_map/ppermute | solution.py:34
  21.4 2.7 %shard_map.51 = (bf16[352,1024]{1,0:T(8,128)(2,1)S(1)}, f32[352,1024]{1,0:T(8,128)S(1)}, f32[352,1]{1,0:T(8,128)S(1)}, bf16[352,640]{1,0:T(8,128)(2,1)S(1)}, f32[352,1024]{1,0:T(8,128)S(1)}) custom-call(bf16[176,1024]{1,0:T(8,128)(2,1)S(1)} %collective-permute-done.refs_0_.refs_1_, bf16[176,1024]{1,0:T(8,128)(2,1)S(1)} %collective-permute-done.1.refs_1_.refs_2_, ...), custom_call_target="tpu_custom_call" | custom-call | flops 1 | bytes 1 | tf_op jit(solution)/shard_map/pallas_call | solution.py:166
  24.2 0.0 collective-permute-done.4.refs_0_.refs_3_
  24.2 0.3 collective-permute-done.5.refs_1_.refs_4_
  24.5 0.1 collective-permute-start.6
  24.6 0.5 collective-permute-start.7
  25.1 2.3 %shard_map.52 = (bf16[288,1024]{1,0:T(8,128)(2,1)S(1)}, f32[288,1024]{1,0:T(8,128)S(1)}, f32[288,1]{1,0:T(8,128)S(1)}, bf16[288,640]{1,0:T(8,128)(2,1)S(1)}, f32[288,1024]{1,0:T(8,128)S(1)}) custom-call(bf16[144,1024]{1,0:T(8,128)(2,1)S(1)} %collective-permute-done.4.refs_0_.refs_3_, bf16[144,1024]{1,0:T(8,128)(2,1)S(1)} %collective-permute-done.5.refs_1_.refs_4_, ...), custom_call_target="tpu_custom_call" | custom-call | flops 1 | bytes 1 | tf_op jit(solution)/shard_map/pallas_call | solution.py:166
  27.5 0.0 copy-start.2
  27.5 4.6 %shard_map.53 = (bf16[640,1024]{1,0:T(8,128)(2,1)S(1)}, bf16[320,640]{1,0:T(8,128)(2,1)S(1)}, bf16[320,1024]{1,0:T(8,128)(2,1)S(1)}, bf16[352,640]{1,0:T(8,128)(...) custom-call(bf16[320,1024]{1,0:T(8,128)(2,1)S(1)} %get-tuple-element.60.refs_0_, ...), custom_call_target="tpu_custom_call" | custom-call | flops 1 | bytes 1 | tf_op jit(solution)/shard_map/pallas_call | solution.py:166
  32.2 6.5 %shard_map.54 = (bf16[320,1024]{1,0:T(8,128)(2,1)S(1)}, bf16[320,640]{1,0:T(8,128)(2,1)S(1)}, bf16[320,640]{1,0:T(8,128)(2,1)S(1)}, f32[8,64,1024]{2,1,0:T(8,128)S(1)}, bf16[8,64,1024]{2,1,0:T(8,128)(2,1)S(1)}) custom-call(bf16[320,1024]{1,0:T(8,128)(2,1)S(1)} %copy-done.2, bf16[176,1024]{1,0:T(8,128)(2,1)S(1)} %collective-permute-done.refs_0_.refs_1_, ...), custom_call_target="tpu_custom_call" | custom-call | flops 1 | bytes 1 | tf_op jit(solution)/shard_map/pallas_call | solution.py:166
  38.7 0.6 collective-permute-start.10
  39.4 2.6 %shard_map.55 = f32[320,1024]{1,0:T(8,128)} custom-call(bf16[320,1024]{1,0:T(8,128)(2,1)S(1)} %get-tuple-element.60.refs_0_, bf16[352,1024]{1,0:T(8,128)(2,1)S(1)} %get-tuple-element.64.refs_4_.refs_1_, bf16[288,1024]{1,0:T(8,128)(2,1)S(1)} %get-tuple-element.68.refs_8_.refs_2_, bf16[320,1024]{1,0:T(8,128)(2,1)S(1)} %get-tuple-element.82.refs_3_, ...), custom_call_target="tpu_custom_call" | custom-call | flops 1 | bytes 1 | tf_op jit(solution)/shard_map/pallas_call | solution.py:166
  42.0 0.3 collective-permute-start.15
  42.3 1.1 %shard_map.56 = bf16[8,64,1024]{2,1,0:T(8,128)(2,1)} custom-call(f32[8,64,1024]{2,1,0:T(8,128)S(1)} %get-tuple-element.80.mine, bf16[8,64,1024]{2,1,0:T(8,128)(2,1)S(1)} %collective-permute-done.10.received), custom_call_target="tpu_custom_call" | custom-call | flops 1 | bytes 1 | tf_op jit(solution)/shard_map/pallas_call | solution.py:166
  43.4 4.3 %all-to-all-start = ((bf16[8,64,1024]{2,1,0:T(8,128)(2,1)}), bf16[8,64,1024]{2,1,0:T(8,128)(2,1)}, u32[]{:S(2)}, u32[]{:S(2)}) async-start(bf16[8,64,1024]{2,1,0:T(8,128)(2,1)} %shard_map.56), calls=%async_computation | async-start | bytes 2097152 | tf_op jit(solution)/shard_map/all_to_all | solution.py:251
  47.7 1.0 %copy-done.19 = f32[320,1024]{1,0:T(8,128)} copy-done((f32[320,1024]{1,0:T(8,128)}, f32[320,1024]{1,0:T(8,128)S(1)}, u32[]{:S(2)}) %copy-start.19) | copy-done | bytes 1310744
  48.7 9.0 %shard_map.57 = (bf16[320,1024]{1,0:T(8,128)(2,1)}, f32[320,1024]{1,0:T(8,128)}, f32[320,1024]{1,0:T(8,128)}) custom-call(bf16[320,1024]{1,0:T(8,128)(2,1)} %copy-done.5, bf16[352,1024]{1,0:T(8,128)(2,1)} %copy-done.3, bf16[288,1024]{1,0:T(8,128)(2,1)} %copy-done.6, bf16[320,1024]{1,0:T(8,128)(2,1)} %copy-done.9, bf16[320,640]{1,0:T(8,128)(2,1)} %copy-done.16, ...), custom_call_target="tpu_custom_call" | custom-call | flops 1 | bytes 1 | tf_op jit(solution)/shard_map/pallas_call | solution.py:166
  57.8 0.3 collective-permute-start.16
  58.1 3.2 %collective-permute-start.17 = (bf16[320,1024]{1,0:T(8,128)(2,1)}, bf16[320,1024]{1,0:T(8,128)(2,1)S(1)}, u32[]{:S(2)}, u32[]{:S(2)}) collective-permute-start(bf16[320,1024]{1,0:T(8,128)(2,1)} %get-tuple-element.95), channel_id=1, source_target_pairs={{0,16},{1,17},{2,18},{3,19},{4,20},{5,21},{6,22},{7,23},{8,24},{9,... | collective-permute-start | bytes 1966088 | tf_op jit(solution)/shard_map/ppermute | solution.py:34
  61.3 3.9 %all-to-all-done = bf16[8,64,1024]{2,1,0:T(8,128)(2,1)} async-done(((bf16[8,64,1024]{2,1,0:T(8,128)(2,1)}), bf16[8,64,1024]{2,1,0:T(8,128)(2,1)}, u32[]{:S(2)}, u32[]{:S(2)}) %all-to-all-start) | async-done | bytes 1048608 | tf_op jit(solution)/shard_map/all_to_all | solution.py:251
  65.2 1.4 %reduce_sum.12 = bf16[64,1024]{1,0:T(8,128)(2,1)S(1)} reduce(bf16[8,64,1024]{2,1,0:T(8,128)(2,1)} %all-to-all-done, bf16[]{:T(256)} %constant.2.clone.1), dimensions={0}, to_apply=%region_0.0 | reduce | flops 458752 | bytes 1179650 | tf_op jit(solution)/shard_map/reduce_sum | solution.py:262
  66.7 3.9 %collective-permute-start.11 = (bf16[64,1024]{1,0:T(8,128)(2,1)S(1)}, bf16[64,1024]{1,0:T(8,128)(2,1)S(1)}, u32[]{:S(2)}, u32[]{:S(2)}) collective-permute-start(bf16[64,1024]{1,0:T(8,128)(2,1)S(1)} %reduce_sum.12), channel_id=1, source_target_pairs={{0,4},{1,5},{2,6},{3,7},{4,0},{5,1},{6,2},{7,3},{8,12},{9,13},{10,... | collective-permute-start | bytes 393224 | tf_op jit(solution)/shard_map/ppermute | solution.py:34
  70.6 1.0 %collective-permute-start.12 = (bf16[64,1024]{1,0:T(8,128)(2,1)S(1)}, bf16[64,1024]{1,0:T(8,128)(2,1)S(1)}, u32[]{:S(2)}, u32[]{:S(2)}) collective-permute-start(bf16[64,1024]{1,0:T(8,128)(2,1)S(1)} %reduce_sum.12), channel_id=1, source_target_pairs={{0,2},{1,3},{2,4},{3,5},{4,6},{5,7},{6,0},{7,1},{8,10},{9,11},{10,... | collective-permute-start | bytes 393224 | tf_op jit(solution)/shard_map/ppermute | solution.py:34
  71.6 2.2 %collective-permute-start.13 = (bf16[64,1024]{1,0:T(8,128)(2,1)S(1)}, bf16[64,1024]{1,0:T(8,128)(2,1)S(1)}, u32[]{:S(2)}, u32[]{:S(2)}) collective-permute-start(bf16[64,1024]{1,0:T(8,128)(2,1)S(1)} %reduce_sum.12), channel_id=1, source_target_pairs={{0,6},{1,7},{2,0},{3,1},{4,2},{5,3},{6,4},{7,5},{8,14},{9,15},{10,... | collective-permute-start | bytes 393224 | tf_op jit(solution)/shard_map/ppermute | solution.py:34
  73.8 1.1 %collective-permute-done.11 = bf16[64,1024]{1,0:T(8,128)(2,1)S(1)} collective-permute-done((bf16[64,1024]{1,0:T(8,128)(2,1)S(1)}, bf16[64,1024]{1,0:T(8,128)(2,1)S(1)}, u32[]{:S(2)}, u32[]{:S(2)}) %collective-permute-start.11) | collective-permute-done | bytes 131104 | tf_op jit(solution)/shard_map/ppermute | solution.py:34
  74.9 2.1 %collective-permute-done.12 = bf16[64,1024]{1,0:T(8,128)(2,1)S(1)} collective-permute-done((bf16[64,1024]{1,0:T(8,128)(2,1)S(1)}, bf16[64,1024]{1,0:T(8,128)(2,1)S(1)}, u32[]{:S(2)}, u32[]{:S(2)}) %collective-permute-start.12) | collective-permute-done | bytes 131104 | tf_op jit(solution)/shard_map/ppermute | solution.py:34
  77.0 0.3 collective-permute-done.13
  77.3 0.1 add_convert_fusion
  77.4 0.6 collective-permute-start.14
  77.9 0.5 collective-permute-done.17.rest
  78.4 1.3 %copy-done.14 = f32[320,1024]{1,0:T(8,128)S(1)} copy-done((f32[320,1024]{1,0:T(8,128)S(1)}, f32[320,1024]{1,0:T(8,128)}, u32[]{:S(2)}) %copy-start.14) | copy-done | bytes 1310744
  79.7 1.7 %shard_map.58 = f32[320,1024]{1,0:T(8,128)} custom-call(f32[320,1024]{1,0:T(8,128)S(1)} %copy-done.14, f32[320,1024]{1,0:T(8,128)S(1)} %collective-permute-done.16.received, bf16[320,1024]{1,0:T(8,128)(2,1)S(1)} %collective-permute-done.17.rest, bf16[320,1024]{1,0:T(8,128)(2,1)S(1)} %copy-done.8), custom_call_target="tpu_custom_call" | custom-call | flops 1 | bytes 1 | tf_op jit(solution)/shard_map/pallas_call | solution.py:166
  81.4 1.0 %collective-permute-done.14 = bf16[64,1024]{1,0:T(8,128)(2,1)S(1)} collective-permute-done((bf16[64,1024]{1,0:T(8,128)(2,1)S(1)}, bf16[64,1024]{1,0:T(8,128)(2,1)S(1)}, u32[]{:S(2)}, u32[]{:S(2)}) %collective-permute-start.14) | collective-permute-done | bytes 131104 | tf_op jit(solution)/shard_map/ppermute | solution.py:34
  82.4 0.7 convert_add_fusion
  (45 shorter events, 0.1 us)
Async XLA Ops:
  0.6 12.4 %copy-start = (bf16[1024,1024]{1,0:T(8,128)(2,1)S(1)}, bf16[1024,1024]{1,0:T(8,128)(2,1)}, u32[]{:S(2)}) copy-start(bf16[1024,1024]{1,0:T(8,128)(2,1)} %refs_10_.1) | copy-start | bytes 6291460
  1.9 8.1 %collective-permute-start.2 = (bf16[320,1024]{1,0:T(8,128)(2,1)}, bf16[320,1024]{1,0:T(8,128)(2,1)S(1)}, u32[]{:S(2)}, u32[]{:S(2)}) collective-permute-start(bf16[320,1024]{1,0:T(8,128)(2,1)} %feats.3), channel_id=1, source_target_pairs={{0,8},{1,9},{2,10},{3,11},{4,12},{5,13},{6,14},{7,15},{8,0},{9,1},... | collective-permute-start | bytes 1966088 | tf_op jit(solution)/shard_map/ppermute | solution.py:34
  2.0 22.5 %collective-permute-start.3 = (bf16[320,1024]{1,0:T(8,128)(2,1)}, bf16[320,1024]{1,0:T(8,128)(2,1)S(1)}, u32[]{:S(2)}, u32[]{:S(2)}) collective-permute-start(bf16[320,1024]{1,0:T(8,128)(2,1)} %feats.3), channel_id=1, source_target_pairs={{0,16},{1,17},{2,18},{3,19},{4,20},{5,21},{6,22},{7,23},{8,24},{9,... | collective-permute-start | bytes 1966088 | tf_op jit(solution)/shard_map/ppermute | solution.py:34
  5.4 12.5 %collective-permute-start = (bf16[176,1024]{1,0:T(8,128)(2,1)S(1)}, bf16[176,1024]{1,0:T(8,128)(2,1)S(1)}, u32[]{:S(2)}, u32[]{:S(2)}) collective-permute-start(bf16[176,1024]{1,0:T(8,128)(2,1)S(1)} %get-tuple-element.50), channel_id=1, source_target_pairs={{0,32},{1,33},{2,34},{3,35},{4,36},{5,37},{6,38},{7,39},{8,40},{9,... | collective-permute-start | bytes 1081352 | tf_op jit(solution)/shard_map/ppermute | solution.py:34
  6.9 11.3 %collective-permute-start.1 = (bf16[176,1024]{1,0:T(8,128)(2,1)S(1)}, bf16[176,1024]{1,0:T(8,128)(2,1)S(1)}, u32[]{:S(2)}, u32[]{:S(2)}) collective-permute-start(bf16[176,1024]{1,0:T(8,128)(2,1)S(1)} %get-tuple-element.51), channel_id=1, source_target_pairs={{0,96},{1,97},{2,98},{3,99},{4,100},{5,101},{6,102},{7,103},{8,104... | collective-permute-start | bytes 1081352 | tf_op jit(solution)/shard_map/ppermute | solution.py:34
  9.7 14.5 %collective-permute-start.4 = (bf16[144,1024]{1,0:T(8,128)(2,1)S(1)}, bf16[144,1024]{1,0:T(8,128)(2,1)S(1)}, u32[]{:S(2)}, u32[]{:S(2)}) collective-permute-start(bf16[144,1024]{1,0:T(8,128)(2,1)S(1)} %get-tuple-element.101), channel_id=1, source_target_pairs={{0,32},{1,33},{2,34},{3,35},{4,36},{5,37},{6,38},{7,39},{8,40},{9,... | collective-permute-start | bytes 884744 | tf_op jit(solution)/shard_map/ppermute | solution.py:34
  10.1 14.4 %collective-permute-start.5 = (bf16[144,1024]{1,0:T(8,128)(2,1)S(1)}, bf16[144,1024]{1,0:T(8,128)(2,1)S(1)}, u32[]{:S(2)}, u32[]{:S(2)}) collective-permute-start(bf16[144,1024]{1,0:T(8,128)(2,1)S(1)} %get-tuple-element.100), channel_id=1, source_target_pairs={{0,96},{1,97},{2,98},{3,99},{4,100},{5,101},{6,102},{7,103},{8,104... | collective-permute-start | bytes 884744 | tf_op jit(solution)/shard_map/ppermute | solution.py:34
  13.0 1.1 %copy-start.1 = (bf16[320,1024]{1,0:T(8,128)(2,1)S(1)}, bf16[320,1024]{1,0:T(8,128)(2,1)}, u32[]{:S(2)}) copy-start(bf16[320,1024]{1,0:T(8,128)(2,1)} %refs_0_.1) | copy-start | bytes 1966084
  14.1 1.1 %copy-start.7 = (bf16[320,1024]{1,0:T(8,128)(2,1)S(1)}, bf16[320,1024]{1,0:T(8,128)(2,1)}, u32[]{:S(2)}) copy-start(bf16[320,1024]{1,0:T(8,128)(2,1)} %feats.3) | copy-start | bytes 1966084
  17.8 6.3 %copy-start.16 = (bf16[320,640]{1,0:T(8,128)(2,1)}, bf16[320,640]{1,0:T(8,128)(2,1)S(1)}, u32[]{:S(2)}) copy-start(bf16[320,640]{1,0:T(8,128)(2,1)S(1)} %get-tuple-element.88.refs_4_) | copy-start | bytes 1228804
  17.8 21.5 %copy-start.5 = (bf16[320,1024]{1,0:T(8,128)(2,1)}, bf16[320,1024]{1,0:T(8,128)(2,1)S(1)}, u32[]{:S(2)}) copy-start(bf16[320,1024]{1,0:T(8,128)(2,1)S(1)} %get-tuple-element.60.refs_0_) | copy-start | bytes 1966084
  18.2 14.0 %collective-permute-start.8 = (bf16[176,1024]{1,0:T(8,128)(2,1)S(1)}, bf16[176,1024]{1,0:T(8,128)(2,1)S(1)}, u32[]{:S(2)}, u32[]{:S(2)}) collective-permute-start(bf16[176,1024]{1,0:T(8,128)(2,1)S(1)} %collective-permute-done.refs_0_.refs_1_), channel_id=1, source_target_pairs={{0,32},{1,33},{2,34},{3,35},{4,36},{5,37},{6,38},{7,39},{8,40},{9,... | collective-permute-start | bytes 1081352 | tf_op jit(solution)/shard_map/ppermute | solution.py:34
  19.7 12.5 %collective-permute-start.9 = (bf16[176,1024]{1,0:T(8,128)(2,1)S(1)}, bf16[176,1024]{1,0:T(8,128)(2,1)S(1)}, u32[]{:S(2)}, u32[]{:S(2)}) collective-permute-start(bf16[176,1024]{1,0:T(8,128)(2,1)S(1)} %collective-permute-done.1.refs_1_.refs_2_), channel_id=1, source_target_pairs={{0,96},{1,97},{2,98},{3,99},{4,100},{5,101},{6,102},{7,103},{8,104... | collective-permute-start | bytes 1081352 | tf_op jit(solution)/shard_map/ppermute | solution.py:34
  24.1 3.3 %copy-start.15 = (bf16[352,640]{1,0:T(8,128)(2,1)}, bf16[352,640]{1,0:T(8,128)(2,1)S(1)}, u32[]{:S(2)}) copy-start(bf16[352,640]{1,0:T(8,128)(2,1)S(1)} %get-tuple-element.89.refs_5_) | copy-start | bytes 1351684
  24.1 15.2 %copy-start.3 = (bf16[352,1024]{1,0:T(8,128)(2,1)}, bf16[352,1024]{1,0:T(8,128)(2,1)S(1)}, u32[]{:S(2)}) copy-start(bf16[352,1024]{1,0:T(8,128)(2,1)S(1)} %get-tuple-element.64.refs_4_.refs_1_) | copy-start | bytes 2162692
  24.5 3.0 %copy-start.4 = (bf16[320,1024]{1,0:T(8,128)(2,1)}, bf16[320,1024]{1,0:T(8,128)(2,1)S(1)}, u32[]{:S(2)}) copy-start(bf16[320,1024]{1,0:T(8,128)(2,1)S(1)} %collective-permute-done.3.refs_12_.refs_13_) | copy-start | bytes 1966084
  24.5 2.9 %collective-permute-start.6 = (bf16[160,1024]{1,0:T(8,128)(2,1)S(1)}, bf16[160,1024]{1,0:T(8,128)(2,1)S(1)}, u32[]{:S(2)}, u32[]{:S(2)}) collective-permute-start(bf16[160,1024]{1,0:T(8,128)(2,1)S(1)} %get-tuple-element.99), channel_id=1, source_target_pairs={{0,8},{1,9},{2,10},{3,11},{4,12},{5,13},{6,14},{7,15},{8,0},{9,1},... | collective-permute-start | bytes 983048 | tf_op jit(solution)/shard_map/ppermute | solution.py:34
  24.6 2.9 %collective-permute-start.7 = (bf16[160,1024]{1,0:T(8,128)(2,1)S(1)}, bf16[160,1024]{1,0:T(8,128)(2,1)S(1)}, u32[]{:S(2)}, u32[]{:S(2)}) collective-permute-start(bf16[160,1024]{1,0:T(8,128)(2,1)S(1)} %get-tuple-element.98), channel_id=1, source_target_pairs={{0,8},{1,9},{2,10},{3,11},{4,12},{5,13},{6,14},{7,15},{8,0},{9,1},... | collective-permute-start | bytes 983048 | tf_op jit(solution)/shard_map/ppermute | solution.py:34
  27.5 4.7 %copy-start.18 = (bf16[288,640]{1,0:T(8,128)(2,1)}, bf16[288,640]{1,0:T(8,128)(2,1)S(1)}, u32[]{:S(2)}) copy-start(bf16[288,640]{1,0:T(8,128)(2,1)S(1)} %get-tuple-element.90.refs_6_) | copy-start | bytes 1105924
  27.5 11.9 %copy-start.6 = (bf16[288,1024]{1,0:T(8,128)(2,1)}, bf16[288,1024]{1,0:T(8,128)(2,1)S(1)}, u32[]{:S(2)}) copy-start(bf16[288,1024]{1,0:T(8,128)(2,1)S(1)} %get-tuple-element.68.refs_8_.refs_2_) | copy-start | bytes 1769476
  27.5 4.7 %copy-start.2 = (bf16[320,1024]{1,0:T(8,128)(2,1)S(1)}, bf16[320,1024]{1,0:T(8,128)(2,1)}, u32[]{:S(2)}) copy-start(bf16[320,1024]{1,0:T(8,128)(2,1)} %refs_0_.1) | copy-start | bytes 1966084
  32.1 7.2 %copy-start.10 = (bf16[352,640]{1,0:T(8,128)(2,1)}, bf16[352,640]{1,0:T(8,128)(2,1)S(1)}, u32[]{:S(2)}) copy-start(bf16[352,640]{1,0:T(8,128)(2,1)S(1)} %get-tuple-element.84.refs_5_.refs_9_) | copy-start | bytes 1351684
  32.2 7.2 %copy-start.11 = (bf16[320,640]{1,0:T(8,128)(2,1)}, bf16[320,640]{1,0:T(8,128)(2,1)S(1)}, u32[]{:S(2)}) copy-start(bf16[320,640]{1,0:T(8,128)(2,1)S(1)} %get-tuple-element.83.refs_4_.refs_8_) | copy-start | bytes 1228804
  32.2 7.2 %copy-start.13 = (bf16[288,640]{1,0:T(8,128)(2,1)}, bf16[288,640]{1,0:T(8,128)(2,1)S(1)}, u32[]{:S(2)}) copy-start(bf16[288,640]{1,0:T(8,128)(2,1)S(1)} %get-tuple-element.85.refs_6_.refs_10_) | copy-start | bytes 1105924
  38.7 3.3 %copy-start.9 = (bf16[320,1024]{1,0:T(8,128)(2,1)}, bf16[320,1024]{1,0:T(8,128)(2,1)S(1)}, u32[]{:S(2)}) copy-start(bf16[320,1024]{1,0:T(8,128)(2,1)S(1)} %get-tuple-element.82.refs_3_) | copy-start | bytes 1966084
  38.7 3.3 %copy-start.12 = (bf16[320,640]{1,0:T(8,128)(2,1)}, bf16[320,640]{1,0:T(8,128)(2,1)S(1)}, u32[]{:S(2)}) copy-start(bf16[320,640]{1,0:T(8,128)(2,1)S(1)} %get-tuple-element.86.refs_7_.refs_11_) | copy-start | bytes 1228804
  38.7 3.3 %copy-start.17 = (bf16[320,640]{1,0:T(8,128)(2,1)}, bf16[320,640]{1,0:T(8,128)(2,1)S(1)}, u32[]{:S(2)}) copy-start(bf16[320,640]{1,0:T(8,128)(2,1)S(1)} %get-tuple-element.91.refs_7_) | copy-start | bytes 1228804
  38.7 3.3 %collective-permute-start.10 = (bf16[8,64,1024]{2,1,0:T(8,128)(2,1)S(1)}, bf16[8,64,1024]{2,1,0:T(8,128)(2,1)S(1)}, u32[]{:S(2)}, u32[]{:S(2)}) collective-permute-start(bf16[8,64,1024]{2,1,0:T(8,128)(2,1)S(1)} %get-tuple-element.81), channel_id=1, source_target_pairs={{0,8},{1,9},{2,10},{3,11},{4,12},{5,13},{6,14},{7,15},{8,0},{9,1},... | collective-permute-start | bytes 3145736 | tf_op jit(solution)/shard_map/ppermute | solution.py:34
  42.0 5.7 %collective-permute-start.15 = (f32[320,1024]{1,0:T(8,128)}, f32[320,1024]{1,0:T(8,128)S(1)}, u32[]{:S(2)}, u32[]{:S(2)}) collective-permute-start(f32[320,1024]{1,0:T(8,128)} %shard_map.55), channel_id=1, source_target_pairs={{0,8},{1,9},{2,10},{3,11},{4,12},{5,13},{6,14},{7,15},{8,0},{9,1},... | collective-permute-start | bytes 3932168 | tf_op jit(solution)/shard_map/ppermute | solution.py:34
  43.4 21.8 %all-to-all-start = ((bf16[8,64,1024]{2,1,0:T(8,128)(2,1)}), bf16[8,64,1024]{2,1,0:T(8,128)(2,1)}, u32[]{:S(2)}, u32[]{:S(2)}) async-start(bf16[8,64,1024]{2,1,0:T(8,128)(2,1)} %shard_map.56), calls=%async_computation | async-start | bytes 2097152 | tf_op jit(solution)/shard_map/all_to_all | solution.py:251
  47.7 1.1 %copy-start.19 = (f32[320,1024]{1,0:T(8,128)}, f32[320,1024]{1,0:T(8,128)S(1)}, u32[]{:S(2)}) copy-start(f32[320,1024]{1,0:T(8,128)S(1)} %collective-permute-done.15.refs_12_) | copy-start | bytes 3932164
  57.8 20.6 %copy-start.8 = (bf16[320,1024]{1,0:T(8,128)(2,1)S(1)}, bf16[320,1024]{1,0:T(8,128)(2,1)}, u32[]{:S(2)}) copy-start(bf16[320,1024]{1,0:T(8,128)(2,1)} %feats.3) | copy-start | bytes 1966084
  57.8 20.6 %collective-permute-start.16 = (f32[320,1024]{1,0:T(8,128)}, f32[320,1024]{1,0:T(8,128)S(1)}, u32[]{:S(2)}, u32[]{:S(2)}) collective-permute-start(f32[320,1024]{1,0:T(8,128)} %get-tuple-element.94), channel_id=1, source_target_pairs={{0,8},{1,9},{2,10},{3,11},{4,12},{5,13},{6,14},{7,15},{8,0},{9,1},... | collective-permute-start | bytes 3932168 | tf_op jit(solution)/shard_map/ppermute | solution.py:34
  58.1 20.3 %collective-permute-start.17 = (bf16[320,1024]{1,0:T(8,128)(2,1)}, bf16[320,1024]{1,0:T(8,128)(2,1)S(1)}, u32[]{:S(2)}, u32[]{:S(2)}) collective-permute-start(bf16[320,1024]{1,0:T(8,128)(2,1)} %get-tuple-element.95), channel_id=1, source_target_pairs={{0,16},{1,17},{2,18},{3,19},{4,20},{5,21},{6,22},{7,23},{8,24},{9,... | collective-permute-start | bytes 1966088 | tf_op jit(solution)/shard_map/ppermute | solution.py:34
  66.7 8.3 %collective-permute-start.11 = (bf16[64,1024]{1,0:T(8,128)(2,1)S(1)}, bf16[64,1024]{1,0:T(8,128)(2,1)S(1)}, u32[]{:S(2)}, u32[]{:S(2)}) collective-permute-start(bf16[64,1024]{1,0:T(8,128)(2,1)S(1)} %reduce_sum.12), channel_id=1, source_target_pairs={{0,4},{1,5},{2,6},{3,7},{4,0},{5,1},{6,2},{7,3},{8,12},{9,13},{10,... | collective-permute-start | bytes 393224 | tf_op jit(solution)/shard_map/ppermute | solution.py:34
  70.6 6.5 %collective-permute-start.12 = (bf16[64,1024]{1,0:T(8,128)(2,1)S(1)}, bf16[64,1024]{1,0:T(8,128)(2,1)S(1)}, u32[]{:S(2)}, u32[]{:S(2)}) collective-permute-start(bf16[64,1024]{1,0:T(8,128)(2,1)S(1)} %reduce_sum.12), channel_id=1, source_target_pairs={{0,2},{1,3},{2,4},{3,5},{4,6},{5,7},{6,0},{7,1},{8,10},{9,11},{10,... | collective-permute-start | bytes 393224 | tf_op jit(solution)/shard_map/ppermute | solution.py:34
  71.6 5.7 %collective-permute-start.13 = (bf16[64,1024]{1,0:T(8,128)(2,1)S(1)}, bf16[64,1024]{1,0:T(8,128)(2,1)S(1)}, u32[]{:S(2)}, u32[]{:S(2)}) collective-permute-start(bf16[64,1024]{1,0:T(8,128)(2,1)S(1)} %reduce_sum.12), channel_id=1, source_target_pairs={{0,6},{1,7},{2,0},{3,1},{4,2},{5,3},{6,4},{7,5},{8,14},{9,15},{10,... | collective-permute-start | bytes 393224 | tf_op jit(solution)/shard_map/ppermute | solution.py:34
  77.4 5.0 %collective-permute-start.14 = (bf16[64,1024]{1,0:T(8,128)(2,1)S(1)}, bf16[64,1024]{1,0:T(8,128)(2,1)S(1)}, u32[]{:S(2)}, u32[]{:S(2)}) collective-permute-start(bf16[64,1024]{1,0:T(8,128)(2,1)S(1)} %add_convert_fusion), channel_id=1, source_target_pairs={{0,1},{1,0},{2,3},{3,2},{4,5},{5,4},{6,7},{7,6},{8,9},{9,8},{10,11... | collective-permute-start | bytes 393224 | tf_op jit(solution)/shard_map/ppermute | solution.py:34
  78.4 1.3 %copy-start.14 = (f32[320,1024]{1,0:T(8,128)S(1)}, f32[320,1024]{1,0:T(8,128)}, u32[]{:S(2)}) copy-start(f32[320,1024]{1,0:T(8,128)} %get-tuple-element.93.home) | copy-start | bytes 3932164

commit v6 on v5

--- a/solution.py
+++ b/solution.py
@@ -53,10 +53,8 @@
     return slopes.astype(BF16)
 
 
-def text_units(first, second, out):
-    rows = first.shape[0]
-    out[:rows] = normalize(first.astype(F32))[0].astype(BF16)
-    out[rows:] = normalize(second.astype(F32))[0].astype(BF16)
+def unit_rows(texts):
+    return normalize(texts.astype(F32))[0].astype(BF16)
 
 
 def stacked(refs):
@@ -64,8 +62,11 @@
     return blocks[0] if len(blocks) == 1 else jnp.concatenate(blocks)
 
 
-def first_kernel(feats, proj_weight, text, text_c, *outs):
-    text_units(text[...], text_c[...], outs[0])
+def first_kernel(feats, proj_weight, text, text_c, rest, *outs):
+    texts, rows = outs[0], text.shape[0]
+    units = unit_rows(text_c[...])
+    texts[:rows], texts[rows:] = unit_rows(text[...]), units[: texts.shape[0] - rows]
+    rest[...] = units[texts.shape[0] - rows :]
     early_kernel(1, True, feats, proj_weight, *outs)
 
 
@@ -93,10 +94,13 @@
 
 
 def middle_kernel(count, *refs):
-    early, (text_y, *text_yc), (texts, *outs) = (
-        refs[: 4 * count], refs[4 * count : 4 * count + 3], refs[4 * count + 3 :]
-    )
-    text_units(text_y[...], stacked(text_yc), texts)
+    early, (rest, text_y, *text_yc), (texts, *outs) = (
+        refs[: 4 * count], refs[4 * count : 4 * count + 4], refs[4 * count + 4 :]
+    )
+    rows = rest.shape[0]
+    texts[:rows] = rest[...]
+    texts[rows : rows + text_y.shape[0]] = unit_rows(text_y[...])
+    texts[rows + text_y.shape[0] :] = unit_rows(stacked(text_yc))
     for k in range(count):
         unit, norm, length, grad = early[4 * k : 4 * k + 4]
         slopes = slopes_of(unit[...], texts[...], False)
@@ -141,23 +145,33 @@
 
 def away_kernel(count, *refs):
     units, slopes, away = refs[:count], refs[count : 2 * count], refs[2 * count]
-    rows = away.shape[0]
-    away[...] = text_rows(units, slopes, rows, 2 * rows)
+    stop = slopes[0].shape[1]
+    away[...] = text_rows(units, slopes, stop - away.shape[0], stop)
 
 
 def home_kernel(count, *refs):
     units, slopes_a, slopes_b = (refs[k * count : (k + 1) * count] for k in range(3))
-    received, feats, y_out, home, away = refs[3 * count :]
-    rows = feats.shape[0]
-    total = received[...] + text_rows(units, slopes_b, 0, rows)
-    y_out[...] = project(total, *normalize(feats[...].astype(F32))).astype(BF16)
-    total = text_rows(units, slopes_a, 0, 2 * rows)
-    home[...], away[...] = total[:rows], total[rows:]
-
-
-def final_kernel(home, received, rest, feats, out):
-    norm, length = normalize(feats[...].astype(F32))
-    out[...] = project(home[...] + received[...], norm, length) + rest[...].astype(F32)
+    received, feats_y, feats, feats_c, y_out, home, away = refs[3 * count :]
+    rows, first = feats.shape[0], slopes_a[0].shape[1]
+    rest = 2 * rows - first
+
+    def through(total, feats):
+        return project(total, *normalize(feats[...].astype(F32)))
+
+    total = received[...] + text_rows(units, slopes_b, rest, rest + rows)
+    y_out[...] = through(total, feats_y).astype(BF16)
+    total = text_rows(units, slopes_a, 0, first)
+    home[...] = through(total[:rows], feats)
+    total = jnp.concatenate([total[rows:], text_rows(units, slopes_b, 0, rest)])
+    away[...] = through(total, feats_c).astype(BF16)
+
+
+def sum_kernel(parts, out):
+    out[...] = jnp.sum(parts[...].astype(F32), axis=0).astype(out.dtype)
+
+
+def add_text_kernel(first, second, out):
+    out[...] = first[...] + second[...].astype(F32)
 
 
 def call(kernel, outs, operands, mib, scratch=()):
@@ -177,7 +191,9 @@
 def local(sensor_feats, proj_weight, text_feats):
     rows, depth = sensor_feats.shape
     width = proj_weight.shape[1]
-    half, texts = rows // 2, 2 * rows
+    half = rows // 2
+    texts = 2 * rows // 256 * 256
+    texts_rest = 4 * rows - texts
     more, less = half + 16, half - 16
 
     def early_like(rows):
@@ -200,11 +216,11 @@
     right_rest = send(sensor_feats[more:], x=1)
     left_rest = send(sensor_feats[:less], x=-1)
 
-    texts_like = ((texts, width), BF16)
+    texts_like, rest_like = ((texts, width), BF16), ((2 * rows - texts, width), BF16)
     unit_like, grad_like, _, slopes_like, _ = early_like(rows)
-    texts_a, unit, norm, length, slopes_a, grad = call(
+    rest, texts_a, unit, norm, length, slopes_a, grad = call(
         first_kernel,
-        [texts_like, *early_like(rows)], [sensor_feats, proj_weight, text_feats, text_c], 18,
+        [rest_like, texts_like, *early_like(rows)], [sensor_feats, proj_weight, text_feats, text_c], 18,
     )
     right_low, left_high, grad = lax.optimization_barrier((right_low, left_high, grad))
     far_low, far_high = send(right_low, x=1), send(left_high, x=-1)
@@ -219,23 +235,23 @@
         (near_unit, near_norm, near_length, near),
         (next_unit, next_norm, next_length, next_),
     ]
-    outs = [[((g[0].shape[0], texts), BF16), ((g[0].shape[0], width), BF16)] for g in groups]
+    outs = [[((g[0].shape[0], texts_rest), BF16), ((g[0].shape[0], width), BF16)] for g in groups]
     texts_b, slopes_b, raw_grad, near_b, near_grad, next_b, next_grad = call(
         functools.partial(middle_kernel, 3),
-        [texts_like, *itertools.chain(*outs)],
-        [*itertools.chain(*groups), text_y, *text_yc],
-        32,
+        [((texts_rest, width), BF16), *itertools.chain(*outs)],
+        [*itertools.chain(*groups), rest, text_y, *text_yc],
+        24,
     )
     next_grad, far_low, far_high = lax.optimization_barrier((next_grad, far_low, far_high))
     share = (8, depth // 16, width)
     far_unit, far_a, far_b, mine, other = call(
         late_kernel,
-        [unit_like, slopes_like, slopes_like, (share, F32), (share, BF16)],
+        [unit_like, slopes_like, ((rows, texts_rest), BF16), (share, F32), (share, BF16)],
         [
             sensor_feats, right_low, left_high, right_rest, left_rest, far_low, far_high,
             raw_grad, near_grad, next_grad, proj_weight, texts_a, texts_b,
         ],
-        30,
+        24,
         scratch=[pltpu.VMEM((depth, width), F32)],
     )
 
@@ -251,22 +267,26 @@
     weight_all = lax.all_to_all(weight_sum, ("x", "yh"), split_axis=0, concat_axis=0, tiled=True)
     text_send, home_a, away_a = text_sums(
         home_kernel,
-        [unit_like, grad_like, grad_like],
+        [unit_like, grad_like, unit_like],
         58,
         [slopes_a, near_a, next_a, far_a, *half_b],
         send(away_b, c=1),
         text_y,
+        text_feats,
+        text_c,
     )
     text_out, away_a = send(text_send, yh=1), send(away_a, c=1)
 
-    weight_sum = jnp.sum(weight_all.astype(F32), axis=0).astype(BF16)
+    weight_sum = call(sum_kernel, [(share[1:], BF16)], [weight_all], 8)[0]
     across = send(weight_sum, z=2)
     ahead, behind = send(weight_sum, z=1), send(weight_sum, z=-1)
+    home_a = call(add_text_kernel, [grad_like], [home_a, away_a], 12)[0]
+    across, ahead, behind, home_a = lax.optimization_barrier((across, ahead, behind, home_a))
     weight_sum = (
         (weight_sum.astype(F32) + across.astype(F32)) + (ahead.astype(F32) + behind.astype(F32))
     ).astype(BF16)
     across = send(weight_sum, yl=1)
-    text_grad = call(final_kernel, [grad_like], [home_a, away_a, text_out, text_feats], 16)[0]
+    text_grad = call(add_text_kernel, [grad_like], [home_a, text_out], 12)[0]
     across, text_grad = lax.optimization_barrier((across, text_grad))
     return (text_grad, weight_sum.astype(F32) + across.astype(F32))
 

time: 83.5 us -> 82.7 us (level)
  other arithmetic: 2.21 us -> 0.8 us
  Pallas kernels: 33.1 us -> 31.8 us
  starting transfers between devices: 30.2 us -> 31.1 us
    ppermute x18, waiting for transfers between devices: 5.69 us -> 7.41 us  [send(): return lax.ppermute(block, AXES, route)]
    reduce_sum x1 -> x0, other arithmetic: 1.41 us -> none  [local(): weight_sum = jnp.sum(weight_all.astype(F32), axis=0).astype(BF16)]
    pallas_call x9 -> x11, Pallas kernels: 33.1 us -> 31.8 us  [call(): pl.pallas_call(kernel, out_shape=shapes, in_specs=[vmem] * len(operands),...]
    all_to_all x1, waiting for transfers between devices: 3.93 us -> 2.65 us  [local(): lax.all_to_all(weight_sum, ('x', 'yh'), split_axis=0, concat_axis=0, tile...]
    ppermute x18, starting transfers between devices: 26 us -> 26.9 us  [send(): return lax.ppermute(block, AXES, route)]
  transfers between devices with their start and end apart: 19 -> 19, of which waited for: 8 -> 9; matrix products, arithmetic and copies ran while one was open for 3% -> 1% of each run, Pallas kernels for 32% -> 31%
where the time goes in v6:
time: 82.7 us; the launch traced here: 81.8 us
  Pallas kernels  31.8 us (38%)
  starting transfers between devices  31.1 us (38%)
  waiting for transfers between devices  10.1 us (12%)
  local copies, waits for them, and re-layouts  7.03 us (9%)
  between operations  0.95 us (1%)
    pallas_call x11, Pallas kernels, call(): pl.pallas_call(kernel, out_shape=shapes, in_specs=[vmem] * len(operands),...  31.8 us
    ppermute x18, starting transfers between devices, send(): return lax.ppermute(block, AXES, route)  26.9 us
    ppermute x18, waiting for transfers between devices, send(): return lax.ppermute(block, AXES, route)  7.41 us
    unnamed x40, local copies, waits for them, and re-layouts  4.61 us
    all_to_all x1, starting transfers between devices, local(): lax.all_to_all(weight_sum, ('x', 'yh'), split_axis=0, concat_axis=0, tile...  4.22 us
    all_to_all x1, waiting for transfers between devices, local(): lax.all_to_all(weight_sum, ('x', 'yh'), split_axis=0, concat_axis=0, tile...  2.65 us
  transfers between devices with their start and end apart: 19, of which 9 were waited for; matrix products, arithmetic and copies ran while one was open for 1% of the time, Pallas kernels for 31%

profile of v6, /device:TPU:0, one launch (start us, length us, event | category | flops | bytes accessed | tf_op | source)
XLA Modules:
  0.0 81.8 jit_solution(7464965495752353822)
XLA Ops:
  0.6 1.3 %fusion.2 = (bf16[176,1024]{1,0:T(8,128)(2,1)S(1)}, bf16[176,1024]{1,0:T(8,128)(2,1)S(1)}) fusion(bf16[320,1024]{1,0:T(8,128)(2,1)} %refs_0_.1), kind=kLoop, calls=%fused_computation.4 | loop fusion | bytes 1441792 | tf_op jit(solution)/shard_map/slice | solution.py:212
  1.9 0.1 collective-permute-start.2
  2.0 3.4 %collective-permute-start.3 = (bf16[320,1024]{1,0:T(8,128)(2,1)}, bf16[320,1024]{1,0:T(8,128)(2,1)S(1)}, u32[]{:S(2)}, u32[]{:S(2)}) collective-permute-start(bf16[320,1024]{1,0:T(8,128)(2,1)} %refs_14_.1), channel_id=1, source_target_pairs={{0,16},{1,17},{2,18},{3,19},{4,20},{5,21},{6,22},{7,23},{8,24},{9,... | collective-permute-start | bytes 1966088 | tf_op jit(solution)/shard_map/ppermute | solution.py:34
  5.4 1.5 %collective-permute-start = (bf16[176,1024]{1,0:T(8,128)(2,1)S(1)}, bf16[176,1024]{1,0:T(8,128)(2,1)S(1)}, u32[]{:S(2)}, u32[]{:S(2)}) collective-permute-start(bf16[176,1024]{1,0:T(8,128)(2,1)S(1)} %get-tuple-element.55), channel_id=1, source_target_pairs={{0,32},{1,33},{2,34},{3,35},{4,36},{5,37},{6,38},{7,39},{8,40},{9,... | collective-permute-start | bytes 1081352 | tf_op jit(solution)/shard_map/ppermute | solution.py:34
  6.9 1.7 %collective-permute-start.1 = (bf16[176,1024]{1,0:T(8,128)(2,1)S(1)}, bf16[176,1024]{1,0:T(8,128)(2,1)S(1)}, u32[]{:S(2)}, u32[]{:S(2)}) collective-permute-start(bf16[176,1024]{1,0:T(8,128)(2,1)S(1)} %get-tuple-element.56), channel_id=1, source_target_pairs={{0,96},{1,97},{2,98},{3,99},{4,100},{5,101},{6,102},{7,103},{8,104... | collective-permute-start | bytes 1081352 | tf_op jit(solution)/shard_map/ppermute | solution.py:34
  8.6 1.1 %fusion.1 = (bf16[144,1024]{1,0:T(8,128)(2,1)S(1)}, bf16[144,1024]{1,0:T(8,128)(2,1)S(1)}) fusion(bf16[320,1024]{1,0:T(8,128)(2,1)} %refs_0_.1), kind=kLoop, calls=%fused_computation.3 | loop fusion | bytes 1179648 | tf_op jit(solution)/shard_map/slice | solution.py:217
  9.7 0.3 collective-permute-start.4
  10.1 3.0 %collective-permute-start.5 = (bf16[144,1024]{1,0:T(8,128)(2,1)S(1)}, bf16[144,1024]{1,0:T(8,128)(2,1)S(1)}, u32[]{:S(2)}, u32[]{:S(2)}) collective-permute-start(bf16[144,1024]{1,0:T(8,128)(2,1)S(1)} %get-tuple-element.110), channel_id=1, source_target_pairs={{0,96},{1,97},{2,98},{3,99},{4,100},{5,101},{6,102},{7,103},{8,104... | collective-permute-start | bytes 884744 | tf_op jit(solution)/shard_map/ppermute | solution.py:34
  13.0 1.1 %copy-done.1 = bf16[320,1024]{1,0:T(8,128)(2,1)S(1)} copy-done((bf16[320,1024]{1,0:T(8,128)(2,1)S(1)}, bf16[320,1024]{1,0:T(8,128)(2,1)}, u32[]{:S(2)}) %copy-start.1) | copy-done | bytes 655384
  14.1 1.1 %copy-done.7 = bf16[320,1024]{1,0:T(8,128)(2,1)S(1)} copy-done((bf16[320,1024]{1,0:T(8,128)(2,1)S(1)}, bf16[320,1024]{1,0:T(8,128)(2,1)}, u32[]{:S(2)}) %copy-start.7) | copy-done | bytes 655384
  15.2 2.0 %shard_map.50 = (bf16[128,1024]{1,0:T(8,128)(2,1)S(1)}, bf16[512,1024]{1,0:T(8,128)(2,1)S(1)}, bf16[320,1024]{1,0:T(8,128)(2,1)S(1)}, f32[320,1024]{1,0:T(8,128)...) custom-call(bf16[320,1024]{1,0:T(8,128)(2,1)S(1)} %copy-done.1, ...), custom_call_target="tpu_custom_call" | custom-call | flops 1 | bytes 1 | tf_op jit(solution)/shard_map/pallas_call | solution.py:180
  17.2 0.7 collective-permute-done.refs_0_.refs_1_
  17.9 0.3 collective-permute-done.1.refs_1_.refs_2_
  18.2 1.5 %collective-permute-start.8 = (bf16[176,1024]{1,0:T(8,128)(2,1)S(1)}, bf16[176,1024]{1,0:T(8,128)(2,1)S(1)}, u32[]{:S(2)}, u32[]{:S(2)}) collective-permute-start(bf16[176,1024]{1,0:T(8,128)(2,1)S(1)} %collective-permute-done.refs_0_.refs_1_), channel_id=1, source_target_pairs={{0,32},{1,33},{2,34},{3,35},{4,36},{5,37},{6,38},{7,39},{8,40},{9,... | collective-permute-start | bytes 1081352 | tf_op jit(solution)/shard_map/ppermute | solution.py:34
  19.7 1.7 %collective-permute-start.9 = (bf16[176,1024]{1,0:T(8,128)(2,1)S(1)}, bf16[176,1024]{1,0:T(8,128)(2,1)S(1)}, u32[]{:S(2)}, u32[]{:S(2)}) collective-permute-start(bf16[176,1024]{1,0:T(8,128)(2,1)S(1)} %collective-permute-done.1.refs_1_.refs_2_), channel_id=1, source_target_pairs={{0,96},{1,97},{2,98},{3,99},{4,100},{5,101},{6,102},{7,103},{8,104... | collective-permute-start | bytes 1081352 | tf_op jit(solution)/shard_map/ppermute | solution.py:34
  21.4 2.0 %shard_map.51 = (bf16[352,1024]{1,0:T(8,128)(2,1)S(1)}, f32[352,1024]{1,0:T(8,128)S(1)}, f32[352,1]{1,0:T(8,128)S(1)}, bf16[352,512]{1,0:T(8,128)(2,1)S(1)}, f32[352,1024]{1,0:T(8,128)S(1)}) custom-call(bf16[176,1024]{1,0:T(8,128)(2,1)S(1)} %collective-permute-done.refs_0_.refs_1_, bf16[176,1024]{1,0:T(8,128)(2,1)S(1)} %collective-permute-done.1.refs_1_.refs_2_, ...), custom_call_target="tpu_custom_call" | custom-call | flops 1 | bytes 1 | tf_op jit(solution)/shard_map/pallas_call | solution.py:180
  23.4 0.7 collective-permute-done.4.refs_0_.refs_3_
  24.2 0.3 collective-permute-done.5.refs_1_.refs_4_
  24.5 0.1 collective-permute-start.6
  24.6 0.5 collective-permute-start.7
  25.1 1.7 %shard_map.52 = (bf16[288,1024]{1,0:T(8,128)(2,1)S(1)}, f32[288,1024]{1,0:T(8,128)S(1)}, f32[288,1]{1,0:T(8,128)S(1)}, bf16[288,512]{1,0:T(8,128)(2,1)S(1)}, f32[288,1024]{1,0:T(8,128)S(1)}) custom-call(bf16[144,1024]{1,0:T(8,128)(2,1)S(1)} %collective-permute-done.4.refs_0_.refs_3_, bf16[144,1024]{1,0:T(8,128)(2,1)S(1)} %collective-permute-done.5.refs_1_.refs_4_, ...), custom_call_target="tpu_custom_call" | custom-call | flops 1 | bytes 1 | tf_op jit(solution)/shard_map/pallas_call | solution.py:180
  26.9 0.0 copy-start.2
  27.0 4.5 %shard_map.53 = (bf16[768,1024]{1,0:T(8,128)(2,1)S(1)}, bf16[320,768]{1,0:T(8,128)(2,1)S(1)}, bf16[320,1024]{1,0:T(8,128)(2,1)S(1)}, bf16[352,768]{1,0:T(8,128)(...) custom-call(bf16[320,1024]{1,0:T(8,128)(2,1)S(1)} %get-tuple-element.65.refs_0_, ...), custom_call_target="tpu_custom_call" | custom-call | flops 1 | bytes 1 | tf_op jit(solution)/shard_map/pallas_call | solution.py:180
  31.5 6.5 %shard_map.54 = (bf16[320,1024]{1,0:T(8,128)(2,1)S(1)}, bf16[320,512]{1,0:T(8,128)(2,1)S(1)}, bf16[320,768]{1,0:T(8,128)(2,1)S(1)}, f32[8,64,1024]{2,1,0:T(8,128)S(1)}, bf16[8,64,1024]{2,1,0:T(8,128)(2,1)S(1)}) custom-call(bf16[320,1024]{1,0:T(8,128)(2,1)S(1)} %copy-done.2, bf16[176,1024]{1,0:T(8,128)(2,1)S(1)} %collective-permute-done.refs_0_.refs_1_, ...), custom_call_target="tpu_custom_call" | custom-call | flops 1 | bytes 1 | tf_op jit(solution)/shard_map/pallas_call | solution.py:180
  38.1 0.7 collective-permute-start.10
  38.9 2.6 %shard_map.55 = f32[320,1024]{1,0:T(8,128)} custom-call(bf16[320,1024]{1,0:T(8,128)(2,1)S(1)} %get-tuple-element.65.refs_0_, bf16[352,1024]{1,0:T(8,128)(2,1)S(1)} %get-tuple-element.69.refs_4_.refs_1_, bf16[288,1024]{1,0:T(8,128)(2,1)S(1)} %get-tuple-element.73.refs_8_.refs_2_, bf16[320,1024]{1,0:T(8,128)(2,1)S(1)} %get-tuple-element.88.refs_3_, ...), custom_call_target="tpu_custom_call" | custom-call | flops 1 | bytes 1 | tf_op jit(solution)/shard_map/pallas_call | solution.py:180
  41.5 0.2 collective-permute-start.14
  41.6 1.2 %shard_map.56 = bf16[8,64,1024]{2,1,0:T(8,128)(2,1)} custom-call(f32[8,64,1024]{2,1,0:T(8,128)S(1)} %get-tuple-element.86.mine, bf16[8,64,1024]{2,1,0:T(8,128)(2,1)S(1)} %collective-permute-done.10.received), custom_call_target="tpu_custom_call" | custom-call | flops 1 | bytes 1 | tf_op jit(solution)/shard_map/pallas_call | solution.py:180
  42.8 4.2 %all-to-all-start = ((bf16[8,64,1024]{2,1,0:T(8,128)(2,1)}), bf16[8,64,1024]{2,1,0:T(8,128)(2,1)S(1)}, u32[]{:S(2)}, u32[]{:S(2)}) async-start(bf16[8,64,1024]{2,1,0:T(8,128)(2,1)} %shard_map.56), calls=%async_computation | async-start | bytes 2097152 | tf_op jit(solution)/shard_map/all_to_all | solution.py:267
  47.1 1.0 %copy-done.19 = f32[320,1024]{1,0:T(8,128)} copy-done((f32[320,1024]{1,0:T(8,128)}, f32[320,1024]{1,0:T(8,128)S(1)}, u32[]{:S(2)}) %copy-start.19) | copy-done | bytes 1310744
  48.1 9.9 %shard_map.58 = (bf16[320,1024]{1,0:T(8,128)(2,1)}, f32[320,1024]{1,0:T(8,128)}, bf16[320,1024]{1,0:T(8,128)(2,1)}) custom-call(bf16[320,1024]{1,0:T(8,128)(2,1)} %copy-done.5, bf16[352,1024]{1,0:T(8,128)(2,1)} %copy-done.3, bf16[288,1024]{1,0:T(8,128)(2,1)} %copy-done.6, bf16[320,1024]{1,0:T(8,128)(2,1)} %copy-done.9, bf16[320,512]{1,0:T(8,128)(2,1)} %copy-done.16, ...), custom_call_target="tpu_custom_call" | custom-call | flops 1 | bytes 1 | tf_op jit(solution)/shard_map/pallas_call | solution.py:180
  58.0 0.2 collective-permute-start.15
  58.2 3.4 %collective-permute-start.17 = (bf16[320,1024]{1,0:T(8,128)(2,1)}, bf16[320,1024]{1,0:T(8,128)(2,1)S(1)}, u32[]{:S(2)}, u32[]{:S(2)}) collective-permute-start(bf16[320,1024]{1,0:T(8,128)(2,1)} %get-tuple-element.105), channel_id=1, source_target_pairs={{0,16},{1,17},{2,18},{3,19},{4,20},{5,21},{6,22},{7,23},{8,24},{9,... | collective-permute-start | bytes 1966088 | tf_op jit(solution)/shard_map/ppermute | solution.py:34
  61.6 2.6 %all-to-all-done.parts = bf16[8,64,1024]{2,1,0:T(8,128)(2,1)S(1)} async-done(((bf16[8,64,1024]{2,1,0:T(8,128)(2,1)}), bf16[8,64,1024]{2,1,0:T(8,128)(2,1)S(1)}, u32[]{:S(2)}, u32[]{:S(2)}) %all-to-all-start) | async-done | bytes 1048608 | tf_op jit(solution)/shard_map/all_to_all | solution.py:267
  64.3 0.1 shard_map.57
  64.4 4.0 %collective-permute-start.11 = (bf16[64,1024]{1,0:T(8,128)(2,1)S(1)}, bf16[64,1024]{1,0:T(8,128)(2,1)S(1)}, u32[]{:S(2)}, u32[]{:S(2)}) collective-permute-start(bf16[64,1024]{1,0:T(8,128)(2,1)S(1)} %shard_map.57), channel_id=1, source_target_pairs={{0,4},{1,5},{2,6},{3,7},{4,0},{5,1},{6,2},{7,3},{8,12},{9,13},{10,... | collective-permute-start | bytes 393224 | tf_op jit(solution)/shard_map/ppermute | solution.py:34
  68.4 1.0 %collective-permute-start.12 = (bf16[64,1024]{1,0:T(8,128)(2,1)S(1)}, bf16[64,1024]{1,0:T(8,128)(2,1)S(1)}, u32[]{:S(2)}, u32[]{:S(2)}) collective-permute-start(bf16[64,1024]{1,0:T(8,128)(2,1)S(1)} %shard_map.57), channel_id=1, source_target_pairs={{0,2},{1,3},{2,4},{3,5},{4,6},{5,7},{6,0},{7,1},{8,10},{9,11},{10,... | collective-permute-start | bytes 393224 | tf_op jit(solution)/shard_map/ppermute | solution.py:34
  69.4 2.2 %collective-permute-start.13 = (bf16[64,1024]{1,0:T(8,128)(2,1)S(1)}, bf16[64,1024]{1,0:T(8,128)(2,1)S(1)}, u32[]{:S(2)}, u32[]{:S(2)}) collective-permute-start(bf16[64,1024]{1,0:T(8,128)(2,1)S(1)} %shard_map.57), channel_id=1, source_target_pairs={{0,6},{1,7},{2,0},{3,1},{4,2},{5,3},{6,4},{7,5},{8,14},{9,15},{10,... | collective-permute-start | bytes 393224 | tf_op jit(solution)/shard_map/ppermute | solution.py:34
  71.6 1.3 %copy-done.14 = f32[320,1024]{1,0:T(8,128)S(1)} copy-done((f32[320,1024]{1,0:T(8,128)S(1)}, f32[320,1024]{1,0:T(8,128)}, u32[]{:S(2)}) %copy-start.14) | copy-done | bytes 1310744
  72.9 0.1 shard_map.59.first
  73.1 1.6 %collective-permute-done.12 = bf16[64,1024]{1,0:T(8,128)(2,1)S(1)} collective-permute-done((bf16[64,1024]{1,0:T(8,128)(2,1)S(1)}, bf16[64,1024]{1,0:T(8,128)(2,1)S(1)}, u32[]{:S(2)}, u32[]{:S(2)}) %collective-permute-start.12) | collective-permute-done | bytes 131104 | tf_op jit(solution)/shard_map/ppermute | solution.py:34
  74.7 0.3 collective-permute-done.13
  75.0 0.1 add_convert_fusion
  75.1 1.4 %collective-permute-start.16 = (bf16[64,1024]{1,0:T(8,128)(2,1)S(1)}, bf16[64,1024]{1,0:T(8,128)(2,1)S(1)}, u32[]{:S(2)}, u32[]{:S(2)}) collective-permute-start(bf16[64,1024]{1,0:T(8,128)(2,1)S(1)} %add_convert_fusion), channel_id=1, source_target_pairs={{0,1},{1,0},{2,3},{3,2},{4,5},{5,4},{6,7},{7,6},{8,9},{9,8},{10,11... | collective-permute-start | bytes 393224 | tf_op jit(solution)/shard_map/ppermute | solution.py:34
  76.5 1.2 %collective-permute-done.17.second = bf16[320,1024]{1,0:T(8,128)(2,1)S(1)} collective-permute-done((bf16[320,1024]{1,0:T(8,128)(2,1)}, bf16[320,1024]{1,0:T(8,128)(2,1)S(1)}, u32[]{:S(2)}, u32[]{:S(2)}) %collective-permute-start.17) | collective-permute-done | bytes 655392 | tf_op jit(solution)/shard_map/ppermute | solution.py:34
  77.7 1.2 %shard_map.60 = f32[320,1024]{1,0:T(8,128)} custom-call(f32[320,1024]{1,0:T(8,128)S(1)} %shard_map.59.first, bf16[320,1024]{1,0:T(8,128)(2,1)S(1)} %collective-permute-done.17.second), custom_call_target="tpu_custom_call" | custom-call | flops 1 | bytes 1 | tf_op jit(solution)/shard_map/pallas_call | solution.py:180
  78.9 2.2 %collective-permute-done.16 = bf16[64,1024]{1,0:T(8,128)(2,1)S(1)} collective-permute-done((bf16[64,1024]{1,0:T(8,128)(2,1)S(1)}, bf16[64,1024]{1,0:T(8,128)(2,1)S(1)}, u32[]{:S(2)}, u32[]{:S(2)}) %collective-permute-start.16) | collective-permute-done | bytes 131104 | tf_op jit(solution)/shard_map/ppermute | solution.py:34
  81.1 0.7 convert_add_fusion
  (46 shorter events, 0.1 us)
Async XLA Ops:
  0.6 12.4 %copy-start = (bf16[1024,1024]{1,0:T(8,128)(2,1)S(1)}, bf16[1024,1024]{1,0:T(8,128)(2,1)}, u32[]{:S(2)}) copy-start(bf16[1024,1024]{1,0:T(8,128)(2,1)} %refs_10_.1) | copy-start | bytes 6291460
  1.9 8.1 %collective-permute-start.2 = (bf16[320,1024]{1,0:T(8,128)(2,1)}, bf16[320,1024]{1,0:T(8,128)(2,1)S(1)}, u32[]{:S(2)}, u32[]{:S(2)}) collective-permute-start(bf16[320,1024]{1,0:T(8,128)(2,1)} %refs_14_.1), channel_id=1, source_target_pairs={{0,8},{1,9},{2,10},{3,11},{4,12},{5,13},{6,14},{7,15},{8,0},{9,1},... | collective-permute-start | bytes 1966088 | tf_op jit(solution)/shard_map/ppermute | solution.py:34
  2.0 22.5 %collective-permute-start.3 = (bf16[320,1024]{1,0:T(8,128)(2,1)}, bf16[320,1024]{1,0:T(8,128)(2,1)S(1)}, u32[]{:S(2)}, u32[]{:S(2)}) collective-permute-start(bf16[320,1024]{1,0:T(8,128)(2,1)} %refs_14_.1), channel_id=1, source_target_pairs={{0,16},{1,17},{2,18},{3,19},{4,20},{5,21},{6,22},{7,23},{8,24},{9,... | collective-permute-start | bytes 1966088 | tf_op jit(solution)/shard_map/ppermute | solution.py:34
  5.4 12.5 %collective-permute-start = (bf16[176,1024]{1,0:T(8,128)(2,1)S(1)}, bf16[176,1024]{1,0:T(8,128)(2,1)S(1)}, u32[]{:S(2)}, u32[]{:S(2)}) collective-permute-start(bf16[176,1024]{1,0:T(8,128)(2,1)S(1)} %get-tuple-element.55), channel_id=1, source_target_pairs={{0,32},{1,33},{2,34},{3,35},{4,36},{5,37},{6,38},{7,39},{8,40},{9,... | collective-permute-start | bytes 1081352 | tf_op jit(solution)/shard_map/ppermute | solution.py:34
  6.9 11.3 %collective-permute-start.1 = (bf16[176,1024]{1,0:T(8,128)(2,1)S(1)}, bf16[176,1024]{1,0:T(8,128)(2,1)S(1)}, u32[]{:S(2)}, u32[]{:S(2)}) collective-permute-start(bf16[176,1024]{1,0:T(8,128)(2,1)S(1)} %get-tuple-element.56), channel_id=1, source_target_pairs={{0,96},{1,97},{2,98},{3,99},{4,100},{5,101},{6,102},{7,103},{8,104... | collective-permute-start | bytes 1081352 | tf_op jit(solution)/shard_map/ppermute | solution.py:34
  9.7 14.5 %collective-permute-start.4 = (bf16[144,1024]{1,0:T(8,128)(2,1)S(1)}, bf16[144,1024]{1,0:T(8,128)(2,1)S(1)}, u32[]{:S(2)}, u32[]{:S(2)}) collective-permute-start(bf16[144,1024]{1,0:T(8,128)(2,1)S(1)} %get-tuple-element.111), channel_id=1, source_target_pairs={{0,32},{1,33},{2,34},{3,35},{4,36},{5,37},{6,38},{7,39},{8,40},{9,... | collective-permute-start | bytes 884744 | tf_op jit(solution)/shard_map/ppermute | solution.py:34
  10.1 7.1 %copy-start.8 = (bf16[320,1024]{1,0:T(8,128)(2,1)}, bf16[320,1024]{1,0:T(8,128)(2,1)S(1)}, u32[]{:S(2)}) copy-start(bf16[320,1024]{1,0:T(8,128)(2,1)S(1)} %collective-permute-done.2.text_c.refs_15_) | copy-start | bytes 1966084
  10.1 14.4 %collective-permute-start.5 = (bf16[144,1024]{1,0:T(8,128)(2,1)S(1)}, bf16[144,1024]{1,0:T(8,128)(2,1)S(1)}, u32[]{:S(2)}, u32[]{:S(2)}) collective-permute-start(bf16[144,1024]{1,0:T(8,128)(2,1)S(1)} %get-tuple-element.110), channel_id=1, source_target_pairs={{0,96},{1,97},{2,98},{3,99},{4,100},{5,101},{6,102},{7,103},{8,104... | collective-permute-start | bytes 884744 | tf_op jit(solution)/shard_map/ppermute | solution.py:34
  13.0 1.1 %copy-start.1 = (bf16[320,1024]{1,0:T(8,128)(2,1)S(1)}, bf16[320,1024]{1,0:T(8,128)(2,1)}, u32[]{:S(2)}) copy-start(bf16[320,1024]{1,0:T(8,128)(2,1)} %refs_0_.1) | copy-start | bytes 1966084
  14.1 1.1 %copy-start.7 = (bf16[320,1024]{1,0:T(8,128)(2,1)S(1)}, bf16[320,1024]{1,0:T(8,128)(2,1)}, u32[]{:S(2)}) copy-start(bf16[320,1024]{1,0:T(8,128)(2,1)} %refs_14_.1) | copy-start | bytes 1966084
  17.2 6.2 %copy-start.16 = (bf16[320,512]{1,0:T(8,128)(2,1)}, bf16[320,512]{1,0:T(8,128)(2,1)S(1)}, u32[]{:S(2)}) copy-start(bf16[320,512]{1,0:T(8,128)(2,1)S(1)} %get-tuple-element.94.refs_4_) | copy-start | bytes 983044
  17.2 21.7 %copy-start.5 = (bf16[320,1024]{1,0:T(8,128)(2,1)}, bf16[320,1024]{1,0:T(8,128)(2,1)S(1)}, u32[]{:S(2)}) copy-start(bf16[320,1024]{1,0:T(8,128)(2,1)S(1)} %get-tuple-element.65.refs_0_) | copy-start | bytes 1966084
  18.2 13.3 %collective-permute-start.8 = (bf16[176,1024]{1,0:T(8,128)(2,1)S(1)}, bf16[176,1024]{1,0:T(8,128)(2,1)S(1)}, u32[]{:S(2)}, u32[]{:S(2)}) collective-permute-start(bf16[176,1024]{1,0:T(8,128)(2,1)S(1)} %collective-permute-done.refs_0_.refs_1_), channel_id=1, source_target_pairs={{0,32},{1,33},{2,34},{3,35},{4,36},{5,37},{6,38},{7,39},{8,40},{9,... | collective-permute-start | bytes 1081352 | tf_op jit(solution)/shard_map/ppermute | solution.py:34
  19.7 11.8 %collective-permute-start.9 = (bf16[176,1024]{1,0:T(8,128)(2,1)S(1)}, bf16[176,1024]{1,0:T(8,128)(2,1)S(1)}, u32[]{:S(2)}, u32[]{:S(2)}) collective-permute-start(bf16[176,1024]{1,0:T(8,128)(2,1)S(1)} %collective-permute-done.1.refs_1_.refs_2_), channel_id=1, source_target_pairs={{0,96},{1,97},{2,98},{3,99},{4,100},{5,101},{6,102},{7,103},{8,104... | collective-permute-start | bytes 1081352 | tf_op jit(solution)/shard_map/ppermute | solution.py:34
  23.4 3.5 %copy-start.15 = (bf16[352,512]{1,0:T(8,128)(2,1)}, bf16[352,512]{1,0:T(8,128)(2,1)S(1)}, u32[]{:S(2)}) copy-start(bf16[352,512]{1,0:T(8,128)(2,1)S(1)} %get-tuple-element.95.refs_5_) | copy-start | bytes 1081348
  23.4 15.4 %copy-start.3 = (bf16[352,1024]{1,0:T(8,128)(2,1)}, bf16[352,1024]{1,0:T(8,128)(2,1)S(1)}, u32[]{:S(2)}) copy-start(bf16[352,1024]{1,0:T(8,128)(2,1)S(1)} %get-tuple-element.69.refs_4_.refs_1_) | copy-start | bytes 2162692
  24.5 2.4 %copy-start.4 = (bf16[320,1024]{1,0:T(8,128)(2,1)}, bf16[320,1024]{1,0:T(8,128)(2,1)S(1)}, u32[]{:S(2)}) copy-start(bf16[320,1024]{1,0:T(8,128)(2,1)S(1)} %collective-permute-done.3.refs_13_) | copy-start | bytes 1966084
  24.5 2.4 %collective-permute-start.6 = (bf16[160,1024]{1,0:T(8,128)(2,1)S(1)}, bf16[160,1024]{1,0:T(8,128)(2,1)S(1)}, u32[]{:S(2)}, u32[]{:S(2)}) collective-permute-start(bf16[160,1024]{1,0:T(8,128)(2,1)S(1)} %get-tuple-element.109), channel_id=1, source_target_pairs={{0,8},{1,9},{2,10},{3,11},{4,12},{5,13},{6,14},{7,15},{8,0},{9,1},... | collective-permute-start | bytes 983048 | tf_op jit(solution)/shard_map/ppermute | solution.py:34
  24.6 2.3 %collective-permute-start.7 = (bf16[160,1024]{1,0:T(8,128)(2,1)S(1)}, bf16[160,1024]{1,0:T(8,128)(2,1)S(1)}, u32[]{:S(2)}, u32[]{:S(2)}) collective-permute-start(bf16[160,1024]{1,0:T(8,128)(2,1)S(1)} %get-tuple-element.108), channel_id=1, source_target_pairs={{0,8},{1,9},{2,10},{3,11},{4,12},{5,13},{6,14},{7,15},{8,0},{9,1},... | collective-permute-start | bytes 983048 | tf_op jit(solution)/shard_map/ppermute | solution.py:34
  26.9 4.6 %copy-start.18 = (bf16[288,512]{1,0:T(8,128)(2,1)}, bf16[288,512]{1,0:T(8,128)(2,1)S(1)}, u32[]{:S(2)}) copy-start(bf16[288,512]{1,0:T(8,128)(2,1)S(1)} %get-tuple-element.96.refs_6_) | copy-start | bytes 884740
  26.9 11.9 %copy-start.6 = (bf16[288,1024]{1,0:T(8,128)(2,1)}, bf16[288,1024]{1,0:T(8,128)(2,1)S(1)}, u32[]{:S(2)}) copy-start(bf16[288,1024]{1,0:T(8,128)(2,1)S(1)} %get-tuple-element.73.refs_8_.refs_2_) | copy-start | bytes 1769476
  26.9 4.6 %copy-start.2 = (bf16[320,1024]{1,0:T(8,128)(2,1)S(1)}, bf16[320,1024]{1,0:T(8,128)(2,1)}, u32[]{:S(2)}) copy-start(bf16[320,1024]{1,0:T(8,128)(2,1)} %refs_0_.1) | copy-start | bytes 1966084
  31.5 7.4 %copy-start.10 = (bf16[352,768]{1,0:T(8,128)(2,1)}, bf16[352,768]{1,0:T(8,128)(2,1)S(1)}, u32[]{:S(2)}) copy-start(bf16[352,768]{1,0:T(8,128)(2,1)S(1)} %get-tuple-element.90.refs_5_.refs_9_) | copy-start | bytes 1622020
  31.5 7.4 %copy-start.11 = (bf16[320,768]{1,0:T(8,128)(2,1)}, bf16[320,768]{1,0:T(8,128)(2,1)S(1)}, u32[]{:S(2)}) copy-start(bf16[320,768]{1,0:T(8,128)(2,1)S(1)} %get-tuple-element.89.refs_4_.refs_8_) | copy-start | bytes 1474564
  31.5 7.4 %copy-start.13 = (bf16[288,768]{1,0:T(8,128)(2,1)}, bf16[288,768]{1,0:T(8,128)(2,1)S(1)}, u32[]{:S(2)}) copy-start(bf16[288,768]{1,0:T(8,128)(2,1)S(1)} %get-tuple-element.91.refs_6_.refs_10_) | copy-start | bytes 1327108
  38.1 3.4 %copy-start.9 = (bf16[320,1024]{1,0:T(8,128)(2,1)}, bf16[320,1024]{1,0:T(8,128)(2,1)S(1)}, u32[]{:S(2)}) copy-start(bf16[320,1024]{1,0:T(8,128)(2,1)S(1)} %get-tuple-element.88.refs_3_) | copy-start | bytes 1966084
  38.1 3.4 %copy-start.12 = (bf16[320,768]{1,0:T(8,128)(2,1)}, bf16[320,768]{1,0:T(8,128)(2,1)S(1)}, u32[]{:S(2)}) copy-start(bf16[320,768]{1,0:T(8,128)(2,1)S(1)} %get-tuple-element.92.refs_7_.refs_11_) | copy-start | bytes 1474564
  38.1 3.4 %copy-start.17 = (bf16[320,512]{1,0:T(8,128)(2,1)}, bf16[320,512]{1,0:T(8,128)(2,1)S(1)}, u32[]{:S(2)}) copy-start(bf16[320,512]{1,0:T(8,128)(2,1)S(1)} %get-tuple-element.97.refs_7_) | copy-start | bytes 983044
  38.1 3.4 %collective-permute-start.10 = (bf16[8,64,1024]{2,1,0:T(8,128)(2,1)S(1)}, bf16[8,64,1024]{2,1,0:T(8,128)(2,1)S(1)}, u32[]{:S(2)}, u32[]{:S(2)}) collective-permute-start(bf16[8,64,1024]{2,1,0:T(8,128)(2,1)S(1)} %get-tuple-element.87), channel_id=1, source_target_pairs={{0,8},{1,9},{2,10},{3,11},{4,12},{5,13},{6,14},{7,15},{8,0},{9,1},... | collective-permute-start | bytes 3145736 | tf_op jit(solution)/shard_map/ppermute | solution.py:34
  41.5 5.6 %collective-permute-start.14 = (f32[320,1024]{1,0:T(8,128)}, f32[320,1024]{1,0:T(8,128)S(1)}, u32[]{:S(2)}, u32[]{:S(2)}) collective-permute-start(f32[320,1024]{1,0:T(8,128)} %shard_map.55), channel_id=1, source_target_pairs={{0,8},{1,9},{2,10},{3,11},{4,12},{5,13},{6,14},{7,15},{8,0},{9,1},... | collective-permute-start | bytes 3932168 | tf_op jit(solution)/shard_map/ppermute | solution.py:34
  42.8 21.5 %all-to-all-start = ((bf16[8,64,1024]{2,1,0:T(8,128)(2,1)}), bf16[8,64,1024]{2,1,0:T(8,128)(2,1)S(1)}, u32[]{:S(2)}, u32[]{:S(2)}) async-start(bf16[8,64,1024]{2,1,0:T(8,128)(2,1)} %shard_map.56), calls=%async_computation | async-start | bytes 2097152 | tf_op jit(solution)/shard_map/all_to_all | solution.py:267
  47.0 1.1 %copy-start.19 = (f32[320,1024]{1,0:T(8,128)}, f32[320,1024]{1,0:T(8,128)S(1)}, u32[]{:S(2)}) copy-start(f32[320,1024]{1,0:T(8,128)S(1)} %collective-permute-done.14.refs_12_) | copy-start | bytes 3932164
  58.0 13.6 %collective-permute-start.15 = (bf16[320,1024]{1,0:T(8,128)(2,1)}, bf16[320,1024]{1,0:T(8,128)(2,1)S(1)}, u32[]{:S(2)}, u32[]{:S(2)}) collective-permute-start(bf16[320,1024]{1,0:T(8,128)(2,1)} %get-tuple-element.100), channel_id=1, source_target_pairs={{0,8},{1,9},{2,10},{3,11},{4,12},{5,13},{6,14},{7,15},{8,0},{9,1},... | collective-permute-start | bytes 1966088 | tf_op jit(solution)/shard_map/ppermute | solution.py:34
  58.2 19.5 %collective-permute-start.17 = (bf16[320,1024]{1,0:T(8,128)(2,1)}, bf16[320,1024]{1,0:T(8,128)(2,1)S(1)}, u32[]{:S(2)}, u32[]{:S(2)}) collective-permute-start(bf16[320,1024]{1,0:T(8,128)(2,1)} %get-tuple-element.105), channel_id=1, source_target_pairs={{0,16},{1,17},{2,18},{3,19},{4,20},{5,21},{6,22},{7,23},{8,24},{9,... | collective-permute-start | bytes 1966088 | tf_op jit(solution)/shard_map/ppermute | solution.py:34
  64.4 8.6 %collective-permute-start.11 = (bf16[64,1024]{1,0:T(8,128)(2,1)S(1)}, bf16[64,1024]{1,0:T(8,128)(2,1)S(1)}, u32[]{:S(2)}, u32[]{:S(2)}) collective-permute-start(bf16[64,1024]{1,0:T(8,128)(2,1)S(1)} %shard_map.57), channel_id=1, source_target_pairs={{0,4},{1,5},{2,6},{3,7},{4,0},{5,1},{6,2},{7,3},{8,12},{9,13},{10,... | collective-permute-start | bytes 393224 | tf_op jit(solution)/shard_map/ppermute | solution.py:34
  68.4 6.3 %collective-permute-start.12 = (bf16[64,1024]{1,0:T(8,128)(2,1)S(1)}, bf16[64,1024]{1,0:T(8,128)(2,1)S(1)}, u32[]{:S(2)}, u32[]{:S(2)}) collective-permute-start(bf16[64,1024]{1,0:T(8,128)(2,1)S(1)} %shard_map.57), channel_id=1, source_target_pairs={{0,2},{1,3},{2,4},{3,5},{4,6},{5,7},{6,0},{7,1},{8,10},{9,11},{10,... | collective-permute-start | bytes 393224 | tf_op jit(solution)/shard_map/ppermute | solution.py:34
  69.4 5.6 %collective-permute-start.13 = (bf16[64,1024]{1,0:T(8,128)(2,1)S(1)}, bf16[64,1024]{1,0:T(8,128)(2,1)S(1)}, u32[]{:S(2)}, u32[]{:S(2)}) collective-permute-start(bf16[64,1024]{1,0:T(8,128)(2,1)S(1)} %shard_map.57), channel_id=1, source_target_pairs={{0,6},{1,7},{2,0},{3,1},{4,2},{5,3},{6,4},{7,5},{8,14},{9,15},{10,... | collective-permute-start | bytes 393224 | tf_op jit(solution)/shard_map/ppermute | solution.py:34
  71.6 1.3 %copy-start.14 = (f32[320,1024]{1,0:T(8,128)S(1)}, f32[320,1024]{1,0:T(8,128)}, u32[]{:S(2)}) copy-start(f32[320,1024]{1,0:T(8,128)} %get-tuple-element.99.first) | copy-start | bytes 3932164
  75.1 6.0 %collective-permute-start.16 = (bf16[64,1024]{1,0:T(8,128)(2,1)S(1)}, bf16[64,1024]{1,0:T(8,128)(2,1)S(1)}, u32[]{:S(2)}, u32[]{:S(2)}) collective-permute-start(bf16[64,1024]{1,0:T(8,128)(2,1)S(1)} %add_convert_fusion), channel_id=1, source_target_pairs={{0,1},{1,0},{2,3},{3,2},{4,5},{5,4},{6,7},{7,6},{8,9},{9,8},{10,11... | collective-permute-start | bytes 393224 | tf_op jit(solution)/shard_map/ppermute | solution.py:34

commit v7 on v6

--- a/solution.py
+++ b/solution.py
@@ -114,22 +114,20 @@
     core = lax.axis_index("c")
     feats, (low, high), grads = refs[:5], refs[5:7], refs[7:10]
     (proj_weight, texts_a, texts_b), outs = refs[10:13], refs[13:]
-    unit_out, slopes_a, slopes_b, mine_out, other_out, weight = outs
+    unit_out, slopes_a, slopes_b, mine_out, other_out, flipped = outs
     half = unit_out.shape[0] // 2
     far = jnp.concatenate([low[:half], high[high.shape[0] - half :]])
+    flipped[...] = jnp.concatenate([stacked(feats), far]).T
     unit_out[...], slopes_a[...], slopes_b[...], far_grad = whole_block(
         far, proj_weight, texts_a, texts_b
     )
-    feats = jnp.concatenate([stacked(feats), far])
     grads = jnp.concatenate([stacked(grads), far_grad])
-    weight[...] = jnp.dot(feats.T, grads, preferred_element_type=F32)
-    slices, rows = mine_out.shape[0], mine_out.shape[1]
-    for k in range(slices):
-        start = 2 * k * rows
-        mine = pl.ds(pl.multiple_of(start + core * rows, rows), rows)
-        other = pl.ds(pl.multiple_of(start + (1 - core) * rows, rows), rows)
-        mine_out[k] = weight[mine]
-        other_out[k] = weight[other].astype(BF16)
+    slices, rows, width = mine_out.shape
+    for out, side in ((other_out, 1 - core), (mine_out, core)):
+        starts = [pl.multiple_of((2 * k + side) * rows, rows) for k in range(slices)]
+        part = jnp.concatenate([flipped[pl.ds(start, rows)] for start in starts])
+        product = jnp.dot(part, grads, preferred_element_type=F32)
+        out[...] = product.reshape(slices, rows, width).astype(out.dtype)
 
 
 def add_kernel(mine, received, out):
@@ -252,7 +250,7 @@
             raw_grad, near_grad, next_grad, proj_weight, texts_a, texts_b,
         ],
         24,
-        scratch=[pltpu.VMEM((depth, width), F32)],
+        scratch=[pltpu.VMEM((depth, 4 * rows), BF16)],
     )
 
     def text_sums(kernel, outs, mib, slopes, *others):

time: 82.7 us -> 82.4 us (level)
  no operation moved by 1% of the time
where the time goes in v7:
time: 82.4 us; the launch traced here: 81.5 us
  Pallas kernels  31.6 us (38%)
  starting transfers between devices  31.1 us (38%)
  waiting for transfers between devices  10.1 us (12%)
  local copies, waits for them, and re-layouts  7.03 us (9%)
  between operations  0.96 us (1%)
    pallas_call x11, Pallas kernels, call(): pl.pallas_call(kernel, out_shape=shapes, in_specs=[vmem] * len(operands),...  31.6 us
    ppermute x18, starting transfers between devices, send(): return lax.ppermute(block, AXES, route)  26.9 us
    ppermute x18, waiting for transfers between devices, send(): return lax.ppermute(block, AXES, route)  7.89 us
    unnamed x40, local copies, waits for them, and re-layouts  4.61 us
    all_to_all x1, starting transfers between devices, local(): lax.all_to_all(weight_sum, ('x', 'yh'), split_axis=0, concat_axis=0, tile...  4.22 us
    all_to_all x1, waiting for transfers between devices, local(): lax.all_to_all(weight_sum, ('x', 'yh'), split_axis=0, concat_axis=0, tile...  2.22 us
  transfers between devices with their start and end apart: 19, of which 9 were waited for; matrix products, arithmetic and copies ran while one was open for 1% of the time, Pallas kernels for 31%

profile of v7, /device:TPU:0, one launch (start us, length us, event | category | flops | bytes accessed | tf_op | source)
XLA Modules:
  0.0 81.5 jit_solution(11525605751144058154)
XLA Ops:
  0.6 1.3 %fusion.2 = (bf16[176,1024]{1,0:T(8,128)(2,1)S(1)}, bf16[176,1024]{1,0:T(8,128)(2,1)S(1)}) fusion(bf16[320,1024]{1,0:T(8,128)(2,1)} %refs_0_.1), kind=kLoop, calls=%fused_computation.4 | loop fusion | bytes 1441792 | tf_op jit(solution)/shard_map/slice | solution.py:210
  1.9 0.1 collective-permute-start.2
  2.0 3.4 %collective-permute-start.3 = (bf16[320,1024]{1,0:T(8,128)(2,1)}, bf16[320,1024]{1,0:T(8,128)(2,1)S(1)}, u32[]{:S(2)}, u32[]{:S(2)}) collective-permute-start(bf16[320,1024]{1,0:T(8,128)(2,1)} %refs_14_.1), channel_id=1, source_target_pairs={{0,16},{1,17},{2,18},{3,19},{4,20},{5,21},{6,22},{7,23},{8,24},{9,... | collective-permute-start | bytes 1966088 | tf_op jit(solution)/shard_map/ppermute | solution.py:34
  5.4 1.5 %collective-permute-start = (bf16[176,1024]{1,0:T(8,128)(2,1)S(1)}, bf16[176,1024]{1,0:T(8,128)(2,1)S(1)}, u32[]{:S(2)}, u32[]{:S(2)}) collective-permute-start(bf16[176,1024]{1,0:T(8,128)(2,1)S(1)} %get-tuple-element.55), channel_id=1, source_target_pairs={{0,32},{1,33},{2,34},{3,35},{4,36},{5,37},{6,38},{7,39},{8,40},{9,... | collective-permute-start | bytes 1081352 | tf_op jit(solution)/shard_map/ppermute | solution.py:34
  6.9 1.7 %collective-permute-start.1 = (bf16[176,1024]{1,0:T(8,128)(2,1)S(1)}, bf16[176,1024]{1,0:T(8,128)(2,1)S(1)}, u32[]{:S(2)}, u32[]{:S(2)}) collective-permute-start(bf16[176,1024]{1,0:T(8,128)(2,1)S(1)} %get-tuple-element.56), channel_id=1, source_target_pairs={{0,96},{1,97},{2,98},{3,99},{4,100},{5,101},{6,102},{7,103},{8,104... | collective-permute-start | bytes 1081352 | tf_op jit(solution)/shard_map/ppermute | solution.py:34
  8.6 1.1 %fusion.1 = (bf16[144,1024]{1,0:T(8,128)(2,1)S(1)}, bf16[144,1024]{1,0:T(8,128)(2,1)S(1)}) fusion(bf16[320,1024]{1,0:T(8,128)(2,1)} %refs_0_.1), kind=kLoop, calls=%fused_computation.3 | loop fusion | bytes 1179648 | tf_op jit(solution)/shard_map/slice | solution.py:215
  9.7 0.3 collective-permute-start.4
  10.1 3.0 %collective-permute-start.5 = (bf16[144,1024]{1,0:T(8,128)(2,1)S(1)}, bf16[144,1024]{1,0:T(8,128)(2,1)S(1)}, u32[]{:S(2)}, u32[]{:S(2)}) collective-permute-start(bf16[144,1024]{1,0:T(8,128)(2,1)S(1)} %get-tuple-element.110), channel_id=1, source_target_pairs={{0,96},{1,97},{2,98},{3,99},{4,100},{5,101},{6,102},{7,103},{8,104... | collective-permute-start | bytes 884744 | tf_op jit(solution)/shard_map/ppermute | solution.py:34
  13.0 1.1 %copy-done.1 = bf16[320,1024]{1,0:T(8,128)(2,1)S(1)} copy-done((bf16[320,1024]{1,0:T(8,128)(2,1)S(1)}, bf16[320,1024]{1,0:T(8,128)(2,1)}, u32[]{:S(2)}) %copy-start.1) | copy-done | bytes 655384
  14.1 1.1 %copy-done.7 = bf16[320,1024]{1,0:T(8,128)(2,1)S(1)} copy-done((bf16[320,1024]{1,0:T(8,128)(2,1)S(1)}, bf16[320,1024]{1,0:T(8,128)(2,1)}, u32[]{:S(2)}) %copy-start.7) | copy-done | bytes 655384
  15.2 2.0 %shard_map.50 = (bf16[128,1024]{1,0:T(8,128)(2,1)S(1)}, bf16[512,1024]{1,0:T(8,128)(2,1)S(1)}, bf16[320,1024]{1,0:T(8,128)(2,1)S(1)}, f32[320,1024]{1,0:T(8,128)...) custom-call(bf16[320,1024]{1,0:T(8,128)(2,1)S(1)} %copy-done.1, ...), custom_call_target="tpu_custom_call" | custom-call | flops 1 | bytes 1 | tf_op jit(solution)/shard_map/pallas_call | solution.py:178
  17.2 0.7 collective-permute-done.refs_0_.refs_1_
  17.9 0.3 collective-permute-done.1.refs_1_.refs_2_
  18.2 1.5 %collective-permute-start.8 = (bf16[176,1024]{1,0:T(8,128)(2,1)S(1)}, bf16[176,1024]{1,0:T(8,128)(2,1)S(1)}, u32[]{:S(2)}, u32[]{:S(2)}) collective-permute-start(bf16[176,1024]{1,0:T(8,128)(2,1)S(1)} %collective-permute-done.refs_0_.refs_1_), channel_id=1, source_target_pairs={{0,32},{1,33},{2,34},{3,35},{4,36},{5,37},{6,38},{7,39},{8,40},{9,... | collective-permute-start | bytes 1081352 | tf_op jit(solution)/shard_map/ppermute | solution.py:34
  19.7 1.7 %collective-permute-start.9 = (bf16[176,1024]{1,0:T(8,128)(2,1)S(1)}, bf16[176,1024]{1,0:T(8,128)(2,1)S(1)}, u32[]{:S(2)}, u32[]{:S(2)}) collective-permute-start(bf16[176,1024]{1,0:T(8,128)(2,1)S(1)} %collective-permute-done.1.refs_1_.refs_2_), channel_id=1, source_target_pairs={{0,96},{1,97},{2,98},{3,99},{4,100},{5,101},{6,102},{7,103},{8,104... | collective-permute-start | bytes 1081352 | tf_op jit(solution)/shard_map/ppermute | solution.py:34
  21.4 2.0 %shard_map.51 = (bf16[352,1024]{1,0:T(8,128)(2,1)S(1)}, f32[352,1024]{1,0:T(8,128)S(1)}, f32[352,1]{1,0:T(8,128)S(1)}, bf16[352,512]{1,0:T(8,128)(2,1)S(1)}, f32[352,1024]{1,0:T(8,128)S(1)}) custom-call(bf16[176,1024]{1,0:T(8,128)(2,1)S(1)} %collective-permute-done.refs_0_.refs_1_, bf16[176,1024]{1,0:T(8,128)(2,1)S(1)} %collective-permute-done.1.refs_1_.refs_2_, ...), custom_call_target="tpu_custom_call" | custom-call | flops 1 | bytes 1 | tf_op jit(solution)/shard_map/pallas_call | solution.py:178
  23.4 0.7 collective-permute-done.4.refs_0_.refs_3_
  24.2 0.3 collective-permute-done.5.refs_1_.refs_4_
  24.5 0.1 collective-permute-start.6
  24.6 0.5 collective-permute-start.7
  25.1 1.7 %shard_map.52 = (bf16[288,1024]{1,0:T(8,128)(2,1)S(1)}, f32[288,1024]{1,0:T(8,128)S(1)}, f32[288,1]{1,0:T(8,128)S(1)}, bf16[288,512]{1,0:T(8,128)(2,1)S(1)}, f32[288,1024]{1,0:T(8,128)S(1)}) custom-call(bf16[144,1024]{1,0:T(8,128)(2,1)S(1)} %collective-permute-done.4.refs_0_.refs_3_, bf16[144,1024]{1,0:T(8,128)(2,1)S(1)} %collective-permute-done.5.refs_1_.refs_4_, ...), custom_call_target="tpu_custom_call" | custom-call | flops 1 | bytes 1 | tf_op jit(solution)/shard_map/pallas_call | solution.py:178
  26.9 0.0 copy-start.2
  27.0 4.5 %shard_map.53 = (bf16[768,1024]{1,0:T(8,128)(2,1)S(1)}, bf16[320,768]{1,0:T(8,128)(2,1)S(1)}, bf16[320,1024]{1,0:T(8,128)(2,1)S(1)}, bf16[352,768]{1,0:T(8,128)(...) custom-call(bf16[320,1024]{1,0:T(8,128)(2,1)S(1)} %get-tuple-element.65.refs_0_, ...), custom_call_target="tpu_custom_call" | custom-call | flops 1 | bytes 1 | tf_op jit(solution)/shard_map/pallas_call | solution.py:178
  31.5 6.3 %shard_map.54 = (bf16[320,1024]{1,0:T(8,128)(2,1)S(1)}, bf16[320,512]{1,0:T(8,128)(2,1)S(1)}, bf16[320,768]{1,0:T(8,128)(2,1)S(1)}, f32[8,64,1024]{2,1,0:T(8,128)S(1)}, bf16[8,64,1024]{2,1,0:T(8,128)(2,1)S(1)}) custom-call(bf16[320,1024]{1,0:T(8,128)(2,1)S(1)} %copy-done.2, bf16[176,1024]{1,0:T(8,128)(2,1)S(1)} %collective-permute-done.refs_0_.refs_1_, ...), custom_call_target="tpu_custom_call" | custom-call | flops 1 | bytes 1 | tf_op jit(solution)/shard_map/pallas_call | solution.py:178
  37.8 0.4 collective-permute-start.10
  38.2 2.6 %shard_map.55 = f32[320,1024]{1,0:T(8,128)} custom-call(bf16[320,1024]{1,0:T(8,128)(2,1)S(1)} %get-tuple-element.65.refs_0_, bf16[352,1024]{1,0:T(8,128)(2,1)S(1)} %get-tuple-element.69.refs_4_.refs_1_, bf16[288,1024]{1,0:T(8,128)(2,1)S(1)} %get-tuple-element.73.refs_8_.refs_2_, bf16[320,1024]{1,0:T(8,128)(2,1)S(1)} %get-tuple-element.88.refs_3_, ...), custom_call_target="tpu_custom_call" | custom-call | flops 1 | bytes 1 | tf_op jit(solution)/shard_map/pallas_call | solution.py:178
  40.9 0.5 collective-permute-start.14
  41.4 1.2 %shard_map.56 = bf16[8,64,1024]{2,1,0:T(8,128)(2,1)} custom-call(f32[8,64,1024]{2,1,0:T(8,128)S(1)} %get-tuple-element.86.mine, bf16[8,64,1024]{2,1,0:T(8,128)(2,1)S(1)} %collective-permute-done.10.received), custom_call_target="tpu_custom_call" | custom-call | flops 1 | bytes 1 | tf_op jit(solution)/shard_map/pallas_call | solution.py:178
  42.6 4.2 %all-to-all-start = ((bf16[8,64,1024]{2,1,0:T(8,128)(2,1)}), bf16[8,64,1024]{2,1,0:T(8,128)(2,1)S(1)}, u32[]{:S(2)}, u32[]{:S(2)}) async-start(bf16[8,64,1024]{2,1,0:T(8,128)(2,1)} %shard_map.56), calls=%async_computation | async-start | bytes 2097152 | tf_op jit(solution)/shard_map/all_to_all | solution.py:265
  46.8 1.0 %copy-done.19 = f32[320,1024]{1,0:T(8,128)} copy-done((f32[320,1024]{1,0:T(8,128)}, f32[320,1024]{1,0:T(8,128)S(1)}, u32[]{:S(2)}) %copy-start.19) | copy-done | bytes 1310744
  47.8 9.9 %shard_map.58 = (bf16[320,1024]{1,0:T(8,128)(2,1)}, f32[320,1024]{1,0:T(8,128)}, bf16[320,1024]{1,0:T(8,128)(2,1)}) custom-call(bf16[320,1024]{1,0:T(8,128)(2,1)} %copy-done.5, bf16[352,1024]{1,0:T(8,128)(2,1)} %copy-done.3, bf16[288,1024]{1,0:T(8,128)(2,1)} %copy-done.6, bf16[320,1024]{1,0:T(8,128)(2,1)} %copy-done.9, bf16[320,512]{1,0:T(8,128)(2,1)} %copy-done.16, ...), custom_call_target="tpu_custom_call" | custom-call | flops 1 | bytes 1 | tf_op jit(solution)/shard_map/pallas_call | solution.py:178
  57.8 0.0 collective-permute-start.15
  57.8 3.6 %collective-permute-start.17 = (bf16[320,1024]{1,0:T(8,128)(2,1)}, bf16[320,1024]{1,0:T(8,128)(2,1)S(1)}, u32[]{:S(2)}, u32[]{:S(2)}) collective-permute-start(bf16[320,1024]{1,0:T(8,128)(2,1)} %get-tuple-element.105), channel_id=1, source_target_pairs={{0,16},{1,17},{2,18},{3,19},{4,20},{5,21},{6,22},{7,23},{8,24},{9,... | collective-permute-start | bytes 1966088 | tf_op jit(solution)/shard_map/ppermute | solution.py:34
  61.4 2.2 %all-to-all-done.parts = bf16[8,64,1024]{2,1,0:T(8,128)(2,1)S(1)} async-done(((bf16[8,64,1024]{2,1,0:T(8,128)(2,1)}), bf16[8,64,1024]{2,1,0:T(8,128)(2,1)S(1)}, u32[]{:S(2)}, u32[]{:S(2)}) %all-to-all-start) | async-done | bytes 1048608 | tf_op jit(solution)/shard_map/all_to_all | solution.py:265
  63.6 0.1 shard_map.57
  63.7 3.9 %collective-permute-start.11 = (bf16[64,1024]{1,0:T(8,128)(2,1)S(1)}, bf16[64,1024]{1,0:T(8,128)(2,1)S(1)}, u32[]{:S(2)}, u32[]{:S(2)}) collective-permute-start(bf16[64,1024]{1,0:T(8,128)(2,1)S(1)} %shard_map.57), channel_id=1, source_target_pairs={{0,4},{1,5},{2,6},{3,7},{4,0},{5,1},{6,2},{7,3},{8,12},{9,13},{10,... | collective-permute-start | bytes 393224 | tf_op jit(solution)/shard_map/ppermute | solution.py:34
  67.6 1.1 %collective-permute-start.12 = (bf16[64,1024]{1,0:T(8,128)(2,1)S(1)}, bf16[64,1024]{1,0:T(8,128)(2,1)S(1)}, u32[]{:S(2)}, u32[]{:S(2)}) collective-permute-start(bf16[64,1024]{1,0:T(8,128)(2,1)S(1)} %shard_map.57), channel_id=1, source_target_pairs={{0,2},{1,3},{2,4},{3,5},{4,6},{5,7},{6,0},{7,1},{8,10},{9,11},{10,... | collective-permute-start | bytes 393224 | tf_op jit(solution)/shard_map/ppermute | solution.py:34
  68.7 2.2 %collective-permute-start.13 = (bf16[64,1024]{1,0:T(8,128)(2,1)S(1)}, bf16[64,1024]{1,0:T(8,128)(2,1)S(1)}, u32[]{:S(2)}, u32[]{:S(2)}) collective-permute-start(bf16[64,1024]{1,0:T(8,128)(2,1)S(1)} %shard_map.57), channel_id=1, source_target_pairs={{0,6},{1,7},{2,0},{3,1},{4,2},{5,3},{6,4},{7,5},{8,14},{9,15},{10,... | collective-permute-start | bytes 393224 | tf_op jit(solution)/shard_map/ppermute | solution.py:34
  70.9 1.3 %copy-done.14 = f32[320,1024]{1,0:T(8,128)S(1)} copy-done((f32[320,1024]{1,0:T(8,128)S(1)}, f32[320,1024]{1,0:T(8,128)}, u32[]{:S(2)}) %copy-start.14) | copy-done | bytes 1310744
  72.2 0.1 shard_map.59.first
  72.3 1.6 %collective-permute-done.12 = bf16[64,1024]{1,0:T(8,128)(2,1)S(1)} collective-permute-done((bf16[64,1024]{1,0:T(8,128)(2,1)S(1)}, bf16[64,1024]{1,0:T(8,128)(2,1)S(1)}, u32[]{:S(2)}, u32[]{:S(2)}) %collective-permute-start.12) | collective-permute-done | bytes 131104 | tf_op jit(solution)/shard_map/ppermute | solution.py:34
  73.9 0.2 collective-permute-done.13
  74.1 0.1 add_convert_fusion
  74.2 1.4 %collective-permute-start.16 = (bf16[64,1024]{1,0:T(8,128)(2,1)S(1)}, bf16[64,1024]{1,0:T(8,128)(2,1)S(1)}, u32[]{:S(2)}, u32[]{:S(2)}) collective-permute-start(bf16[64,1024]{1,0:T(8,128)(2,1)S(1)} %add_convert_fusion), channel_id=1, source_target_pairs={{0,1},{1,0},{2,3},{3,2},{4,5},{5,4},{6,7},{7,6},{8,9},{9,8},{10,11... | collective-permute-start | bytes 393224 | tf_op jit(solution)/shard_map/ppermute | solution.py:34
  75.6 1.6 %collective-permute-done.17.second = bf16[320,1024]{1,0:T(8,128)(2,1)S(1)} collective-permute-done((bf16[320,1024]{1,0:T(8,128)(2,1)}, bf16[320,1024]{1,0:T(8,128)(2,1)S(1)}, u32[]{:S(2)}, u32[]{:S(2)}) %collective-permute-start.17) | collective-permute-done | bytes 655392 | tf_op jit(solution)/shard_map/ppermute | solution.py:34
  77.2 1.2 %shard_map.60 = f32[320,1024]{1,0:T(8,128)} custom-call(f32[320,1024]{1,0:T(8,128)S(1)} %shard_map.59.first, bf16[320,1024]{1,0:T(8,128)(2,1)S(1)} %collective-permute-done.17.second), custom_call_target="tpu_custom_call" | custom-call | flops 1 | bytes 1 | tf_op jit(solution)/shard_map/pallas_call | solution.py:178
  78.4 2.4 %collective-permute-done.16 = bf16[64,1024]{1,0:T(8,128)(2,1)S(1)} collective-permute-done((bf16[64,1024]{1,0:T(8,128)(2,1)S(1)}, bf16[64,1024]{1,0:T(8,128)(2,1)S(1)}, u32[]{:S(2)}, u32[]{:S(2)}) %collective-permute-start.16) | collective-permute-done | bytes 131104 | tf_op jit(solution)/shard_map/ppermute | solution.py:34
  80.8 0.7 convert_add_fusion
  (46 shorter events, 0.1 us)
Async XLA Ops:
  0.6 12.4 %copy-start = (bf16[1024,1024]{1,0:T(8,128)(2,1)S(1)}, bf16[1024,1024]{1,0:T(8,128)(2,1)}, u32[]{:S(2)}) copy-start(bf16[1024,1024]{1,0:T(8,128)(2,1)} %refs_10_.1) | copy-start | bytes 6291460
  1.9 8.1 %collective-permute-start.2 = (bf16[320,1024]{1,0:T(8,128)(2,1)}, bf16[320,1024]{1,0:T(8,128)(2,1)S(1)}, u32[]{:S(2)}, u32[]{:S(2)}) collective-permute-start(bf16[320,1024]{1,0:T(8,128)(2,1)} %refs_14_.1), channel_id=1, source_target_pairs={{0,8},{1,9},{2,10},{3,11},{4,12},{5,13},{6,14},{7,15},{8,0},{9,1},... | collective-permute-start | bytes 1966088 | tf_op jit(solution)/shard_map/ppermute | solution.py:34
  2.0 22.5 %collective-permute-start.3 = (bf16[320,1024]{1,0:T(8,128)(2,1)}, bf16[320,1024]{1,0:T(8,128)(2,1)S(1)}, u32[]{:S(2)}, u32[]{:S(2)}) collective-permute-start(bf16[320,1024]{1,0:T(8,128)(2,1)} %refs_14_.1), channel_id=1, source_target_pairs={{0,16},{1,17},{2,18},{3,19},{4,20},{5,21},{6,22},{7,23},{8,24},{9,... | collective-permute-start | bytes 1966088 | tf_op jit(solution)/shard_map/ppermute | solution.py:34
  5.4 12.5 %collective-permute-start = (bf16[176,1024]{1,0:T(8,128)(2,1)S(1)}, bf16[176,1024]{1,0:T(8,128)(2,1)S(1)}, u32[]{:S(2)}, u32[]{:S(2)}) collective-permute-start(bf16[176,1024]{1,0:T(8,128)(2,1)S(1)} %get-tuple-element.55), channel_id=1, source_target_pairs={{0,32},{1,33},{2,34},{3,35},{4,36},{5,37},{6,38},{7,39},{8,40},{9,... | collective-permute-start | bytes 1081352 | tf_op jit(solution)/shard_map/ppermute | solution.py:34
  6.9 11.3 %collective-permute-start.1 = (bf16[176,1024]{1,0:T(8,128)(2,1)S(1)}, bf16[176,1024]{1,0:T(8,128)(2,1)S(1)}, u32[]{:S(2)}, u32[]{:S(2)}) collective-permute-start(bf16[176,1024]{1,0:T(8,128)(2,1)S(1)} %get-tuple-element.56), channel_id=1, source_target_pairs={{0,96},{1,97},{2,98},{3,99},{4,100},{5,101},{6,102},{7,103},{8,104... | collective-permute-start | bytes 1081352 | tf_op jit(solution)/shard_map/ppermute | solution.py:34
  9.7 14.5 %collective-permute-start.4 = (bf16[144,1024]{1,0:T(8,128)(2,1)S(1)}, bf16[144,1024]{1,0:T(8,128)(2,1)S(1)}, u32[]{:S(2)}, u32[]{:S(2)}) collective-permute-start(bf16[144,1024]{1,0:T(8,128)(2,1)S(1)} %get-tuple-element.111), channel_id=1, source_target_pairs={{0,32},{1,33},{2,34},{3,35},{4,36},{5,37},{6,38},{7,39},{8,40},{9,... | collective-permute-start | bytes 884744 | tf_op jit(solution)/shard_map/ppermute | solution.py:34
  10.1 7.1 %copy-start.8 = (bf16[320,1024]{1,0:T(8,128)(2,1)}, bf16[320,1024]{1,0:T(8,128)(2,1)S(1)}, u32[]{:S(2)}) copy-start(bf16[320,1024]{1,0:T(8,128)(2,1)S(1)} %collective-permute-done.2.text_c.refs_15_) | copy-start | bytes 1966084
  10.1 14.4 %collective-permute-start.5 = (bf16[144,1024]{1,0:T(8,128)(2,1)S(1)}, bf16[144,1024]{1,0:T(8,128)(2,1)S(1)}, u32[]{:S(2)}, u32[]{:S(2)}) collective-permute-start(bf16[144,1024]{1,0:T(8,128)(2,1)S(1)} %get-tuple-element.110), channel_id=1, source_target_pairs={{0,96},{1,97},{2,98},{3,99},{4,100},{5,101},{6,102},{7,103},{8,104... | collective-permute-start | bytes 884744 | tf_op jit(solution)/shard_map/ppermute | solution.py:34
  13.0 1.1 %copy-start.1 = (bf16[320,1024]{1,0:T(8,128)(2,1)S(1)}, bf16[320,1024]{1,0:T(8,128)(2,1)}, u32[]{:S(2)}) copy-start(bf16[320,1024]{1,0:T(8,128)(2,1)} %refs_0_.1) | copy-start | bytes 1966084
  14.1 1.1 %copy-start.7 = (bf16[320,1024]{1,0:T(8,128)(2,1)S(1)}, bf16[320,1024]{1,0:T(8,128)(2,1)}, u32[]{:S(2)}) copy-start(bf16[320,1024]{1,0:T(8,128)(2,1)} %refs_14_.1) | copy-start | bytes 1966084
  17.2 6.2 %copy-start.16 = (bf16[320,512]{1,0:T(8,128)(2,1)}, bf16[320,512]{1,0:T(8,128)(2,1)S(1)}, u32[]{:S(2)}) copy-start(bf16[320,512]{1,0:T(8,128)(2,1)S(1)} %get-tuple-element.94.refs_4_) | copy-start | bytes 983044
  17.2 21.0 %copy-start.5 = (bf16[320,1024]{1,0:T(8,128)(2,1)}, bf16[320,1024]{1,0:T(8,128)(2,1)S(1)}, u32[]{:S(2)}) copy-start(bf16[320,1024]{1,0:T(8,128)(2,1)S(1)} %get-tuple-element.65.refs_0_) | copy-start | bytes 1966084
  18.2 13.3 %collective-permute-start.8 = (bf16[176,1024]{1,0:T(8,128)(2,1)S(1)}, bf16[176,1024]{1,0:T(8,128)(2,1)S(1)}, u32[]{:S(2)}, u32[]{:S(2)}) collective-permute-start(bf16[176,1024]{1,0:T(8,128)(2,1)S(1)} %collective-permute-done.refs_0_.refs_1_), channel_id=1, source_target_pairs={{0,32},{1,33},{2,34},{3,35},{4,36},{5,37},{6,38},{7,39},{8,40},{9,... | collective-permute-start | bytes 1081352 | tf_op jit(solution)/shard_map/ppermute | solution.py:34
  19.7 11.8 %collective-permute-start.9 = (bf16[176,1024]{1,0:T(8,128)(2,1)S(1)}, bf16[176,1024]{1,0:T(8,128)(2,1)S(1)}, u32[]{:S(2)}, u32[]{:S(2)}) collective-permute-start(bf16[176,1024]{1,0:T(8,128)(2,1)S(1)} %collective-permute-done.1.refs_1_.refs_2_), channel_id=1, source_target_pairs={{0,96},{1,97},{2,98},{3,99},{4,100},{5,101},{6,102},{7,103},{8,104... | collective-permute-start | bytes 1081352 | tf_op jit(solution)/shard_map/ppermute | solution.py:34
  23.4 3.5 %copy-start.15 = (bf16[352,512]{1,0:T(8,128)(2,1)}, bf16[352,512]{1,0:T(8,128)(2,1)S(1)}, u32[]{:S(2)}) copy-start(bf16[352,512]{1,0:T(8,128)(2,1)S(1)} %get-tuple-element.95.refs_5_) | copy-start | bytes 1081348
  23.4 14.8 %copy-start.3 = (bf16[352,1024]{1,0:T(8,128)(2,1)}, bf16[352,1024]{1,0:T(8,128)(2,1)S(1)}, u32[]{:S(2)}) copy-start(bf16[352,1024]{1,0:T(8,128)(2,1)S(1)} %get-tuple-element.69.refs_4_.refs_1_) | copy-start | bytes 2162692
  24.5 2.4 %copy-start.4 = (bf16[320,1024]{1,0:T(8,128)(2,1)}, bf16[320,1024]{1,0:T(8,128)(2,1)S(1)}, u32[]{:S(2)}) copy-start(bf16[320,1024]{1,0:T(8,128)(2,1)S(1)} %collective-permute-done.3.refs_13_) | copy-start | bytes 1966084
  24.5 2.4 %collective-permute-start.6 = (bf16[160,1024]{1,0:T(8,128)(2,1)S(1)}, bf16[160,1024]{1,0:T(8,128)(2,1)S(1)}, u32[]{:S(2)}, u32[]{:S(2)}) collective-permute-start(bf16[160,1024]{1,0:T(8,128)(2,1)S(1)} %get-tuple-element.109), channel_id=1, source_target_pairs={{0,8},{1,9},{2,10},{3,11},{4,12},{5,13},{6,14},{7,15},{8,0},{9,1},... | collective-permute-start | bytes 983048 | tf_op jit(solution)/shard_map/ppermute | solution.py:34
  24.6 2.3 %collective-permute-start.7 = (bf16[160,1024]{1,0:T(8,128)(2,1)S(1)}, bf16[160,1024]{1,0:T(8,128)(2,1)S(1)}, u32[]{:S(2)}, u32[]{:S(2)}) collective-permute-start(bf16[160,1024]{1,0:T(8,128)(2,1)S(1)} %get-tuple-element.108), channel_id=1, source_target_pairs={{0,8},{1,9},{2,10},{3,11},{4,12},{5,13},{6,14},{7,15},{8,0},{9,1},... | collective-permute-start | bytes 983048 | tf_op jit(solution)/shard_map/ppermute | solution.py:34
  26.9 4.6 %copy-start.18 = (bf16[288,512]{1,0:T(8,128)(2,1)}, bf16[288,512]{1,0:T(8,128)(2,1)S(1)}, u32[]{:S(2)}) copy-start(bf16[288,512]{1,0:T(8,128)(2,1)S(1)} %get-tuple-element.96.refs_6_) | copy-start | bytes 884740
  26.9 11.3 %copy-start.6 = (bf16[288,1024]{1,0:T(8,128)(2,1)}, bf16[288,1024]{1,0:T(8,128)(2,1)S(1)}, u32[]{:S(2)}) copy-start(bf16[288,1024]{1,0:T(8,128)(2,1)S(1)} %get-tuple-element.73.refs_8_.refs_2_) | copy-start | bytes 1769476
  26.9 4.6 %copy-start.2 = (bf16[320,1024]{1,0:T(8,128)(2,1)S(1)}, bf16[320,1024]{1,0:T(8,128)(2,1)}, u32[]{:S(2)}) copy-start(bf16[320,1024]{1,0:T(8,128)(2,1)} %refs_0_.1) | copy-start | bytes 1966084
  31.5 6.7 %copy-start.10 = (bf16[352,768]{1,0:T(8,128)(2,1)}, bf16[352,768]{1,0:T(8,128)(2,1)S(1)}, u32[]{:S(2)}) copy-start(bf16[352,768]{1,0:T(8,128)(2,1)S(1)} %get-tuple-element.90.refs_5_.refs_9_) | copy-start | bytes 1622020
  31.5 6.7 %copy-start.11 = (bf16[320,768]{1,0:T(8,128)(2,1)}, bf16[320,768]{1,0:T(8,128)(2,1)S(1)}, u32[]{:S(2)}) copy-start(bf16[320,768]{1,0:T(8,128)(2,1)S(1)} %get-tuple-element.89.refs_4_.refs_8_) | copy-start | bytes 1474564
  31.5 6.7 %copy-start.13 = (bf16[288,768]{1,0:T(8,128)(2,1)}, bf16[288,768]{1,0:T(8,128)(2,1)S(1)}, u32[]{:S(2)}) copy-start(bf16[288,768]{1,0:T(8,128)(2,1)S(1)} %get-tuple-element.91.refs_6_.refs_10_) | copy-start | bytes 1327108
  37.8 3.0 %copy-start.9 = (bf16[320,1024]{1,0:T(8,128)(2,1)}, bf16[320,1024]{1,0:T(8,128)(2,1)S(1)}, u32[]{:S(2)}) copy-start(bf16[320,1024]{1,0:T(8,128)(2,1)S(1)} %get-tuple-element.88.refs_3_) | copy-start | bytes 1966084
  37.8 3.0 %copy-start.12 = (bf16[320,768]{1,0:T(8,128)(2,1)}, bf16[320,768]{1,0:T(8,128)(2,1)S(1)}, u32[]{:S(2)}) copy-start(bf16[320,768]{1,0:T(8,128)(2,1)S(1)} %get-tuple-element.92.refs_7_.refs_11_) | copy-start | bytes 1474564
  37.8 3.0 %copy-start.17 = (bf16[320,512]{1,0:T(8,128)(2,1)}, bf16[320,512]{1,0:T(8,128)(2,1)S(1)}, u32[]{:S(2)}) copy-start(bf16[320,512]{1,0:T(8,128)(2,1)S(1)} %get-tuple-element.97.refs_7_) | copy-start | bytes 983044
  37.8 3.0 %collective-permute-start.10 = (bf16[8,64,1024]{2,1,0:T(8,128)(2,1)S(1)}, bf16[8,64,1024]{2,1,0:T(8,128)(2,1)S(1)}, u32[]{:S(2)}, u32[]{:S(2)}) collective-permute-start(bf16[8,64,1024]{2,1,0:T(8,128)(2,1)S(1)} %get-tuple-element.87), channel_id=1, source_target_pairs={{0,8},{1,9},{2,10},{3,11},{4,12},{5,13},{6,14},{7,15},{8,0},{9,1},... | collective-permute-start | bytes 3145736 | tf_op jit(solution)/shard_map/ppermute | solution.py:34
  40.9 5.9 %collective-permute-start.14 = (f32[320,1024]{1,0:T(8,128)}, f32[320,1024]{1,0:T(8,128)S(1)}, u32[]{:S(2)}, u32[]{:S(2)}) collective-permute-start(f32[320,1024]{1,0:T(8,128)} %shard_map.55), channel_id=1, source_target_pairs={{0,8},{1,9},{2,10},{3,11},{4,12},{5,13},{6,14},{7,15},{8,0},{9,1},... | collective-permute-start | bytes 3932168 | tf_op jit(solution)/shard_map/ppermute | solution.py:34
  42.6 21.0 %all-to-all-start = ((bf16[8,64,1024]{2,1,0:T(8,128)(2,1)}), bf16[8,64,1024]{2,1,0:T(8,128)(2,1)S(1)}, u32[]{:S(2)}, u32[]{:S(2)}) async-start(bf16[8,64,1024]{2,1,0:T(8,128)(2,1)} %shard_map.56), calls=%async_computation | async-start | bytes 2097152 | tf_op jit(solution)/shard_map/all_to_all | solution.py:265
  46.8 1.1 %copy-start.19 = (f32[320,1024]{1,0:T(8,128)}, f32[320,1024]{1,0:T(8,128)S(1)}, u32[]{:S(2)}) copy-start(f32[320,1024]{1,0:T(8,128)S(1)} %collective-permute-done.14.refs_12_) | copy-start | bytes 3932164
  57.8 13.1 %collective-permute-start.15 = (bf16[320,1024]{1,0:T(8,128)(2,1)}, bf16[320,1024]{1,0:T(8,128)(2,1)S(1)}, u32[]{:S(2)}, u32[]{:S(2)}) collective-permute-start(bf16[320,1024]{1,0:T(8,128)(2,1)} %get-tuple-element.100), channel_id=1, source_target_pairs={{0,8},{1,9},{2,10},{3,11},{4,12},{5,13},{6,14},{7,15},{8,0},{9,1},... | collective-permute-start | bytes 1966088 | tf_op jit(solution)/shard_map/ppermute | solution.py:34
  57.8 19.4 %collective-permute-start.17 = (bf16[320,1024]{1,0:T(8,128)(2,1)}, bf16[320,1024]{1,0:T(8,128)(2,1)S(1)}, u32[]{:S(2)}, u32[]{:S(2)}) collective-permute-start(bf16[320,1024]{1,0:T(8,128)(2,1)} %get-tuple-element.105), channel_id=1, source_target_pairs={{0,16},{1,17},{2,18},{3,19},{4,20},{5,21},{6,22},{7,23},{8,24},{9,... | collective-permute-start | bytes 1966088 | tf_op jit(solution)/shard_map/ppermute | solution.py:34
  63.7 8.6 %collective-permute-start.11 = (bf16[64,1024]{1,0:T(8,128)(2,1)S(1)}, bf16[64,1024]{1,0:T(8,128)(2,1)S(1)}, u32[]{:S(2)}, u32[]{:S(2)}) collective-permute-start(bf16[64,1024]{1,0:T(8,128)(2,1)S(1)} %shard_map.57), channel_id=1, source_target_pairs={{0,4},{1,5},{2,6},{3,7},{4,0},{5,1},{6,2},{7,3},{8,12},{9,13},{10,... | collective-permute-start | bytes 393224 | tf_op jit(solution)/shard_map/ppermute | solution.py:34
  67.6 6.3 %collective-permute-start.12 = (bf16[64,1024]{1,0:T(8,128)(2,1)S(1)}, bf16[64,1024]{1,0:T(8,128)(2,1)S(1)}, u32[]{:S(2)}, u32[]{:S(2)}) collective-permute-start(bf16[64,1024]{1,0:T(8,128)(2,1)S(1)} %shard_map.57), channel_id=1, source_target_pairs={{0,2},{1,3},{2,4},{3,5},{4,6},{5,7},{6,0},{7,1},{8,10},{9,11},{10,... | collective-permute-start | bytes 393224 | tf_op jit(solution)/shard_map/ppermute | solution.py:34
  68.7 5.4 %collective-permute-start.13 = (bf16[64,1024]{1,0:T(8,128)(2,1)S(1)}, bf16[64,1024]{1,0:T(8,128)(2,1)S(1)}, u32[]{:S(2)}, u32[]{:S(2)}) collective-permute-start(bf16[64,1024]{1,0:T(8,128)(2,1)S(1)} %shard_map.57), channel_id=1, source_target_pairs={{0,6},{1,7},{2,0},{3,1},{4,2},{5,3},{6,4},{7,5},{8,14},{9,15},{10,... | collective-permute-start | bytes 393224 | tf_op jit(solution)/shard_map/ppermute | solution.py:34
  70.9 1.3 %copy-start.14 = (f32[320,1024]{1,0:T(8,128)S(1)}, f32[320,1024]{1,0:T(8,128)}, u32[]{:S(2)}) copy-start(f32[320,1024]{1,0:T(8,128)} %get-tuple-element.99.first) | copy-start | bytes 3932164
  74.2 6.6 %collective-permute-start.16 = (bf16[64,1024]{1,0:T(8,128)(2,1)S(1)}, bf16[64,1024]{1,0:T(8,128)(2,1)S(1)}, u32[]{:S(2)}, u32[]{:S(2)}) collective-permute-start(bf16[64,1024]{1,0:T(8,128)(2,1)S(1)} %add_convert_fusion), channel_id=1, source_target_pairs={{0,1},{1,0},{2,3},{3,2},{4,5},{5,4},{6,7},{7,6},{8,9},{9,8},{10,11... | collective-permute-start | bytes 393224 | tf_op jit(solution)/shard_map/ppermute | solution.py:34
